TPU v7x, 32 devices: a whole 2x2x4 slice. The times are simulated.
32 devices in a mesh: ctx: 4 (over y, x), fsdp: 8 (over z, core).
Axes of the slice: x: 2, y: 2, z: 4, core: 2. Of those that a mesh axis runs over, the one named last changes fastest.
Arguments:
- tokens: bfloat16 [8, 2048, 1024], P('fsdp', 'ctx'), may hold values from -6 to 6
- teacher: bfloat16 [8, 2048, 1024], P('fsdp', 'ctx'), may hold values from -6 to 6
- cotangent: bfloat16 [8, 2048, 1024], P('fsdp', 'ctx'), may hold values from -6 to 6
- lengths: int32 [8, 8], P('fsdp'), may hold values from 1 to 1789, as said below
- variate: int32 [8, 2048], P('fsdp'), may hold values from 0 to 7
- observed: int32 [8, 2048], P('fsdp'), may hold values from 0 to 1, as said below
- norm_gains: bfloat16 [4, 1024], P(None, 'fsdp'), may hold values from 0.5 to 2
- var_bias: bfloat16 [32], P('fsdp'), may hold values from -3 to 3
- qkv_weight: bfloat16 [1024, 3072], P('fsdp'), may hold values from -0.1875 to 0.1875
- out_weight: bfloat16 [1024, 1024], P('fsdp'), may hold values from -1 to 1
- ffn_in: bfloat16 [1024, 5632], P('fsdp'), may hold values from -0.1875 to 0.1875
- ffn_out: bfloat16 [2816, 1024], P('fsdp'), may hold values from -0.109375 to 0.109375
Outputs:
- loss: float32 [], replicated
- activations: bfloat16 [8, 2048, 1024], P('fsdp', 'ctx')
- input_grad: float32 [8, 2048, 1024], P('fsdp', 'ctx')
- gains_grad: float32 [4, 1024], P(None, 'fsdp')
- var_bias_grad: float32 [32], P('fsdp')
- qkv_weight_grad: float32 [1024, 3072], P('fsdp')
- out_weight_grad: float32 [1024, 1024], P('fsdp')
- ffn_in_grad: float32 [1024, 5632], P('fsdp')
- ffn_out_grad: float32 [2816, 1024], P('fsdp')
Inputs may be any that keep to these rules, and one draw needn't show every extreme that they name: Each sequence's lengths sum to 2048. In each sequence exactly one document has length 1789; all others are at most 64. The first token of every sequence is observed.
All inputs are finite; a program needn't handle non-finite values.
Results may differ from a plain program's by a relative error of at most 0.018.
Values may be sent and summed in bfloat16 or wider, within the bound.
No kernel may reach another device: no remote copies, remote signals or barrier semaphores. Data moves between devices by JAX's collectives and lax.ppermute only.
A program may use at most 192 MiB of HBM per device.

v0:
```python
import math

import jax
import jax.numpy as jnp
from jax import lax
from jax.sharding import PartitionSpec as P

D = 1024
HEADS = 16
HEAD = 64
FF = 2816
WINDOW = 1024


EPSILON = 1e-06
MASKED = -1e30


def padded(shard, sides, width):
    for axis, dim in sides:
        size, length = (lax.axis_size(axis), shard.shape[dim])
        up = [(i, (i + 1) % size) for i in range(size - 1)]
        down = [(j, i) for i, j in up]
        last = lax.slice_in_dim(shard, length - width, length, axis=dim)
        initial = lax.slice_in_dim(shard, 0, width, axis=dim)
        before = lax.ppermute(last, axis, up)
        after = lax.ppermute(initial, axis, down)
        shard = jnp.concatenate([before, shard, after], axis=dim)
    return shard


def shifted(shard, axis, by):
    size = lax.axis_size(axis)
    pairs = [(i, i + by) for i in range(size) if 0 <= i + by < size]
    return lax.ppermute(shard, axis, pairs)


def rms_scale(vector, scales):
    return vector * lax.rsqrt(jnp.mean(vector * vector, axis=-1, keepdims=True) + EPSILON) * scales


def rotary(positions):
    half_dim = HEAD // 2
    frequency = jnp.exp(
        jnp.arange(half_dim).astype(jnp.float32) * (-2.0 * math.log(10000.0) / HEAD)
    )
    angles = positions.astype(jnp.float32)[:, None] * frequency[None, :]
    return (jnp.cos(angles)[:, None, :], jnp.sin(angles)[:, None, :])


def head_prep(vector, scales, cosine_table, sine_table):
    total_rows = vector.shape[0]
    heads_view = vector.reshape(total_rows, HEADS, HEAD)
    heads_view = heads_view * lax.rsqrt(
        jnp.mean(heads_view * heads_view, axis=-1, keepdims=True) + EPSILON
    )
    heads_view = heads_view * scales.reshape(HEADS, HEAD)
    front_half = heads_view[..., : HEAD // 2]
    back_half = heads_view[..., HEAD // 2 :]
    turned = jnp.concatenate(
        [
            front_half * cosine_table - back_half * sine_table,
            back_half * cosine_table + front_half * sine_table,
        ],
        axis=-1,
    )
    return turned.reshape(total_rows, HEADS * HEAD)


def document_ids(doc_lengths, positions):
    doc_ends = jnp.cumsum(doc_lengths)
    return jnp.sum((positions[:, None] >= doc_ends[None, :]).astype(jnp.int32), axis=1)


def gated_unit(gate_up):
    gate_part = gate_up[:, :FF]
    up_part = gate_up[:, FF:]
    return gate_part / (1.0 + jnp.exp(-gate_part)) * up_part


def times_transposed(left, right):
    return lax.dot_general(
        left, right, (((1,), (1,)), ((), ())), preferred_element_type=jnp.float32
    )


def transposed_times(left, right):
    return lax.dot_general(
        left, right, (((0,), (0,)), ((), ())), preferred_element_type=jnp.float32
    )


def per_device(
    tokens,
    teacher,
    cotangent,
    lengths,
    variate,
    observed,
    norm_gains,
    var_bias,
    qkv_weight,
    out_weight,
    ffn_in,
    ffn_out,
):
    row_count = tokens.shape[1]
    n_context = lax.axis_size("ctx")
    n_shards = lax.axis_size("fsdp")
    half_span = WINDOW // 2
    extent = row_count + 2 * half_span
    block_rows = min(512, row_count)
    key_rows = block_rows + 2 * half_span
    pair_width = 2 * HEAD
    scale_factor = HEAD ** (-0.5)
    row_start = lax.axis_index("ctx") * row_count
    seq_len = observed.shape[1]
    inputs = tokens[0].astype(jnp.float32)
    gains_all, bias_all, w_qkv, w_attn = (
        lax.all_gather(norm_gains, "fsdp", axis=1, tiled=True),
        lax.all_gather(var_bias, "fsdp", axis=0, tiled=True),
        lax.all_gather(qkv_weight, "fsdp", axis=0, tiled=True),
        lax.all_gather(out_weight, "fsdp", axis=0, tiled=True),
    )
    w_upper, w_lower = (
        lax.all_gather(ffn_in, "fsdp", axis=0, tiled=True),
        lax.all_gather(ffn_out, "fsdp", axis=0, tiled=True),
    )
    gains_f = gains_all.astype(jnp.float32)
    bias_f = bias_all.astype(jnp.float32)
    doc_lengths = lengths[0]
    all_var = variate[0]
    all_obs = observed[0]
    query_pos = row_start + jnp.arange(row_count, dtype=jnp.int32)
    query_doc = document_ids(doc_lengths, query_pos)
    query_var = lax.dynamic_slice_in_dim(all_var, row_start, row_count, 0)
    query_obs = lax.dynamic_slice_in_dim(all_obs, row_start, row_count, 0)
    key_pos = row_start - half_span + jnp.arange(extent, dtype=jnp.int32)
    key_doc = document_ids(doc_lengths, key_pos)
    key_var = lax.dynamic_slice_in_dim(jnp.pad(all_var, half_span), row_start, extent, 0)
    key_obs = lax.dynamic_slice_in_dim(jnp.pad(all_obs, half_span), row_start, extent, 0)
    key_inside = (key_pos >= 0) & (key_pos < seq_len)
    block_masks = []
    relative = key_pos[None, :] - query_pos[:, None]
    allowed = (jnp.abs(relative) <= half_span) & key_inside[None, :]
    allowed = allowed & (key_doc[None, :] == query_doc[:, None])
    allowed = allowed & ((key_obs[None, :] == 1) | (relative == 0))
    same_var = key_var[None, :] == query_var[:, None]
    block_masks.append((allowed, same_var))
    normed_f, norm_one_pull = jax.vjp(rms_scale, inputs, gains_f[0])
    normed = normed_f.astype(jnp.bfloat16)
    projected = jnp.dot(normed, w_qkv, preferred_element_type=jnp.float32)
    cosine_table, sine_table = rotary(query_pos)

    def query_key_prep(query_part, key_part, query_gain, key_gain):
        return (
            head_prep(query_part, query_gain, cosine_table, sine_table),
            head_prep(key_part, key_gain, cosine_table, sine_table),
        )

    (query_f, key_f), prep_pull = jax.vjp(
        query_key_prep, projected[:, :D], projected[:, D : 2 * D], gains_f[2], gains_f[3]
    )
    query_low = query_f.astype(jnp.bfloat16)
    kv_low = jnp.concatenate(
        [key_f.astype(jnp.bfloat16), projected[:, 2 * D :].astype(jnp.bfloat16)], axis=1
    )
    kv_ext = padded(kv_low, (("ctx", 0),), half_span)

    def block_scores(query_blk, key_blk, same_bias, other_bias, allowed, same_var):
        raw = jnp.einsum("qhd,khd->hqk", query_blk, key_blk, preferred_element_type=jnp.float32)
        scores = raw * scale_factor + jnp.where(
            same_var[None], same_bias[:, None, None], other_bias[:, None, None]
        )
        return jnp.where(allowed[None], scores, MASKED)

    def group_inputs(group):
        column = group * pair_width
        query_grp = lax.dynamic_slice_in_dim(query_low, column, pair_width, 1)
        key_grp = lax.dynamic_slice_in_dim(kv_ext, column, pair_width, 1)
        value_grp = lax.dynamic_slice_in_dim(kv_ext, D + column, pair_width, 1)
        same_bias = lax.dynamic_slice_in_dim(bias_f, 2 * group, 2, 0)
        other_bias = lax.dynamic_slice_in_dim(bias_f, HEADS + 2 * group, 2, 0)
        return (column, query_grp, key_grp, value_grp, same_bias, other_bias)

    def forward_group(group, carry):
        out_buf, lse_buf = carry
        column, query_grp, key_grp, value_grp, same_bias, other_bias = group_inputs(group)
        allowed, same_var = block_masks[0 // block_rows]
        query_blk = query_grp.reshape(block_rows, 2, HEAD)
        key_blk = key_grp.reshape(key_rows, 2, HEAD)
        value_blk = value_grp.reshape(key_rows, 2, HEAD)
        scores = block_scores(query_blk, key_blk, same_bias, other_bias, allowed, same_var)
        top_score = jnp.max(scores, axis=-1, keepdims=True)
        expo = jnp.exp(scores - top_score)
        total_exp = jnp.sum(expo, axis=-1, keepdims=True)
        prob_low = (expo / total_exp).astype(jnp.bfloat16)
        result = jnp.einsum("hqk,khd->qhd", prob_low, value_blk, preferred_element_type=jnp.float32)
        out_parts = [result.reshape(block_rows, pair_width)]
        lse_parts = [(top_score + jnp.log(total_exp))[..., 0]]
        out_buf = lax.dynamic_update_slice_in_dim(
            out_buf, jnp.concatenate(out_parts, axis=0), column, 1
        )
        lse_buf = lax.dynamic_update_slice_in_dim(
            lse_buf, jnp.concatenate(lse_parts, axis=1), 2 * group, 0
        )
        return (out_buf, lse_buf)

    attended, log_totals = lax.fori_loop(
        0,
        HEADS // 2,
        forward_group,
        (jnp.zeros((row_count, D), jnp.float32), jnp.zeros((HEADS, row_count), jnp.float32)),
    )
    attn = attended.astype(jnp.bfloat16)
    mixed = inputs + jnp.dot(attn, w_attn, preferred_element_type=jnp.float32)
    normed_two_f, norm_two_pull = jax.vjp(rms_scale, mixed, gains_f[1])
    normed_two = normed_two_f.astype(jnp.bfloat16)
    gate_up = jnp.dot(normed_two, w_upper, preferred_element_type=jnp.float32)
    hidden_f, glu_pull = jax.vjp(gated_unit, gate_up)
    hidden = hidden_f.astype(jnp.bfloat16)
    final = mixed + jnp.dot(hidden, w_lower, preferred_element_type=jnp.float32)
    valid_col = query_obs.astype(jnp.float32)[:, None]
    distance = final - teacher[0].astype(jnp.float32)
    valid_total, squared_sum = lax.psum(
        (jnp.sum(query_obs.astype(jnp.float32)), jnp.sum(valid_col * distance * distance)),
        ("ctx", "fsdp"),
    )
    loss = squared_sum / (valid_total * D)
    all_tokens = row_count * n_context * n_shards
    d_final = cotangent[0].astype(jnp.float32) + all_tokens * valid_col * distance / valid_total
    d_final_low = d_final.astype(jnp.bfloat16)
    d_hidden = times_transposed(d_final_low, w_lower)
    grad_lower = transposed_times(hidden, d_final_low)
    (d_gate_up,) = glu_pull(d_hidden)
    d_gate_low = d_gate_up.astype(jnp.bfloat16)
    d_normed_two = times_transposed(d_gate_low, w_upper)
    grad_upper = transposed_times(normed_two, d_gate_low)
    d_mixed_part, grad_norm_two = norm_two_pull(d_normed_two)
    d_mixed = d_final + d_mixed_part
    ffn_parts = (
        lax.psum_scatter(
            grad_upper.astype(jnp.bfloat16), "fsdp", scatter_dimension=0, tiled=True
        ).astype(jnp.float32),
        lax.psum_scatter(
            grad_lower.astype(jnp.bfloat16), "fsdp", scatter_dimension=0, tiled=True
        ).astype(jnp.float32),
    )
    ffn_in_grad, ffn_out_grad = (
        lax.psum(ffn_parts[0].astype(jnp.bfloat16), "ctx").astype(jnp.float32),
        lax.psum(ffn_parts[1].astype(jnp.bfloat16), "ctx").astype(jnp.float32),
    )
    d_mixed_low = d_mixed.astype(jnp.bfloat16)
    d_attn = times_transposed(d_mixed_low, w_attn)
    grad_attn = transposed_times(attn, d_mixed_low)
    d_attn_low = d_attn.astype(jnp.bfloat16)

    def backward_group(group, carry):
        dq_buf, dkv_buf, bias_buf = carry
        column, query_grp, key_grp, value_grp, same_bias, other_bias = group_inputs(group)
        dout_grp = lax.dynamic_slice_in_dim(d_attn_low, column, pair_width, 1)
        lse_grp = lax.dynamic_slice_in_dim(log_totals, 2 * group, 2, 0)
        dk_group = jnp.zeros((extent, pair_width), jnp.float32)
        dv_group = jnp.zeros((extent, pair_width), jnp.float32)
        allowed, same_var = block_masks[0 // block_rows]
        query_blk = query_grp.reshape(block_rows, 2, HEAD)
        key_blk = key_grp.reshape(key_rows, 2, HEAD)
        value_blk = value_grp.reshape(key_rows, 2, HEAD)
        dout_blk = dout_grp.reshape(block_rows, 2, HEAD)
        scores = block_scores(query_blk, key_blk, same_bias, other_bias, allowed, same_var)
        prob = jnp.exp(scores - lse_grp[:, 0:block_rows, None])
        prob_low = prob.astype(jnp.bfloat16)
        d_prob = jnp.einsum("qhd,khd->hqk", dout_blk, value_blk, preferred_element_type=jnp.float32)
        d_scores = prob * (d_prob - jnp.sum(prob * d_prob, axis=-1, keepdims=True))
        same_sum = jnp.sum(jnp.where(same_var[None], d_scores, 0.0), axis=(1, 2))
        other_sum = jnp.sum(jnp.where(same_var[None], 0.0, d_scores), axis=(1, 2))
        d_raw_low = (d_scores * scale_factor).astype(jnp.bfloat16)
        dq_parts = [
            jnp.einsum(
                "hqk,khd->qhd", d_raw_low, key_blk, preferred_element_type=jnp.float32
            ).reshape(block_rows, pair_width)
        ]
        dk_block = jnp.einsum(
            "hqk,qhd->khd", d_raw_low, query_blk, preferred_element_type=jnp.float32
        ).reshape(key_rows, pair_width)
        dv_block = jnp.einsum(
            "hqk,qhd->khd", prob_low, dout_blk, preferred_element_type=jnp.float32
        ).reshape(key_rows, pair_width)
        dk_group = dk_group.at[0:key_rows].add(dk_block)
        dv_group = dv_group.at[0:key_rows].add(dv_block)
        dq_buf = lax.dynamic_update_slice_in_dim(
            dq_buf, jnp.concatenate(dq_parts, axis=0), column, 1
        )
        dkv_buf = lax.dynamic_update_slice_in_dim(dkv_buf, dk_group, column, 1)
        dkv_buf = lax.dynamic_update_slice_in_dim(dkv_buf, dv_group, D + column, 1)
        bias_buf = lax.dynamic_update_slice_in_dim(bias_buf, same_sum, 2 * group, 0)
        bias_buf = lax.dynamic_update_slice_in_dim(bias_buf, other_sum, HEADS + 2 * group, 0)
        return (dq_buf, dkv_buf, bias_buf)

    d_query, dkv_ext, grad_bias = lax.fori_loop(
        0,
        HEADS // 2,
        backward_group,
        (
            jnp.zeros((row_count, D), jnp.float32),
            jnp.zeros((extent, 2 * D), jnp.float32),
            jnp.zeros((2 * HEADS,), jnp.float32),
        ),
    )
    from_next = shifted(dkv_ext[:half_span].astype(jnp.bfloat16), "ctx", -1).astype(jnp.float32)
    from_prev = shifted(dkv_ext[extent - half_span :].astype(jnp.bfloat16), "ctx", 1).astype(
        jnp.float32
    )
    d_kv = dkv_ext[half_span : half_span + row_count]
    d_kv = d_kv.at[row_count - half_span :].add(from_next)
    d_kv = d_kv.at[:half_span].add(from_prev)
    d_query_pre, d_key_pre, grad_query_gain, grad_key_gain = prep_pull((d_query, d_kv[:, :D]))
    d_projected_low = jnp.concatenate([d_query_pre, d_key_pre, d_kv[:, D:]], axis=1).astype(
        jnp.bfloat16
    )
    d_normed = times_transposed(d_projected_low, w_qkv)
    grad_qkv = transposed_times(normed, d_projected_low)
    d_input_part, grad_norm_one = norm_one_pull(d_normed)
    input_grad = d_mixed + d_input_part
    grad_gains = jnp.stack([grad_norm_one, grad_norm_two, grad_query_gain, grad_key_gain])
    attn_parts = (
        lax.psum_scatter(
            grad_gains.astype(jnp.bfloat16), "fsdp", scatter_dimension=1, tiled=True
        ).astype(jnp.float32),
        lax.psum_scatter(
            grad_bias.astype(jnp.bfloat16), "fsdp", scatter_dimension=0, tiled=True
        ).astype(jnp.float32),
        lax.psum_scatter(
            grad_qkv.astype(jnp.bfloat16), "fsdp", scatter_dimension=0, tiled=True
        ).astype(jnp.float32),
        lax.psum_scatter(
            grad_attn.astype(jnp.bfloat16), "fsdp", scatter_dimension=0, tiled=True
        ).astype(jnp.float32),
    )
    gains_grad, var_bias_grad, qkv_weight_grad, out_weight_grad = (
        lax.psum(attn_parts[0].astype(jnp.bfloat16), "ctx").astype(jnp.float32),
        lax.psum(attn_parts[1].astype(jnp.bfloat16), "ctx").astype(jnp.float32),
        lax.psum(attn_parts[2].astype(jnp.bfloat16), "ctx").astype(jnp.float32),
        lax.psum(attn_parts[3].astype(jnp.bfloat16), "ctx").astype(jnp.float32),
    )
    return (
        loss,
        final.astype(jnp.bfloat16)[None],
        input_grad[None],
        gains_grad,
        var_bias_grad,
        qkv_weight_grad,
        out_weight_grad,
        ffn_in_grad,
        ffn_out_grad,
    )


def solution(mesh):
    return jax.shard_map(
        per_device,
        mesh=mesh,
        in_specs=(
            P("fsdp", "ctx", None),
            P("fsdp", "ctx", None),
            P("fsdp", "ctx", None),
            P("fsdp", None),
            P("fsdp", None),
            P("fsdp", None),
            P(None, "fsdp"),
            P("fsdp"),
            P("fsdp", None),
            P("fsdp", None),
            P("fsdp", None),
            P("fsdp", None),
        ),
        out_specs=(
            P(),
            P("fsdp", "ctx", None),
            P("fsdp", "ctx", None),
            P(None, "fsdp"),
            P("fsdp"),
            P("fsdp", None),
            P("fsdp", None),
            P("fsdp", None),
            P("fsdp", None),
        ),
        check_vma=False,
    )
```

profile of v0, /device:TPU:0, one launch (start us, length us, event | category | flops | bytes accessed | tf_op | source)
XLA Modules:
  0.0 1229.5 jit_solution(292680622891030648)
XLA Ops:
  9.5 13.7 %all_gather.18 = bf16[4,1024]{1,0:T(4,128)(2,1)S(1)} all-gather(bf16[4,128]{1,0:T(4,128)(2,1)} %param.38), channel_id=1, replica_groups=mesh['ctx'=4,'fsdp'=8] {'fsdp'}, dimensions={1}, use_global_device_ids=true | all-gather | bytes 9216 | tf_op jit(solution)/shard_map/all_gather | solution.py:120
  24.0 53.2 %all-gather.5.cloned.1.call-done = bf16[1024,3072]{1,0:T(8,128)(2,1)} async-done(((bf16[128,3072]{1,0:T(8,128)(2,1)}), bf16[1024,3072]{1,0:T(8,128)(2,1)}) %all-gather.5.cloned.1.call-update) | async-done | bytes 6291472 | tf_op jit(solution)/shard_map/all_gather | solution.py:122
  105.7 13.9 %all-reduce.8 = bf16[32]{0:T(256)(128)(2,1)S(1)} all-reduce(bf16[32]{0:T(256)(128)(2,1)S(1)} %dynamic-update-slice.8), channel_id=1, replica_groups=mesh['ctx'=4,'fsdp'=8] {'fsdp'}, use_global_device_ids=true, to_apply=%add.8 | all-reduce | flops 32 | bytes 128
  122.9 24.5 %collective-permute-done.1 = bf16[512,2048]{1,0:T(8,128)(2,1)} collective-permute-done((bf16[512,2048]{1,0:T(8,128)(2,1)}, bf16[512,2048]{1,0:T(8,128)(2,1)}, u32[]{:S(2)}, u32[]{:S(2)}) %collective-permute-start.1) | collective-permute-done | bytes 2097184 | tf_op jit(solution)/shard_map/ppermute | solution.py:27
  153.9 8.8 copy.46
  162.7 71.7 %while.60 = (s32[]{:T(128)}, bf16[512,1024]{0,1:T(8,128)(2,1)S(1)}, f32[16,512]{1,0:T(8,128)S(1)}, bf16[1536,2048]{0,1:T(8,128)(2,1)}, bf16[512,1024]{0,1:T(8,12...) while((s32[]{:T(128)}, bf16[512,1024]{0,1:T(8,128)(2,1)S(1)}, ...), condition=%wide.region_9.10_spmd.clone, body=%wide.region_6.9_spmd.clone.sunk | while | flops 426245120 | bytes 25226744 | solution.py:209
  239.1 9.9 fusion.77
  256.5 19.5 %all-gather.11.cloned.1.call-done = bf16[2816,1024]{1,0:T(8,128)(2,1)} async-done(((bf16[352,1024]{1,0:T(8,128)(2,1)}), bf16[2816,1024]{1,0:T(8,128)(2,1)}) %all-gather.11.cloned.1.call-update) | async-done | bytes 5767184 | tf_op jit(solution)/shard_map/all_gather | solution.py:127
  276.1 8.6 fusion.46
  284.7 63.3 %all-reduce.10 = (f32[]{:T(128)}, f32[]{:T(128)}) all-reduce(f32[]{:T(128)} %get-tuple-element.925, f32[]{:T(128)} %get-tuple-element.881), channel_id=1, replica_groups=mesh['ctx'=4,'fsdp'=8] {'ctx','fsdp'}, use_global_device_ids=true, to_apply=%region_12.13 | all-reduce | flops 2 | bytes 16 | tf_op jit(solution)/shard_map/psum | solution.py:225
  352.9 11.7 fusion.55
  364.7 14.1 %multiply_reduce_fusion.3 = (bf16[1024]{0:T(1024)(128)(2,1)}, f32[512]{0:T(512)S(1)}, f32[512,1024]{1,0:T(8,128)}) fusion(f32[512,1024]{1,0:T(8,128)S(1)} %get-tuple-element.924, f32[512]{0:T(512)S(1)} %fusion.71, f32[1024]{0:T(1024)S(1)} %bitcast.172, bf16[1024,5632]{1,0:T(8,128)(2,1)} %all-gather.9.cloned.1.call-done, ...), kind=kOutput, calls=%fused_computation.95 | convolution fusion | flops 5914491392 | bytes 27273216 | tf_op jit(solution)/shard_map/dot_general | solution.py:82
  385.6 6.9 convolution_convert_fusion.1
  404.7 377.3 %while.61 = (s32[]{:T(128)}, f32[512,1024]{0,1:T(8,128)}, f32[1536,2048]{0,1:T(8,128)}, bf16[32]{0:T(256)(128)(2,1)S(1)}, bf16[1536,2048]{0,1:T(8,128)(2,1)}, /*...) while((s32[]{:T(128)}, f32[512,1024]{0,1:T(8,128)}, ...), condition=%wide.region_20.21_spmd.clone, body=%wide.region_16.20_spmd.clone.sunk | while | flops 1453334016 | bytes 64396864 | solution.py:300
  414.0 8.2 select_reduce_fusion.3
  429.7 10.0 fusion.166
  439.7 10.0 fusion.167
  461.4 8.2 select_reduce_fusion.3
  477.1 10.0 fusion.166
  487.1 9.8 fusion.167
  508.7 8.2 select_reduce_fusion.3
  524.3 9.9 fusion.166
  534.2 9.8 fusion.167
  555.8 8.2 select_reduce_fusion.3
  571.4 9.9 fusion.166
  581.3 9.8 fusion.167
  602.9 8.2 select_reduce_fusion.3
  618.5 9.9 fusion.166
  628.4 9.8 fusion.167
  649.9 8.2 select_reduce_fusion.3
  665.6 9.9 fusion.166
  675.5 9.8 fusion.167
  697.0 8.2 select_reduce_fusion.3
  712.6 9.9 fusion.166
  722.5 9.8 fusion.167
  744.0 8.2 select_reduce_fusion.3
  759.6 9.9 fusion.166
  769.6 9.8 fusion.167
  794.0 44.3 %collective-permute-done.2 = bf16[512,2048]{0,1:T(8,128)(2,1)S(1)} collective-permute-done((bf16[512,2048]{0,1:T(8,128)(2,1)S(1)}, bf16[512,2048]{0,1:T(8,128)(2,1)S(1)}, u32[]{:S(2)}, u32[]{:S(2)}) %collective-permute-start.2) | collective-permute-done | bytes 2097184 | tf_op jit(solution)/shard_map/ppermute | solution.py:35
  849.7 8.6 convolution_convert_fusion.2
  859.9 13.5 %convolution_convert_fusion = bf16[1024,5632]{1,0:T(8,128)(2,1)} fusion(f32[512,2816]{1,0:T(8,128)} %get-tuple-element.898, f32[512,2816]{1,0:T(8,128)} %get-tuple-element.897, f32[512,1024]{1,0:T(8,128)S(1)} %copy-done.5, f32[1024]{0:T(1024)S(1)} %bitcast.174, f32[512]{0:T(512)S(1)} %fusion.71), kind=kOutput, calls=%fused_computation.56 | convolution fusion | flops 5918687232 | bytes 25171968 | tf_op jit(solution)/shard_map/dot_general | solution.py:88
  874.9 8.2 fusion.45
  884.1 87.3 %reduce-scatter.8.cloned.1.call-done = bf16[128,3072]{1,0:T(8,128)(2,1)} async-done(((bf16[1024,3072]{1,0:T(8,128)(2,1)}), bf16[128,3072]{1,0:T(8,128)(2,1)}) %reduce-scatter.8.cloned.1.call-update) | async-done | bytes 786448 | tf_op jit(solution)/shard_map/reduce_scatter | solution.py:333
  971.5 120.0 %reduce-scatter.12.cloned.1.call-done = bf16[128,5632]{1,0:T(8,128)(2,1)} async-done(((bf16[1024,5632]{1,0:T(8,128)(2,1)}), bf16[128,5632]{1,0:T(8,128)(2,1)}) %reduce-scatter.12.cloned.1.call-update) | async-done | bytes 1441808 | tf_op jit(solution)/shard_map/reduce_scatter | solution.py:242
  1093.3 13.6 %all-reduce.9 = bf16[32]{0:T(256)(128)(2,1)S(1)} all-reduce(bf16[32]{0:T(256)(128)(2,1)S(1)} %get-tuple-element.590), channel_id=3, replica_groups=mesh['ctx'=4,'fsdp'=8] {'fsdp'}, use_global_device_ids=true, to_apply=%region_30.31.clone | all-reduce | flops 32 | bytes 128
  1110.5 12.6 %reduce-scatter.16.cloned.1.call-done = bf16[128,4]{1,0:T(8,128)(2,1)} async-done(((bf16[1024,4]{1,0:T(8,128)(2,1)}), bf16[128,4]{1,0:T(8,128)(2,1)}) %reduce-scatter.16.cloned.1.call-update) | async-done | bytes 1040
  1124.0 9.8 all-reduce.11
  1134.9 78.9 %all-reduce.15.cloned.1.call-done = (bf16[128,3072]{1,0:T(8,128)(2,1)}, bf16[128,1024]{1,0:T(8,128)(2,1)}, bf16[128,5632]{1,0:T(8,128)(2,1)}, bf16[352,1024]{1,0:T(8,128)(2,1)}) async-done(((bf16[128,3072]{1,0:T(8,128)(2,1)}, bf16[128,1024]{1,0:T(8,128)(2,1)}, bf16[128,5632]{1,0:T(8,128)(2,1)}, bf16[352,1024]{1,0:T(8,128)(2,1)}), (bf16[128,3072]{1,0:T(8,128)(2,1)}, bf16[128,1024]{1,0:T(8,128)(2,1)}, ...) | async-done | bytes 3211280 | tf_op jit(solution)/shard_map/psum | solution.py:343
  (416 shorter events, 341.4 us)
Async XLA Ops:
  7.2 16.2 %copy-start.7 = (bf16[1,512,1024]{2,1,0:T(8,128)(2,1)S(1)}, bf16[1,512,1024]{2,1,0:T(8,128)(2,1)}, u32[]{:S(2)}) copy-start(bf16[1,512,1024]{2,1,0:T(8,128)(2,1)} %param.32) | copy-start | bytes 3145732
  7.2 70.0 %all-gather.5.cloned.1.call-start = ((), (), s32[]{:S(2)}) async-start(), calls=%async_computation.5 | async-start | bytes 7077888 | tf_op jit(solution)/shard_map/all_gather | solution.py:122
  7.9 226.5 %all-gather.7.cloned.1.call-start = ((), (), s32[]{:S(2)}) async-start(), calls=%async_computation.6 | async-start | bytes 2359296 | tf_op jit(solution)/shard_map/all_gather | solution.py:123
  8.7 230.4 %all-gather.9.cloned.1.call-start = ((), (), s32[]{:S(2)}) async-start(), calls=%async_computation.7 | async-start | bytes 12976128 | tf_op jit(solution)/shard_map/all_gather | solution.py:126
  9.4 266.6 %all-gather.11.cloned.1.call-start = ((), (), s32[]{:S(2)}) async-start(), calls=%async_computation.8 | async-start | bytes 6488064 | tf_op jit(solution)/shard_map/all_gather | solution.py:127
  23.2 69.1 %copy-start.42 = (f32[16,64]{1,0:T(8,128)}, f32[16,64]{1,0:T(8,128)S(1)}, u32[]{:S(2)}) copy-start(f32[16,64]{1,0:T(8,128)S(1)} %mul.531) | copy-start | bytes 12292
  23.3 69.0 %copy-start.40 = (f32[16,64]{1,0:T(8,128)}, f32[16,64]{1,0:T(8,128)S(1)}, u32[]{:S(2)}) copy-start(f32[16,64]{1,0:T(8,128)S(1)} %mul.514) | copy-start | bytes 12292
  23.6 59.3 %copy-start.44 = (f32[512]{0:T(512)}, f32[512]{0:T(512)S(1)}, u32[]{:S(2)}) copy-start(f32[512]{0:T(512)S(1)} %fusion.52) | copy-start | bytes 6148
  23.6 59.3 %copy-start.50 = (f32[512]{0:T(512)}, f32[512]{0:T(512)S(1)}, u32[]{:S(2)}) copy-start(f32[512]{0:T(512)S(1)} %fusion.70) | copy-start | bytes 6148
  23.7 59.3 %copy-start.46 = (f32[1,1024]{1,0:T(1,128)}, f32[1,1024]{1,0:T(1,128)S(1)}, u32[]{:S(2)}) copy-start(f32[1,1024]{1,0:T(1,128)S(1)} %get-tuple-element.918) | copy-start | bytes 12292
  24.0 69.0 %copy-start.28 = (f32[512,32]{0,1:T(8,128)}, f32[512,32]{0,1:T(8,128)S(1)}, u32[]{:S(2)}) copy-start(f32[512,32]{0,1:T(8,128)S(1)} %get-tuple-element.919) | copy-start | bytes 196612
  24.0 69.0 %copy-start.30 = (f32[512,32]{0,1:T(8,128)}, f32[512,32]{0,1:T(8,128)S(1)}, u32[]{:S(2)}) copy-start(f32[512,32]{0,1:T(8,128)S(1)} %get-tuple-element.920) | copy-start | bytes 196612
  88.7 4.2 copy-start
  88.7 3.7 copy-start.2
  94.7 9.4 copy-start.55
  94.7 9.5 copy-start.53
  94.7 10.8 copy-start.56
  94.7 24.9 %copy-start.48 = (s32[1,2048]{1,0:T(1,128)S(1)}, s32[1,2048]{1,0:T(1,128)}, u32[]{:S(2)}) copy-start(s32[1,2048]{1,0:T(1,128)} %param.36) | copy-start | bytes 24580
  94.7 24.9 %copy-start.49 = (s32[1,2048]{1,0:T(1,128)S(1)}, s32[1,2048]{1,0:T(1,128)}, u32[]{:S(2)}) copy-start(s32[1,2048]{1,0:T(1,128)} %param.37) | copy-start | bytes 24580
  96.8 50.7 %collective-permute-start.1 = (bf16[512,2048]{1,0:T(8,128)(2,1)}, bf16[512,2048]{1,0:T(8,128)(2,1)}, u32[]{:S(2)}, u32[]{:S(2)}) collective-permute-start(bf16[512,2048]{1,0:T(8,128)(2,1)} %pad_maximum_fusion.2), channel_id=1, source_target_pairs={{8,0},{16,8},{24,16},{9,1},{17,9},{25,17},{10,2},{18,10},{26,18},{... | collective-permute-start | bytes 6291464 | tf_op jit(solution)/shard_map/ppermute | solution.py:27
  98.1 49.9 %collective-permute-start = (bf16[512,2048]{1,0:T(8,128)(2,1)}, bf16[512,2048]{1,0:T(8,128)(2,1)}, u32[]{:S(2)}, u32[]{:S(2)}) collective-permute-start(bf16[512,2048]{1,0:T(8,128)(2,1)} %pad_maximum_fusion.2), channel_id=1, source_target_pairs={{0,8},{8,16},{16,24},{1,9},{9,17},{17,25},{2,10},{10,18},{18,26},{... | collective-permute-start | bytes 6291464 | tf_op jit(solution)/shard_map/ppermute | solution.py:26
  104.0 780.1 %reduce-scatter.10.cloned.1.call-start = ((), (), s32[]{:S(2)}) async-start(), calls=%async_computation.10 | async-start | bytes 2359296 | tf_op jit(solution)/shard_map/reduce_scatter | solution.py:336
  153.9 8.8 copy-start.17
  162.7 73.0 %copy-start.8 = (bf16[1,512,1024]{2,1,0:T(8,128)(2,1)S(1)}, bf16[1,512,1024]{2,1,0:T(8,128)(2,1)}, u32[]{:S(2)}) copy-start(bf16[1,512,1024]{2,1,0:T(8,128)(2,1)} %param.32) | copy-start | bytes 3145732
  239.0 139.7 %copy-start.4 = (f32[512,1024]{1,0:T(8,128)}, f32[512,1024]{1,0:T(8,128)S(1)}, u32[]{:S(2)}) copy-start(f32[512,1024]{1,0:T(8,128)S(1)} %get-tuple-element.924) | copy-start | bytes 6291460
  249.0 4.2 copy-start.6
  253.2 22.8 %copy-start.23 = (bf16[1,512,1024]{2,1,0:T(8,128)(2,1)S(1)}, bf16[1,512,1024]{2,1,0:T(8,128)(2,1)}, u32[]{:S(2)}) copy-start(bf16[1,512,1024]{2,1,0:T(8,128)(2,1)} %param.33) | copy-start | bytes 3145732
  348.0 5.0 copy-start.54
  352.9 11.8 copy-start.13
  378.8 4.1 copy-start.19
  382.9 2.7 copy-start.14
  385.6 498.6 %reduce-scatter.14.cloned.1.call-start = ((), (), s32[]{:S(2)}) async-start(), calls=%async_computation.12 | async-start | bytes 6488064 | tf_op jit(solution)/shard_map/reduce_scatter | solution.py:245
  392.5 578.9 %reduce-scatter.8.cloned.1.call-start = ((), (), s32[]{:S(2)}) async-start(), calls=%async_computation.9 | async-start | bytes 7077888 | tf_op jit(solution)/shard_map/reduce_scatter | solution.py:333
  787.6 50.7 %collective-permute-start.2 = (bf16[512,2048]{0,1:T(8,128)(2,1)S(1)}, bf16[512,2048]{0,1:T(8,128)(2,1)S(1)}, u32[]{:S(2)}, u32[]{:S(2)}) collective-permute-start(bf16[512,2048]{0,1:T(8,128)(2,1)S(1)} %get-tuple-element.899), channel_id=1, source_target_pairs={{8,0},{16,8},{24,16},{9,1},{17,9},{25,17},{10,2},{18,10},{26,18},{... | collective-permute-start | bytes 6291464 | tf_op jit(solution)/shard_map/ppermute | solution.py:35
  788.9 49.4 %collective-permute-start.3 = (bf16[512,2048]{0,1:T(8,128)(2,1)S(1)}, bf16[512,2048]{0,1:T(8,128)(2,1)S(1)}, u32[]{:S(2)}, u32[]{:S(2)}) collective-permute-start(bf16[512,2048]{0,1:T(8,128)(2,1)S(1)} %get-tuple-element.900), channel_id=1, source_target_pairs={{0,8},{8,16},{16,24},{1,9},{9,17},{17,25},{2,10},{10,18},{18,26},{... | collective-permute-start | bytes 6291464 | tf_op jit(solution)/shard_map/ppermute | solution.py:35
  841.3 2.0 copy-start.15
  841.3 2.0 copy-start.29
  841.4 2.0 copy-start.31
  841.5 7.0 copy-start.21
  847.9 1.8 copy-start.9
  847.9 1.8 copy-start.47
  858.3 233.1 %reduce-scatter.12.cloned.1.call-start = ((), (), s32[]{:S(2)}) async-start(), calls=%async_computation.11 | async-start | bytes 12976128 | tf_op jit(solution)/shard_map/reduce_scatter | solution.py:242
  873.4 249.7 %reduce-scatter.16.cloned.1.call-start = ((), (), s32[]{:S(2)}) async-start(), calls=%async_computation.13 | async-start | bytes 294912
  883.1 223.9 %copy-start.45 = (f32[512]{0:T(512)S(1)}, f32[512]{0:T(512)}, u32[]{:S(2)}) copy-start(f32[512]{0:T(512)} %copy-done.44) | copy-start | bytes 6148
  883.1 224.0 %copy-start.12 = (f32[512,1024]{1,0:T(8,128)S(1)}, f32[512,1024]{1,0:T(8,128)}, u32[]{:S(2)}) copy-start(f32[512,1024]{1,0:T(8,128)} %copy-done.10) | copy-start | bytes 6291460
  884.0 329.7 %all-reduce.15.cloned.1.call-start = ((), (), s32[]{:S(2)}) async-start(), calls=%async_computation.14 | async-start | bytes 6422528 | tf_op jit(solution)/shard_map/psum | solution.py:343
  1213.8 4.4 copy-start.27
  1213.8 5.6 copy-start.20
  (23 other events, 27.5 us)
Sparse Core Ops, SparseCore 0:
  9.7 67.5 all-gather.4
  78.8 27.6 all-gather.6
  108.2 107.5 all-gather.8
  217.3 58.7 all-gather.10
  385.7 35.7 reduce-scatter.9
  423.6 63.4 reduce-scatter.13
  858.4 112.9 reduce-scatter.7
  973.8 117.6 reduce-scatter.11
  1094.3 28.7 reduce-scatter.15
  1126.8 86.9 all-reduce.14
where the time goes:
time: 1240 us; the launch traced here: 1230 us
  matrix products  445 us (36%)
  waiting for transfers between devices  443 us (36%)
  blocking collectives  114 us (9%)
  other arithmetic  97.5 us (8%)
  local copies, waits for them, and re-layouts  95.7 us (8%)
  between operations  18.9 us (2%)
  starting transfers between devices  14.2 us (1%)
    reduce_scatter x1, waiting for transfers between devices, per_device(): lax.psum_scatter(grad_upper.astype(jnp.bfloat16), 'fsdp', scatter_dimensi...  120 us
    reduce_scatter x1, waiting for transfers between devices, per_device(): lax.psum_scatter(grad_qkv.astype(jnp.bfloat16), 'fsdp', scatter_dimension...  87.3 us
    dot_general x8, matrix products, backward_group(): jnp.einsum('hqk,khd->qhd', d_raw_low, key_blk, preferred_element_type=jnp...  79.5 us
    psum x1, waiting for transfers between devices, per_device(): lax.psum(attn_parts[2].astype(jnp.bfloat16), 'ctx').astype(jnp.float32)  78.9 us
    dot_general x8, matrix products, backward_group(): jnp.einsum('hqk,qhd->khd', d_raw_low, query_blk, preferred_element_type=j...  78.4 us
    sub x8, matrix products, backward_group(): d_scores = prob * (d_prob - jnp.sum(prob * d_prob, axis=-1, keepdims=True))  65.4 us
    psum x1, blocking collectives, per_device(): lax.psum((jnp.sum(query_obs.astype(jnp.float32)), jnp.sum(valid_col * dis...  63.3 us
    dot_general x16, matrix products, block_scores(): jnp.einsum('qhd,khd->hqk', query_blk, key_blk, preferred_element_type=jnp...  55.1 us
  transfers between devices with their start and end apart: 14, of which 9 were waited for; matrix products, arithmetic and copies ran while one was open for 46% of the time, Pallas kernels for 0%

commit v1 on v0

v1 whole, which is shorter than its diff:
```python
import math

import jax
import jax.numpy as jnp
from jax import lax
from jax.experimental import pallas as pl
from jax.experimental.pallas import tpu as pltpu
from jax.sharding import PartitionSpec as P


D=1024; HEADS=16; HEAD=64; FF=2816; WINDOW=1024
EPSILON=1e-6; MASKED=-1e30
HALF=WINDOW//2
LANES=128
VAR_AT, LSE_AT, OBS_AT = 8, 32, 35
TILE=256
F32=jnp.float32; BF=jnp.bfloat16


def dot_nn(a,b): return lax.dot_general(a,b,(((1,),(0,)),((),())),preferred_element_type=F32)
def dot_nt(a,b): return lax.dot_general(a,b,(((1,),(1,)),((),())),preferred_element_type=F32)
def dot_tn(a,b): return lax.dot_general(a,b,(((0,),(0,)),((),())),preferred_element_type=F32)

def halves(v):
    high=v.astype(BF)
    return jnp.concatenate([high,(v-high.astype(F32)).astype(BF)],axis=1)

def thirds(v,rounded=lambda a: a.astype(BF).astype(F32)):
    high=rounded(v)
    rest=v-high
    mid=rounded(rest)
    return high,mid,rest-mid

def lane_of(shape): return lax.broadcasted_iota(jnp.int32,shape,1)

def place(v,at):
    high,mid,low=thirds(v)
    lane=lane_of(v.shape)%HEAD
    return jnp.where(lane==at,high,jnp.where(lane==at+1,mid,jnp.where(lane==at+2,low,0.0)))

def band(s,t,tiles,key_axis):
    if t not in (0,tiles-1): return s
    key=lax.broadcasted_iota(jnp.int32,s.shape,key_axis)
    query=lax.broadcasted_iota(jnp.int32,s.shape,1-key_axis)
    keep=key>=query if t==0 else key<=query
    return jnp.where(keep,s,MASKED)

def prep(u,gain,cosine,sine,mean_mat,swap_mat):
    mean=dot_nn(halves(u*u),mean_mat)
    c=lax.rsqrt(mean+EPSILON)
    n=u*c*gain
    return n*cosine+dot_nn(halves(n),swap_mat)*sine, c

def fwd_kernel(xn_ref,wq_ref,wk_ref,wv_ref,gq_ref,gk_ref,cos_ref,sin_ref,qb_ref,kb_ref,sv_ref,mean_ref,swap_ref,
               q_ref,k_ref,v_ref,attn_ref,lse_ref,cq_ref,ck_ref):
    rows=qb_ref.shape[0]; ext=kb_ref.shape[0]
    tiles=2*HALF//TILE+1
    mean_mat=mean_ref[...]; swap_mat=swap_ref[...]
    first=(lane_of((1,LANES))<HEAD)
    kf=dot_nn(xn_ref[...],wk_ref[...])
    for pair in range(2):
        col=slice(pair*LANES,(pair+1)*LANES)
        rot,c=prep(kf[:,col],gk_ref[:,col],cos_ref[...],sin_ref[...],mean_mat,swap_mat)
        k_ref[:,col]=rot.astype(BF)
        if pair==0: ck_ref[...]=c
        else: ck_ref[...]=jnp.where(lane_of((1,LANES))%HEAD==pair,c,ck_ref[...])
    v_ref[...]=dot_nn(xn_ref[...],wv_ref[...]).astype(BF)
    qf=dot_nn(xn_ref[HALF:HALF+rows,:],wq_ref[...])
    for pair in range(2):
        col=slice(pair*LANES,(pair+1)*LANES)
        rot,c=prep(qf[:,col],gq_ref[:,col],cos_ref[HALF:HALF+rows,:],sin_ref[HALF:HALF+rows,:],mean_mat,swap_mat)
        q_ref[:,col]=rot.astype(BF)
        if pair==0: cq_ref[...]=c
        else: cq_ref[...]=jnp.where(lane_of((1,LANES))%HEAD==pair,c,cq_ref[...])
    own=[first.astype(F32).astype(BF),(1.0-first.astype(F32)).astype(BF)]
    no_obs=(lane_of((1,LANES))%HEAD!=OBS_AT).astype(F32).astype(BF)
    diag=lax.broadcasted_iota(jnp.int32,(TILE,TILE),0)==lax.broadcasted_iota(jnp.int32,(TILE,TILE),1)
    for pair in range(2):
        col=slice(pair*LANES,(pair+1)*LANES)
        for i in range(rows//TILE):
            sums=[]
            for par in range(2):
                m,other=own[par],own[1-par]
                sv=sv_ref[2*pair+par:2*pair+par+1,:].astype(BF)*other
                qi=q_ref[i*TILE:(i+1)*TILE,col]*BF(HEAD**-0.5)*m+qb_ref[i*TILE:(i+1)*TILE,:]*sv
                acc=None
                for t in range(tiles):
                    at=slice((i+t)*TILE,(i+t+1)*TILE)
                    kt=k_ref[at,col]*m+kb_ref[at,:]*other
                    vt=v_ref[at,col]*m+other
                    s=band(dot_nt(qi,kt),t,tiles,1)
                    if t==tiles//2:
                        s=jnp.where(diag,dot_nt(qi*(m+other*no_obs),kt),s)
                    p=jnp.exp(s).astype(BF)
                    o=dot_nn(p,vt)
                    acc=o if acc is None else acc+o
                sums.append(acc)
            total=jnp.where(first,sums[1],sums[0])
            lse_ref[i*TILE:(i+1)*TILE,col]=jnp.log(total)
            out=jnp.where(first,sums[0],sums[1])/pltpu.roll(total,HEAD,1)
            attn_ref[i*TILE:(i+1)*TILE,col]=out.astype(BF)

def prep_back(rot,d_rot,c,gain,cosine,sine,mean_mat,swap_mat):
    x=rot.astype(F32)
    m=dot_nn(halves(x*d_rot),mean_mat)
    e=d_rot*cosine-dot_nn(halves(d_rot),swap_mat)*sine
    swapped=dot_nn(rot,swap_mat[:LANES])
    n=(x*cosine-swapped*sine)/gain
    return c*(gain*e-n*m), jnp.sum(e*n,axis=0,keepdims=True)

def bwd_kernel(q_ref,k_ref,v_ref,do_ref,attn_ref,lse_ref,cq_ref,ck_ref,gq_ref,gk_ref,cos_ref,sin_ref,qb_ref,kb_ref,sv_ref,
               mean_ref,swap_ref,cross_ref,spread_ref,
               dq_ref,dk_ref,dv_ref,dgq_ref,dgk_ref,bias_ref,dk_acc,dv_acc,ke_ref,ve_ref):
    rows=qb_ref.shape[0]; ext=kb_ref.shape[0]
    tiles=2*HALF//TILE+1
    mean_mat=mean_ref[...]; swap_mat=swap_ref[...]
    first=(lane_of((1,LANES))<HEAD)
    own=[first.astype(F32).astype(BF),(1.0-first.astype(F32)).astype(BF)]
    no_obs=(lane_of((1,LANES))%HEAD!=OBS_AT).astype(F32).astype(BF)
    diag=lax.broadcasted_iota(jnp.int32,(TILE,TILE),0)==lax.broadcasted_iota(jnp.int32,(TILE,TILE),1)
    lane=lane_of((1,LANES))%HEAD
    is_var=(lane>=VAR_AT)&(lane<VAR_AT+8)
    bias_ref[...]=jnp.zeros_like(bias_ref)
    def one_pair(pair,_):
        col=pl.ds(pl.multiple_of(pair*LANES,LANES),LANES)
        dk_acc[...]=jnp.zeros_like(dk_acc)
        dv_acc[...]=jnp.zeros_like(dv_acc)
        prod=do_ref[:,col].astype(F32)*attn_ref[:,col].astype(F32)
        delta=place(dot_nn(halves(prod),cross_ref[...]),0).astype(BF)
        lse=place(lse_ref[:,col],LSE_AT).astype(BF)
        dqs=[]
        for par in range(2):
            m,other=own[par],own[1-par]
            head=2*pair+par
            sv=sv_ref[pl.ds(head,1),:].astype(BF)*other
            qm=q_ref[:,col]*BF(HEAD**-0.5)*m
            qe=qm+qb_ref[...]*sv-lse*other
            dm=do_ref[:,col]*m
            de=dm-delta*other
            ke_ref[...]=k_ref[:,col]*m+kb_ref[...]*other
            ve_ref[...]=v_ref[:,col]*m+other
            parts=[]
            for i in range(rows//TILE):
                r=slice(i*TILE,(i+1)*TILE)
                dq=None
                for t in range(tiles):
                    at=slice((i+t)*TILE,(i+t+1)*TILE)
                    kt=ke_ref[at,:]
                    s=band(dot_nt(kt,qe[r]),t,tiles,0)
                    if t==tiles//2:
                        s=jnp.where(diag,dot_nt(kt,qe[r]*(m+other*no_obs)),s)
                    p=jnp.exp(s)
                    ds=(p*dot_nt(ve_ref[at,:],de[r])).astype(BF)
                    dv_acc[at,:]+=dot_nn(p.astype(BF),dm[r])
                    dk_acc[at,:]+=dot_nn(ds,qm[r])
                    part=dot_tn(ds,kt)
                    dq=part if dq is None else dq+part
                parts.append(dq)
            dq=jnp.concatenate(parts,axis=0)
            hot=jnp.where(is_var&(first!=(par==0)),dq*qb_ref[...].astype(F32),0.0)
            bias_ref[pl.ds(head,1),:]=jnp.sum(hot,axis=0,keepdims=True)
            dqs.append(dq)
        d_rot=jnp.where(first,dqs[0],dqs[1])*(HEAD**-0.5)
        spread=spread_ref[pair]
        cosq,sinq=cos_ref[HALF:HALF+rows,:],sin_ref[HALF:HALF+rows,:]
        du,dg=prep_back(q_ref[:,col],d_rot,dot_nn(halves(cq_ref[...]),spread),gq_ref[:,col],cosq,sinq,mean_mat,swap_mat)
        dq_ref[:,col]=du.astype(BF)
        dgq_ref[:,col]=dg
        du,dg=prep_back(k_ref[:,col],dk_acc[...],dot_nn(halves(ck_ref[...]),spread),gk_ref[:,col],cos_ref[...],sin_ref[...],mean_mat,swap_mat)
        dk_ref[:,col]=du.astype(BF)
        dgk_ref[:,col]=dg
        dv_ref[:,col]=dv_acc[...].astype(BF)
        return 0
    lax.fori_loop(0,2,one_pair,0)

def blockdiag():
    i=jnp.arange(LANES)
    mean=jnp.where(i[:,None]//HEAD==i[None]//HEAD,1.0/HEAD,0.0)
    cross=jnp.where(i[:,None]//HEAD!=i[None]//HEAD,1.0,0.0)
    swap=jnp.where(i[None]==i[:,None]+jnp.where(i[:,None]%HEAD<HEAD//2,HEAD//2,-(HEAD//2)),1.0,0.0)
    spread=jnp.stack([jnp.where(i[:,None]==pair+HEAD*(i[None]//HEAD),1.0,0.0) for pair in range(2)])
    two=lambda a: jnp.concatenate([a,a],axis=-2).astype(BF)
    return two(mean),two(swap),two(cross),two(spread)

def full(*shape):
    n=len(shape)
    return pl.BlockSpec(shape,lambda j:(0,)*n)
def colb(rows,width,off=0): return pl.BlockSpec((rows,width),lambda j:(0,j+off))
def lead(*shape): return pl.BlockSpec((None,)+shape,lambda j:(j,)+(0,)*len(shape))

def attention_forward(xn,w_qkv,gq,gk,cos,sin,qb,kb,sv,mats,groups=4):
    rows,ext=qb.shape[0],kb.shape[0]
    mean_mat,swap_mat,_,_=mats
    n=groups*256
    return pl.pallas_call(
        fwd_kernel,grid=(groups,),
        in_specs=[full(ext,D),colb(D,256),colb(D,256,groups),colb(D,256,2*groups),lead(1,256),lead(1,256),full(ext,LANES),full(ext,LANES),
                  full(rows,LANES),full(ext,LANES),lead(8,LANES),full(2*LANES,LANES),full(2*LANES,LANES)],
        out_specs=[colb(rows,256),colb(ext,256),colb(ext,256),colb(rows,256),colb(rows,256),lead(rows,LANES),lead(ext,LANES)],
        out_shape=[jax.ShapeDtypeStruct((rows,n),BF),jax.ShapeDtypeStruct((ext,n),BF),jax.ShapeDtypeStruct((ext,n),BF),
                   jax.ShapeDtypeStruct((rows,n),BF),jax.ShapeDtypeStruct((rows,n),F32),
                   jax.ShapeDtypeStruct((groups,rows,LANES),F32),jax.ShapeDtypeStruct((groups,ext,LANES),F32)],
        compiler_params=pltpu.CompilerParams(vmem_limit_bytes=56*2**20),
        name="attention_forward",
    )(xn,w_qkv,w_qkv,w_qkv,gq,gk,cos,sin,qb,kb,sv,mean_mat,swap_mat)

def attention_backward(q,k,v,do,attn,lse,cq,ck,gq,gk,cos,sin,qb,kb,sv,mats,groups=4):
    rows,ext=qb.shape[0],kb.shape[0]
    n=groups*256
    return pl.pallas_call(
        bwd_kernel,grid=(groups,),
        in_specs=[colb(rows,256),colb(ext,256),colb(ext,256),colb(rows,256),colb(rows,256),colb(rows,256),lead(rows,LANES),lead(ext,LANES),
                  lead(1,256),lead(1,256),full(ext,LANES),full(ext,LANES),full(rows,LANES),full(ext,LANES),lead(8,LANES),
                  full(2*LANES,LANES),full(2*LANES,LANES),full(2*LANES,LANES),full(2,2*LANES,LANES)],
        out_specs=[colb(rows,256),colb(ext,256),colb(ext,256),lead(1,256),lead(1,256),lead(8,LANES)],
        out_shape=[jax.ShapeDtypeStruct((rows,n),BF),jax.ShapeDtypeStruct((ext,n),BF),jax.ShapeDtypeStruct((ext,n),BF),
                   jax.ShapeDtypeStruct((groups,1,256),F32),jax.ShapeDtypeStruct((groups,1,256),F32),jax.ShapeDtypeStruct((groups,8,LANES),F32)],
        scratch_shapes=[pltpu.VMEM((ext,LANES),F32),pltpu.VMEM((ext,LANES),F32),pltpu.VMEM((ext,LANES),BF),pltpu.VMEM((ext,LANES),BF)],
        compiler_params=pltpu.CompilerParams(vmem_limit_bytes=56*2**20),
        name="attention_backward",
    )(q,k,v,do,attn,lse,cq,ck,gq,gk,cos,sin,qb,kb,sv,*mats)

def features(query_doc,query_var,key_doc,key_var,key_obs,key_inside):
    lane=jnp.arange(HEAD)[None,:]
    var_lane=(lane>=VAR_AT)&(lane<LSE_AT)
    def tile(a): return jnp.concatenate([a,a],axis=1).astype(BF)
    qv=var_lane&((lane-VAR_AT)%8==query_var[:,None])
    q=((lane<VAR_AT)&(lane==query_doc[:,None]))|qv|(lane==OBS_AT)
    kv=var_lane&((lane-VAR_AT)%8==key_var[:,None])
    closed=(lane<VAR_AT)&~((lane==key_doc[:,None])&key_inside[:,None])
    closed=closed|((lane==OBS_AT)&(key_obs[:,None]!=1))
    ones=kv|((lane>=LSE_AT)&(lane<LSE_AT+3))
    k=jnp.where(closed,MASKED,jnp.where(ones,1.0,0.0))
    return tile(q.astype(F32)),tile(k)

def head_scales(bias_f):
    high,mid,low=thirds(bias_f[:HEADS]-bias_f[HEADS:],lambda a: lax.reduce_precision(a,8,7))
    lane=jnp.arange(HEAD)[None,:]
    part=lambda a: a[:,None]
    s=jnp.where(lane<VAR_AT,1.0,jnp.where(lane<VAR_AT+8,part(high),jnp.where(lane<VAR_AT+16,part(mid),jnp.where(lane<LSE_AT,part(low),1.0))))
    s=jnp.where(lane>OBS_AT,0.0,s)
    s=jnp.concatenate([s,s],axis=1).reshape(HEADS//4,4,LANES)
    return jnp.concatenate([s,jnp.zeros_like(s)],axis=1)

def tables(pos):
    half=HEAD//2
    freq=jnp.exp(jnp.arange(half).astype(F32)*(-2.0*math.log(10000.0)/HEAD))
    ang=pos.astype(F32)[:,None]*freq[None,:]
    c,s=jnp.cos(ang),jnp.sin(ang)
    return jnp.concatenate([c,c,c,c],axis=1),jnp.concatenate([-s,s,-s,s],axis=1)


def shifted(shard, by):
    size = lax.axis_size("ctx")
    return lax.ppermute(shard, "ctx", [(i, i + by) for i in range(size) if 0 <= i + by < size])


def document_ids(doc_lengths, positions):
    doc_ends = jnp.cumsum(doc_lengths)
    return jnp.sum((positions[:, None] >= doc_ends[None, :]).astype(jnp.int32), axis=1)


def rms_scale(vector, scales):
    return vector * lax.rsqrt(jnp.mean(vector * vector, axis=-1, keepdims=True) + EPSILON) * scales


def gated_unit(gate_up):
    gate_part = gate_up[:, :FF]
    up_part = gate_up[:, FF:]
    return gate_part / (1.0 + jnp.exp(-gate_part)) * up_part


def per_device(tokens, teacher, cotangent, lengths, variate, observed, norm_gains, var_bias, qkv_weight, out_weight, ffn_in, ffn_out):
    rows = tokens.shape[1]
    n_context = lax.axis_size("ctx")
    n_shards = lax.axis_size("fsdp")
    ext = rows + 2 * HALF
    start = lax.axis_index("ctx") * rows
    seq_len = observed.shape[1]
    gains_n = norm_gains.shape[1]
    bias_n = var_bias.shape[0]

    own_count = jnp.sum(observed[0])
    small = jnp.zeros((16, gains_n), BF)
    small = small.at[:4].set(norm_gains).at[4, :bias_n].set(var_bias)
    small = small.at[5, 0].set((own_count // 256).astype(BF)).at[5, 1].set((own_count % 256).astype(BF))
    before, after = shifted(tokens[0], 1), shifted(tokens[0], -1)
    w_qkv = lax.all_gather(qkv_weight, "fsdp", axis=0, tiled=True)
    small = lax.all_gather(small, "fsdp", axis=0)
    w_attn = lax.all_gather(out_weight, "fsdp", axis=0, tiled=True)
    w_upper = lax.all_gather(ffn_in, "fsdp", axis=0, tiled=True)
    w_lower = lax.all_gather(ffn_out, "fsdp", axis=0, tiled=True)

    gains = jnp.moveaxis(small[:, :4], 0, 1).reshape(4, D).astype(F32)
    bias = small[:, 4, :bias_n].reshape(2 * HEADS).astype(F32)
    valid_total = jnp.sum(small[:, 5, 0].astype(F32) * 256.0 + small[:, 5, 1].astype(F32))

    key_pos = start - HALF + jnp.arange(ext, dtype=jnp.int32)
    inside = (key_pos >= 0) & (key_pos < seq_len)
    key_doc = document_ids(lengths[0], key_pos)
    key_var = lax.dynamic_slice_in_dim(jnp.pad(variate[0], HALF), start, ext, 0)
    key_obs = lax.dynamic_slice_in_dim(jnp.pad(observed[0], HALF), start, ext, 0)
    own = slice(HALF, HALF + rows)
    query_feat, key_feat = features(key_doc[own], key_var[own], key_doc, key_var, key_obs, inside)
    cosine, sine = tables(key_pos)
    scales = head_scales(bias)
    mats = blockdiag()
    gain_q, gain_k = gains[2].reshape(-1, 1, 256), gains[3].reshape(-1, 1, 256)

    inputs = jnp.concatenate([before, tokens[0], after], axis=0).astype(F32)
    inv = lax.rsqrt(jnp.mean(inputs * inputs, axis=-1, keepdims=True) + EPSILON)
    normed = (inputs * inv * gains[0]).astype(BF)

    q, k, v, attn, lse, c_q, c_k = attention_forward(normed, w_qkv, gain_q, gain_k, cosine, sine, query_feat, key_feat, scales, mats)
    mixed = tokens[0].astype(F32) + jnp.dot(attn, w_attn, preferred_element_type=F32)
    normed_two_f, norm_two_pull = jax.vjp(rms_scale, mixed, gains[1])
    normed_two = normed_two_f.astype(BF)
    gate_up = jnp.dot(normed_two, w_upper, preferred_element_type=F32)
    hidden_f, glu_pull = jax.vjp(gated_unit, gate_up)
    hidden = hidden_f.astype(BF)
    final = mixed + jnp.dot(hidden, w_lower, preferred_element_type=F32)
    valid_col = key_obs[own].astype(F32)[:, None]
    distance = final - teacher[0].astype(F32)
    squared = jnp.sum(valid_col * distance * distance)
    all_tokens = rows * n_context * n_shards
    d_final = cotangent[0].astype(F32) + all_tokens * valid_col * distance / valid_total
    d_final_low = d_final.astype(BF)
    grad_lower = dot_tn(hidden, d_final_low)
    ffn_out_part = lax.psum_scatter(grad_lower.astype(BF), "fsdp", scatter_dimension=0, tiled=True)
    d_hidden = dot_nt(d_final_low, w_lower)
    (d_gate_up,) = glu_pull(d_hidden)
    d_gate_low = d_gate_up.astype(BF)
    grad_upper = dot_tn(normed_two, d_gate_low)
    ffn_in_part = lax.psum_scatter(grad_upper.astype(BF), "fsdp", scatter_dimension=0, tiled=True)
    d_normed_two = dot_nt(d_gate_low, w_upper)
    d_mixed_part, grad_norm_two = norm_two_pull(d_normed_two)
    d_mixed = d_final + d_mixed_part
    d_mixed_low = d_mixed.astype(BF)
    d_attn = dot_nt(d_mixed_low, w_attn).astype(BF)
    grad_attn = dot_tn(attn, d_mixed_low)
    out_part = lax.psum_scatter(grad_attn.astype(BF), "fsdp", scatter_dimension=0, tiled=True)

    d_q, d_k, d_v, d_gain_q, d_gain_k, d_bias = attention_backward(
        q, k, v, d_attn, attn, lse, c_q, c_k, gain_q, gain_k, cosine, sine, query_feat, key_feat, scales, mats
    )
    grad_qkv = jnp.concatenate(
        [dot_tn(normed[own], d_q).astype(BF), dot_tn(normed, d_k).astype(BF), dot_tn(normed, d_v).astype(BF)], axis=1
    )
    qkv_part = lax.psum_scatter(grad_qkv, "fsdp", scatter_dimension=0, tiled=True)
    d_ext = dot_nt(d_k, w_qkv[:, D : 2 * D]) + dot_nt(d_v, w_qkv[:, 2 * D :])
    from_next = shifted(d_ext[:HALF].astype(BF), -1)
    from_prev = shifted(d_ext[HALF + rows :].astype(BF), 1)
    d_own = d_ext[own] + dot_nt(d_q, w_qkv[:, :D])
    unit = inputs * inv
    grad_norm_one = (
        jnp.sum(d_own * unit[own], axis=0)
        + jnp.sum(d_ext[:HALF] * unit[:HALF], axis=0)
        + jnp.sum(d_ext[HALF + rows :] * unit[HALF + rows :], axis=0)
    )
    d_own = d_own.at[rows - HALF :].add(from_next.astype(F32)).at[:HALF].add(from_prev.astype(F32))
    scaled = d_own * gains[0]
    input_grad = d_mixed + inv[own] * (scaled - unit[own] * jnp.mean(unit[own] * scaled, axis=-1, keepdims=True))

    same = jnp.sum(d_bias[:, :4], axis=-1).reshape(HEADS)
    sums = jnp.concatenate(
        [grad_norm_one, grad_norm_two, d_gain_q.reshape(D), d_gain_k.reshape(D), same, jnp.full((LANES,), squared)]
    )
    sums = lax.psum(jnp.pad(sums, (0, -sums.shape[0] % (8 * LANES))).reshape(-1, LANES), ("ctx", "fsdp")).reshape(-1)
    loss = sums[4 * D + HEADS] / (valid_total * D)
    me = lax.axis_index("fsdp")
    gains_grad = lax.dynamic_slice_in_dim(sums[: 4 * D].reshape(4, D), me * gains_n, gains_n, 1)
    bias_sum = sums[4 * D : 4 * D + HEADS]
    var_bias_grad = lax.dynamic_slice_in_dim(jnp.concatenate([bias_sum, -bias_sum]), me * bias_n, bias_n, 0)
    qkv_grad, out_grad, in_grad, low_grad = lax.psum((qkv_part, out_part, ffn_in_part, ffn_out_part), "ctx")
    return (
        loss,
        final.astype(BF)[None],
        input_grad[None],
        gains_grad,
        var_bias_grad,
        qkv_grad.astype(F32),
        out_grad.astype(F32),
        in_grad.astype(F32),
        low_grad.astype(F32),
    )


def solution(mesh):
    split = P("fsdp", "ctx", None)
    rows = P("fsdp", None)
    return jax.shard_map(
        per_device,
        mesh=mesh,
        in_specs=(split, split, split, rows, rows, rows, P(None, "fsdp"), P("fsdp"), rows, rows, rows, rows),
        out_specs=(P(), split, split, P(None, "fsdp"), P("fsdp"), rows, rows, rows, rows),
        check_vma=False,
    )
```

time: 1240 us -> 824 us (0.66)
  matrix products: 445 us -> 107 us
  Pallas kernels: 0 us -> 107 us
  local copies, waits for them, and re-layouts: 95.7 us -> 27.6 us
  blocking collectives: 114 us -> 53.4 us
  other arithmetic: 97.5 us -> 53.5 us
    dot_general x68 -> x15, matrix products: 379 us -> 107 us  [the longest x6 48.6 us: dot_nt(): lax.dot_general(a, b, (((1,), (1,)), ((), ())), preferred_element_type=F32)]
    pallas_call x0 -> x2, Pallas kernels: none -> 107 us  [the longest x1 65.5 us: attention_backward(): pl.pallas_call(bwd_kernel, grid=(groups,), in_specs=[colb(rows, 256), col...]
    all_gather x4, waiting for transfers between devices: 72.8 us -> 156 us  [the longest x1 93.9 us: per_device(): w_upper = lax.all_gather(ffn_in, 'fsdp', axis=0, tiled=True)]
    ppermute x4, waiting for transfers between devices: 69.3 us -> 0.01 us  [shifted(): lax.ppermute(shard, 'ctx', [(i, i + by) for i in range(size) if 0 <= i +...]
    sub x8 -> x0, matrix products: 65.4 us -> none  [backward_group(): d_scores = prob * (d_prob - jnp.sum(prob * d_prob, axis=-1, keepdims=True))]
    psum x1, waiting for transfers between devices: 78.9 us -> 34.8 us  [per_device(): lax.psum((qkv_part, out_part, ffn_in_part, ffn_out_part), 'ctx')]
    and x16 -> x2, other arithmetic: 37.4 us -> 0.01 us  [the longest x1 0.01 us: features(): var_lane = (lane >= VAR_AT) & (lane < LSE_AT)]
    psum x2 -> x1, blocking collectives: 73.1 us -> 38.4 us  [per_device(): lax.psum(jnp.pad(sums, (0, -sums.shape[0] % (8 * LANES))).reshape(-1, LAN...]
  transfers between devices with their start and end apart: 14 -> 13, of which waited for: 9 -> 8; matrix products, arithmetic and copies ran while one was open for 46% -> 12% of each run, Pallas kernels for 0% -> 5%
where the time goes in v1:
time: 824 us; the launch traced here: 815 us
  waiting for transfers between devices  435 us (53%)
  Pallas kernels  107 us (13%)
  matrix products  107 us (13%)
  other arithmetic  53.5 us (6%)
  blocking collectives  53.4 us (6%)
  local copies, waits for them, and re-layouts  27.6 us (3%)
  between operations  19.9 us (2%)
  starting transfers between devices  12.3 us (1%)
    reduce_scatter x1, waiting for transfers between devices, per_device(): lax.psum_scatter(grad_upper.astype(BF), 'fsdp', scatter_dimension=0, tile...  120 us
    all_gather x1, waiting for transfers between devices, per_device(): w_upper = lax.all_gather(ffn_in, 'fsdp', axis=0, tiled=True)  93.9 us
    reduce_scatter x1, waiting for transfers between devices, per_device(): lax.psum_scatter(grad_lower.astype(BF), 'fsdp', scatter_dimension=0, tile...  66 us
    pallas_call x1, Pallas kernels, attention_backward(): pl.pallas_call(bwd_kernel, grid=(groups,), in_specs=[colb(rows, 256), col...  65.5 us
    dot_general x6, matrix products, dot_nt(): lax.dot_general(a, b, (((1,), (1,)), ((), ())), preferred_element_type=F32)  48.6 us
    all_gather x1, waiting for transfers between devices, per_device(): w_lower = lax.all_gather(ffn_out, 'fsdp', axis=0, tiled=True)  43.5 us
    pallas_call x1, Pallas kernels, attention_forward(): pl.pallas_call(fwd_kernel, grid=(groups,), in_specs=[full(ext, D), colb(D...  41.2 us
    psum x1, blocking collectives, per_device(): lax.psum(jnp.pad(sums, (0, -sums.shape[0] % (8 * LANES))).reshape(-1, LAN...  38.4 us
  transfers between devices with their start and end apart: 13, of which 8 were waited for; matrix products, arithmetic and copies ran while one was open for 12% of the time, Pallas kernels for 5%

profile of v1, /device:TPU:0, one launch (start us, length us, event | category | flops | bytes accessed | tf_op | source)
XLA Modules:
  0.0 815.4 jit_solution(16034836960044190014)
XLA Ops:
  9.5 1.3 collective-permute-start.1
  10.8 5.5 collective-permute-start
  20.2 15.0 %all_gather.28 = bf16[8,16,128]{2,1,0:T(8,128)(2,1)S(1)} all-gather(bf16[1,16,128]{2,1,0:T(8,128)(2,1)S(1)} %scatter.19), channel_id=1, replica_groups=mesh['ctx'=4,'fsdp'=8] {'fsdp'}, dimensions={0}, use_global_device_ids=true | all-gather | bytes 36864 | tf_op jit(solution)/shard_map/all_gather | solution.py:289
  41.3 1.5 select_convert_fusion
  43.9 2.8 fusion.27
  46.7 1.6 pad_maximum_fusion.2.cos_ref
  48.3 1.5 pad_maximum_fusion.3.sin_ref
  51.2 8.1 multiply_convert_fusion
  59.3 18.1 %all-gather.5.cloned.1.call-done.wq_ref.wk_ref.wv_ref = bf16[1024,3072]{1,0:T(8,128)(2,1)} async-done(((bf16[128,3072]{1,0:T(8,128)(2,1)}), bf16[1024,3072]{1,0:T(8,128)(2,1)}) %all-gather.5.cloned.1.call-update) | async-done | bytes 6291472 | tf_op jit(solution)/shard_map/all_gather | solution.py:288
  77.4 41.2 %attention_forward.1 = (bf16[512,1024]{1,0:T(8,128)(2,1)}, bf16[1536,1024]{1,0:T(8,128)(2,1)}, bf16[1536,1024]{1,0:T(8,128)(2,1)}, bf16[512,1024]{1,0:T(8,128)(2...) custom-call(bf16[1536,1024]{1,0:T(8,128)(2,1)} %get-tuple-element.177.xn_ref, ...), custom_call_target="tpu_custom_call" | custom-call | tf_op jit(solution)/shard_map/attention_forward/pallas_call | solution.py:195
  118.6 3.4 multiply_reduce_fusion.4
  122.1 93.9 %all-gather.9.cloned.1.call-done = bf16[1024,5632]{1,0:T(8,128)(2,1)} async-done(((bf16[128,5632]{1,0:T(8,128)(2,1)}), bf16[1024,5632]{1,0:T(8,128)(2,1)}) %all-gather.9.cloned.1.call-update) | async-done | bytes 11534352 | tf_op jit(solution)/shard_map/all_gather | solution.py:291
  216.0 9.1 %fusion.41 = f32[512,5632]{1,0:T(8,128)S(1)} fusion(bf16[1024,5632]{1,0:T(8,128)(2,1)} %all-gather.9.cloned.1.call-done, f32[512,1024]{1,0:T(8,128)S(1)} %get-tuple-element.199, f32[1024]{0:T(1024)S(1)} %bitcast.58, f32[512]{0:T(512)S(1)} %fusion.36), kind=kOutput, calls=%fused_computation.144 | convolution fusion | flops 5907152896 | bytes 25171968 | tf_op jit(solution)/shard_map/dot_general | solution.py:318
  225.1 4.3 copy-done.1
  229.4 3.3 multiply_convert_fusion.1
  232.7 43.5 %all-gather.11.cloned.1.call-done = bf16[2816,1024]{1,0:T(8,128)(2,1)} async-done(((bf16[352,1024]{1,0:T(8,128)(2,1)}), bf16[2816,1024]{1,0:T(8,128)(2,1)}) %all-gather.11.cloned.1.call-update) | async-done | bytes 5767184 | tf_op jit(solution)/shard_map/all_gather | solution.py:292
  276.2 9.7 %fusion.2 = (f32[]{:T(128)}, f32[512,1024]{1,0:T(8,128)S(1)}, bf16[1,512,1024]{2,1,0:T(8,128)(2,1)}) fusion(bf16[1,512,1024]{2,1,0:T(8,128)(2,1)S(1)} %copy-done.23, f32[512]{0:T(512)S(1)} %get-tuple-element.172, f32[]{:T(128)} %add_reduce_fusion, f32[512]{0:T(512)S(1)} %get-tuple-element.171, bf16[1,512,1024]{2,1,0:T(8,128)(2,1)} %param.30, ...), kind=kOutput, calls=%fused_computation.17 | convolution fusion | flops 2958557184 | bytes 15994888 | tf_op jit(solution)/shard_map/dot_general | solution.py:321
  286.0 12.0 %fusion.13 = (f32[512,2816]{1,0:T(8,128)}, f32[512,2816]{1,0:T(8,128)}) fusion(f32[512,5632]{1,0:T(8,128)S(1)} %copy-done.2, bf16[2816,1024]{1,0:T(8,128)(2,1)} %all-gather.11.cloned.1.call-done, f32[512,1024]{1,0:T(8,128)S(1)} %get-tuple-element.180), kind=kOutput, calls=%fused_computation.51 | convolution fusion | flops 2973499392 | bytes 30932992 | tf_op jit(solution)/shard_map/dot_general | solution.py:21
  298.0 13.5 %multiply_reduce_fusion.1 = (f32[1024]{0:T(1024)S(1)}, f32[512]{0:T(512)S(1)}, f32[512,1024]{1,0:T(8,128)}) fusion(f32[512,1024]{1,0:T(8,128)S(1)} %get-tuple-element.199, f32[512]{0:T(512)S(1)} %fusion.36, f32[1024]{0:T(1024)S(1)} %bitcast.59, bf16[1024,5632]{1,0:T(8,128)(2,1)} %all-gather.9.cloned.1.call-done, f32[512,2816]{1,0:T(8,128)} %get-tuple-element.174, ...), kind=kOutput, calls=%fused_computation.33 | convolution fusion | flops 5914491392 | bytes 27275264 | tf_op jit(solution)/shard_map/dot_general | solution.py:21
  311.6 3.5 fusion.1
  315.1 2.3 convolution_convert_fusion.6.do_ref
  317.3 65.5 %attention_backward.1 = (bf16[512,1024]{1,0:T(8,128)(2,1)}, bf16[1536,1024]{1,0:T(8,128)(2,1)}, bf16[1536,1024]{1,0:T(8,128)(2,1)}, f32[4,1,256]{2,1,0:T(1,128)}...) custom-call(bf16[512,1024]{1,0:T(8,128)(2,1)} %get-tuple-element.110.q_ref, bf16[1536,1024]{1,0:T(8,128)(2,1)} %get-tuple-element.111.k_ref, ...), custom_call_target="tpu_custom_call" | custom-call | tf_op jit(solution)/shard_map/attention_backward/pallas_call | solution.py:210
  382.9 5.8 convolution_convert_fusion.3
  388.7 3.8 convolution_convert_fusion.4
  392.5 1.3 convolution_convert_fusion.5
  393.8 13.6 %pad_maximum_fusion = bf16[1024,3072]{0,1:T(8,128)(2,1)} fusion(bf16[1024,1024]{0,1:T(8,128)(2,1)S(1)} %convolution_convert_fusion.3, bf16[1024,1024]{0,1:T(8,128)(2,1)S(1)} %convolution_convert_fusion.4, bf16[1024,1024]{0,1:T(8,128)(2,1)S(1)} %convolution_convert_fusion.5), kind=kLoop, calls=%fused_computation.5 | loop fusion | flops 18874368 | bytes 12582912 | tf_op jit(solution)/shard_map/concatenate | solution.py:346
  407.4 8.7 %copy.28 = bf16[1024,3072]{1,0:T(8,128)(2,1)} copy(bf16[1024,3072]{0,1:T(8,128)(2,1)} %pad_maximum_fusion) | data formatting | bytes 12582912
  417.3 2.6 convolution_convert_fusion.2
  419.9 8.6 %convolution_convert_fusion.1 = bf16[2816,1024]{1,0:T(8,128)(2,1)} fusion(bf16[512,2816]{1,0:T(8,128)(2,1)} %multiply_convert_fusion.1, f32[512,1024]{1,0:T(8,128)} %copy-done.5), kind=kOutput, calls=%fused_computation.11 | convolution fusion | flops 2956197888 | bytes 10747904 | tf_op jit(solution)/shard_map/dot_general | solution.py:22
  428.6 13.9 %convolution_convert_fusion = bf16[1024,5632]{1,0:T(8,128)(2,1)} fusion(f32[512,2816]{1,0:T(8,128)} %get-tuple-element.174, f32[512,2816]{1,0:T(8,128)} %get-tuple-element.173, f32[512,1024]{1,0:T(8,128)} %copy-done.3, f32[1024]{0:T(1024)S(1)} %bitcast.61, f32[512]{0:T(512)S(1)} %fusion.36), kind=kOutput, calls=%fused_computation.1 | convolution fusion | flops 5918687232 | bytes 25171968 | tf_op jit(solution)/shard_map/dot_general | solution.py:22
  442.9 6.3 fusion.8
  449.2 5.1 convolution_add_fusion
  454.3 1.8 fusion.43
  456.1 1.4 copy-done.9
  457.6 3.6 collective-permute-start.3
  461.2 1.3 collective-permute-start.2
  462.5 22.2 %reduce-scatter.13.cloned.1.call-done = bf16[128,3072]{1,0:T(8,128)(2,1)} async-done(((bf16[1024,3072]{1,0:T(8,128)(2,1)}), bf16[128,3072]{1,0:T(8,128)(2,1)}) %reduce-scatter.13.cloned.1.call-update) | async-done | bytes 786448
  484.7 2.3 copy.29
  487.0 34.5 %reduce-scatter.7.cloned.1.call-done = bf16[128,1024]{1,0:T(8,128)(2,1)} async-done(((bf16[1024,1024]{1,0:T(8,128)(2,1)}), bf16[128,1024]{1,0:T(8,128)(2,1)}) %reduce-scatter.7.cloned.1.call-update) | async-done | bytes 262160 | tf_op jit(solution)/shard_map/reduce_scatter | solution.py:341
  521.4 66.0 %reduce-scatter.11.cloned.1.call-done = bf16[352,1024]{1,0:T(8,128)(2,1)} async-done(((bf16[2816,1024]{1,0:T(8,128)(2,1)}), bf16[352,1024]{1,0:T(8,128)(2,1)}) %reduce-scatter.11.cloned.1.call-update) | async-done | bytes 720912 | tf_op jit(solution)/shard_map/reduce_scatter | solution.py:329
  587.4 120.0 %reduce-scatter.9.cloned.1.call-done = bf16[128,5632]{1,0:T(8,128)(2,1)} async-done(((bf16[1024,5632]{1,0:T(8,128)(2,1)}), bf16[128,5632]{1,0:T(8,128)(2,1)}) %reduce-scatter.9.cloned.1.call-update) | async-done | bytes 1441808 | tf_op jit(solution)/shard_map/reduce_scatter | solution.py:334
  709.0 9.3 %multiply_reduce_fusion = (f32[512]{0:T(512)S(1)}, f32[1024]{0:T(1024)S(1)}, f32[1024]{0:T(1024)S(1)}, f32[1024]{0:T(1024)S(1)}, f32[512,1024]{1,0:T(8,128)}) fusion(f32[1536,1024]{1,0:T(8,128)} %get-tuple-element.178, f32[1024]{0:T(1024)S(1)} %bitcast.67, bf16[512,1024]{1,0:T(8,128)(2,1)S(1)} %collective-permute-done.3, ...), kind=kOutput, calls=%fused_computation.31 | convolution fusion | flops 1081078272 | bytes 19941376 | tf_op jit(solution)/shard_map/dot_general | solution.py:21
  719.1 38.4 %psum.35 = f32[40,128]{1,0:T(8,128)S(1)} all-reduce(f32[40,128]{1,0:T(8,128)S(1)} %pad_bitcast_fusion), channel_id=1, replica_groups=mesh['ctx'=4,'fsdp'=8] {'ctx','fsdp'}, use_global_device_ids=true, to_apply=%region_13.14 | all-reduce | flops 5120 | bytes 40960 | tf_op jit(solution)/shard_map/psum | solution.py:368
  760.0 4.9 add_bitcast_fusion
  764.8 34.8 %all-reduce.10.cloned.1.call-done = (bf16[128,3072]{0,1:T(8,128)(2,1)}, bf16[128,1024]{1,0:T(8,128)(2,1)}, bf16[128,5632]{1,0:T(8,128)(2,1)}, bf16[352,1024]{1,0:T(8,128)(2,1)}) async-done(((bf16[128,3072]{0,1:T(8,128)(2,1)}, bf16[128,1024]{1,0:T(8,128)(2,1)}, bf16[128,5632]{1,0:T(8,128)(2,1)}, bf16[352,1024]{1,0:T(8,128)(2,1)}), (bf16[128,3072]{0,1:T(8,128)(2,1)}, bf16[128,1024]{1,0:T(8,128)(2,1)}, ...) | async-done | bytes 3211280 | tf_op jit(solution)/shard_map/psum | solution.py:374
  799.6 2.7 copy.27
  802.3 1.9 convert_element_type.177
  804.2 1.9 convert_element_type.179
  (137 shorter events, 18.1 us)
Async XLA Ops:
  7.2 9.2 %copy-start.10 = (s32[1,2048]{1,0:T(1,128)S(1)}, s32[1,2048]{1,0:T(1,128)}, u32[]{:S(2)}) copy-start(s32[1,2048]{1,0:T(1,128)} %param.33) | copy-start | bytes 24580
  7.2 12.6 %copy-start.18 = (bf16[4,128]{1,0:T(4,128)(2,1)S(1)}, bf16[4,128]{1,0:T(4,128)(2,1)}, u32[]{:S(2)}) copy-start(bf16[4,128]{1,0:T(4,128)(2,1)} %param.34) | copy-start | bytes 3076
  7.2 12.6 %copy-start.19 = (bf16[4]{0:T(256)(128)(2,1)S(1)}, bf16[4]{0:T(256)(128)(2,1)}, u32[]{:S(2)}) copy-start(bf16[4]{0:T(256)(128)(2,1)} %param.35) | copy-start | bytes 28
  7.2 28.0 %copy-start.25 = (s32[1,8]{1,0:T(1,128)S(1)}, s32[1,8]{1,0:T(1,128)}, u32[]{:S(2)}) copy-start(s32[1,8]{1,0:T(1,128)} %param.31) | copy-start | bytes 100
  7.2 28.6 %copy-start.14 = (s32[1,2048]{1,0:T(1,128)S(1)}, s32[1,2048]{1,0:T(1,128)}, u32[]{:S(2)}) copy-start(s32[1,2048]{1,0:T(1,128)} %param.32) | copy-start | bytes 24580
  7.2 70.2 %all-gather.5.cloned.1.call-start = ((), (), s32[]{:S(2)}) async-start(), calls=%async_computation.4 | async-start | bytes 7077888 | tf_op jit(solution)/shard_map/all_gather | solution.py:288
  8.0 110.7 %all-gather.7.cloned.1.call-start = ((), (), s32[]{:S(2)}) async-start(), calls=%async_computation.5 | async-start | bytes 2359296 | tf_op jit(solution)/shard_map/all_gather | solution.py:290
  8.7 207.3 %all-gather.9.cloned.1.call-start = ((), (), s32[]{:S(2)}) async-start(), calls=%async_computation.6 | async-start | bytes 12976128 | tf_op jit(solution)/shard_map/all_gather | solution.py:291
  9.4 266.8 %all-gather.11.cloned.1.call-start = ((), (), s32[]{:S(2)}) async-start(), calls=%async_computation.7 | async-start | bytes 6488064 | tf_op jit(solution)/shard_map/all_gather | solution.py:292
  9.5 40.3 %collective-permute-start.1 = (bf16[512,1024]{1,0:T(8,128)(2,1)}, bf16[512,1024]{1,0:T(8,128)(2,1)S(1)}, u32[]{:S(2)}, u32[]{:S(2)}) collective-permute-start(bf16[512,1024]{1,0:T(8,128)(2,1)} %bitcast.54), channel_id=1, source_target_pairs={{8,0},{16,8},{24,16},{9,1},{17,9},{25,17},{10,2},{18,10},{26,18},{... | collective-permute-start | bytes 3145736 | tf_op jit(solution)/shard_map/ppermute | solution.py:255
  10.8 39.0 %collective-permute-start = (bf16[512,1024]{1,0:T(8,128)(2,1)}, bf16[512,1024]{1,0:T(8,128)(2,1)S(1)}, u32[]{:S(2)}, u32[]{:S(2)}) collective-permute-start(bf16[512,1024]{1,0:T(8,128)(2,1)} %bitcast.55), channel_id=1, source_target_pairs={{0,8},{8,16},{16,24},{1,9},{9,17},{17,25},{2,10},{10,18},{18,26},{... | collective-permute-start | bytes 3145736 | tf_op jit(solution)/shard_map/ppermute | solution.py:255
  16.4 468.3 %reduce-scatter.13.cloned.1.call-start = ((), (), s32[]{:S(2)}) async-start(), calls=%async_computation.11 | async-start | bytes 7077888
  41.3 9.3 %copy-start.12 = (f32[1,8,128]{2,0,1:T(1,128)}, f32[1,8,128]{2,0,1:T(1,128)S(1)}, u32[]{:S(2)}) copy-start(f32[1,8,128]{2,0,1:T(1,128)S(1)} %get-tuple-element.189) | copy-start | bytes 12292
  43.8 6.0 copy-start.4
  50.6 0.6 copy-start.11
  122.1 175.9 %copy-start.3 = (f32[512,1024]{1,0:T(8,128)}, f32[512,1024]{1,0:T(8,128)S(1)}, u32[]{:S(2)}) copy-start(f32[512,1024]{1,0:T(8,128)S(1)} %get-tuple-element.199) | copy-start | bytes 6291460
  225.1 4.3 copy-start.1
  229.4 46.8 %copy-start.23 = (bf16[1,512,1024]{2,1,0:T(8,128)(2,1)S(1)}, bf16[1,512,1024]{2,1,0:T(8,128)(2,1)}, u32[]{:S(2)}) copy-start(bf16[1,512,1024]{2,1,0:T(8,128)(2,1)} %param.29) | copy-start | bytes 3145732
  276.2 9.7 %copy-start.2 = (f32[512,5632]{1,0:T(8,128)S(1)}, f32[512,5632]{1,0:T(8,128)}, u32[]{:S(2)}) copy-start(f32[512,5632]{1,0:T(8,128)} %copy-done.1) | copy-start | bytes 34603012
  285.9 12.1 %copy-start.5 = (f32[512,1024]{1,0:T(8,128)}, f32[512,1024]{1,0:T(8,128)S(1)}, u32[]{:S(2)}) copy-start(f32[512,1024]{1,0:T(8,128)S(1)} %get-tuple-element.180) | copy-start | bytes 6291460
  311.5 3.5 copy-start.22
  317.3 65.6 %copy-start = (bf16[1536,1024]{1,0:T(8,128)(2,1)S(1)}, bf16[1536,1024]{1,0:T(8,128)(2,1)}, u32[]{:S(2)}) copy-start(bf16[1536,1024]{1,0:T(8,128)(2,1)} %get-tuple-element.177.xn_ref) | copy-start | bytes 9437188
  382.9 5.8 copy-start.21
  388.7 3.8 copy-start.24
  416.0 1.2 copy-start.7
  416.1 105.4 %reduce-scatter.7.cloned.1.call-start = ((), (), s32[]{:S(2)}) async-start(), calls=%async_computation.8 | async-start | bytes 2359296 | tf_op jit(solution)/shard_map/reduce_scatter | solution.py:341
  419.9 167.5 %reduce-scatter.11.cloned.1.call-start = ((), (), s32[]{:S(2)}) async-start(), calls=%async_computation.10 | async-start | bytes 6488064 | tf_op jit(solution)/shard_map/reduce_scatter | solution.py:329
  428.6 278.8 %reduce-scatter.9.cloned.1.call-start = ((), (), s32[]{:S(2)}) async-start(), calls=%async_computation.9 | async-start | bytes 12976128 | tf_op jit(solution)/shard_map/reduce_scatter | solution.py:334
  442.6 357.1 %all-reduce.10.cloned.1.call-start = ((), (), s32[]{:S(2)}) async-start(), calls=%async_computation.12 | async-start | bytes 6422528 | tf_op jit(solution)/shard_map/psum | solution.py:374
  442.9 6.3 copy-start.20
  454.3 3.3 copy-start.9
  457.6 251.2 %copy-start.17 = (f32[4,8,128]{2,1,0:T(8,128)S(1)}, f32[4,8,128]{2,1,0:T(8,128)}, u32[]{:S(2)}) copy-start(f32[4,8,128]{2,1,0:T(8,128)} %get-tuple-element.122) | copy-start | bytes 49156
  457.6 251.4 %copy-start.13 = (f32[1,8,128]{2,0,1:T(1,128)S(1)}, f32[1,8,128]{2,0,1:T(1,128)}, u32[]{:S(2)}) copy-start(f32[1,8,128]{2,0,1:T(1,128)} %copy-done.12) | copy-start | bytes 12292
  457.6 251.4 %collective-permute-start.3 = (bf16[512,1024]{1,0:T(8,128)(2,1)}, bf16[512,1024]{1,0:T(8,128)(2,1)S(1)}, u32[]{:S(2)}, u32[]{:S(2)}) collective-permute-start(bf16[512,1024]{1,0:T(8,128)(2,1)} %get-tuple-element.176), channel_id=1, source_target_pairs={{0,8},{8,16},{16,24},{1,9},{9,17},{17,25},{2,10},{10,18},{18,26},{... | collective-permute-start | bytes 3145736 | tf_op jit(solution)/shard_map/ppermute | solution.py:255
  461.2 247.8 %collective-permute-start.2 = (bf16[512,1024]{1,0:T(8,128)(2,1)}, bf16[512,1024]{1,0:T(8,128)(2,1)}, u32[]{:S(2)}, u32[]{:S(2)}) collective-permute-start(bf16[512,1024]{1,0:T(8,128)(2,1)} %get-tuple-element.175), channel_id=1, source_target_pairs={{8,0},{16,8},{24,16},{9,1},{17,9},{25,17},{10,2},{18,10},{26,18},{... | collective-permute-start | bytes 3145736 | tf_op jit(solution)/shard_map/ppermute | solution.py:255
  709.0 10.0 %copy-start.15 = (f32[4,1,256]{2,1,0:T(1,128)S(1)}, f32[4,1,256]{2,1,0:T(1,128)}, u32[]{:S(2)}) copy-start(f32[4,1,256]{2,1,0:T(1,128)} %get-tuple-element.120) | copy-start | bytes 12292
  709.0 10.0 %copy-start.16 = (f32[4,1,256]{2,1,0:T(1,128)S(1)}, f32[4,1,256]{2,1,0:T(1,128)}, u32[]{:S(2)}) copy-start(f32[4,1,256]{2,1,0:T(1,128)} %get-tuple-element.121) | copy-start | bytes 12292
  799.6 4.5 copy-start.6
  802.3 3.7 copy-start.8
Sparse Core Ops, SparseCore 0:
  9.7 67.6 all-gather.4
  79.0 27.6 all-gather.6
  108.4 107.5 all-gather.8
  217.5 58.7 all-gather.10
  416.2 68.4 reduce-scatter.12
  487.4 33.9 reduce-scatter.6
  523.7 63.6 reduce-scatter.10
  589.7 117.6 reduce-scatter.8
  711.4 88.1 all-reduce.9

commit v2 on v1

--- a/solution.py
+++ b/solution.py
@@ -2,6 +2,7 @@
 
 import jax
 import jax.numpy as jnp
+import numpy as np
 from jax import lax
 from jax.experimental import pallas as pl
 from jax.experimental.pallas import tpu as pltpu
@@ -51,21 +52,52 @@
     n=u*c*gain
     return n*cosine+dot_nn(halves(n),swap_mat)*sine, c
 
-def fwd_kernel(xn_ref,wq_ref,wk_ref,wv_ref,gq_ref,gk_ref,cos_ref,sin_ref,qb_ref,kb_ref,sv_ref,mean_ref,swap_ref,
-               q_ref,k_ref,v_ref,attn_ref,lse_ref,cq_ref,ck_ref):
+QUADS=4
+SEND_ORDER=(3,1,2,0)
+def position(slot): return jnp.where(slot==0,3,jnp.where(slot==3,0,slot))
+
+def piece_copies(place_ref,pieces,w_ref,sem):
+    me,core=place_ref[0],place_ref[1]
+    half=w_ref.shape[1]//2
+    copies=[[pltpu.make_async_copy(pieces[0],w_ref.at[me],sem.at[0])]]
+    for slot in range(1,QUADS):
+        copies.append([pltpu.make_async_copy(pieces[2*slot-1+side],
+            w_ref.at[me^slot,pl.ds(pl.multiple_of((core if side==0 else 1-core)*half,half),half),:],sem.at[2*slot-1+side]) for side in range(2)])
+    return copies
+
+def await_quarter(place_ref,pieces,w_ref,sem):
+    step=pl.program_id(0)
+    copies=piece_copies(place_ref,pieces,w_ref,sem)
+    @pl.when(step==0)
+    def _():
+        for group in copies:
+            for copy in group: copy.start()
+    slot=step^place_ref[0]
+    for i,group in enumerate(copies):
+        @pl.when(slot==i)
+        def _(group=group):
+            for copy in group: copy.wait()
+
+def fwd_kernel(place_ref,xn_ref,p0,p1,p2,p3,p4,p5,p6,gq_ref,gk_ref,cos_ref,sin_ref,qb_ref,kb_ref,sv_ref,mean_ref,swap_ref,
+               q_ref,k_ref,v_ref,attn_ref,lse_ref,cq_ref,ck_ref,wq_out,wkv_out,wattn_out,w_ref,sem):
     rows=qb_ref.shape[0]; ext=kb_ref.shape[0]
+    await_quarter(place_ref,(p0,p1,p2,p3,p4,p5,p6),w_ref,sem)
+    quad=pl.program_id(0)
+    wq_out[...]=w_ref[quad,:,0:256]
+    wkv_out[...]=w_ref[quad,:,256:768]
+    wattn_out[...]=w_ref[quad,:,768:1024]
     tiles=2*HALF//TILE+1
     mean_mat=mean_ref[...]; swap_mat=swap_ref[...]
     first=(lane_of((1,LANES))<HEAD)
-    kf=dot_nn(xn_ref[...],wk_ref[...])
+    kf=dot_nn(xn_ref[...],w_ref[quad,:,256:512])
     for pair in range(2):
         col=slice(pair*LANES,(pair+1)*LANES)
         rot,c=prep(kf[:,col],gk_ref[:,col],cos_ref[...],sin_ref[...],mean_mat,swap_mat)
         k_ref[:,col]=rot.astype(BF)
         if pair==0: ck_ref[...]=c
         else: ck_ref[...]=jnp.where(lane_of((1,LANES))%HEAD==pair,c,ck_ref[...])
-    v_ref[...]=dot_nn(xn_ref[...],wv_ref[...]).astype(BF)
-    qf=dot_nn(xn_ref[HALF:HALF+rows,:],wq_ref[...])
+    v_ref[...]=dot_nn(xn_ref[...],w_ref[quad,:,512:768]).astype(BF)
+    qf=dot_nn(xn_ref[HALF:HALF+rows,:],w_ref[quad,:,0:256])
     for pair in range(2):
         col=slice(pair*LANES,(pair+1)*LANES)
         rot,c=prep(qf[:,col],gq_ref[:,col],cos_ref[HALF:HALF+rows,:],sin_ref[HALF:HALF+rows,:],mean_mat,swap_mat)
@@ -108,9 +140,9 @@
     n=(x*cosine-swapped*sine)/gain
     return c*(gain*e-n*m), jnp.sum(e*n,axis=0,keepdims=True)
 
-def bwd_kernel(q_ref,k_ref,v_ref,do_ref,attn_ref,lse_ref,cq_ref,ck_ref,gq_ref,gk_ref,cos_ref,sin_ref,qb_ref,kb_ref,sv_ref,
+def bwd_kernel(place_ref,q_ref,k_ref,v_ref,do_ref,attn_ref,lse_ref,cq_ref,ck_ref,gq_ref,gk_ref,cos_ref,sin_ref,qb_ref,kb_ref,sv_ref,
                mean_ref,swap_ref,cross_ref,spread_ref,
-               dq_ref,dk_ref,dv_ref,dgq_ref,dgk_ref,bias_ref,dk_acc,dv_acc,ke_ref,ve_ref):
+               dq_ref,dkv_ref,dgq_ref,dgk_ref,bias_ref,dk_acc,dv_acc,ke_ref,ve_ref):
     rows=qb_ref.shape[0]; ext=kb_ref.shape[0]
     tiles=2*HALF//TILE+1
     mean_mat=mean_ref[...]; swap_mat=swap_ref[...]
@@ -167,9 +199,9 @@
         dq_ref[:,col]=du.astype(BF)
         dgq_ref[:,col]=dg
         du,dg=prep_back(k_ref[:,col],dk_acc[...],dot_nn(halves(ck_ref[...]),spread),gk_ref[:,col],cos_ref[...],sin_ref[...],mean_mat,swap_mat)
-        dk_ref[:,col]=du.astype(BF)
+        dkv_ref[:,col]=du.astype(BF)
         dgk_ref[:,col]=dg
-        dv_ref[:,col]=dv_acc[...].astype(BF)
+        dkv_ref[:,pl.ds(pl.multiple_of(256+pair*LANES,LANES),LANES)]=dv_acc[...].astype(BF)
         return 0
     lax.fori_loop(0,2,one_pair,0)
 
@@ -184,41 +216,78 @@
 
 def full(*shape):
     n=len(shape)
-    return pl.BlockSpec(shape,lambda j:(0,)*n)
-def colb(rows,width,off=0): return pl.BlockSpec((rows,width),lambda j:(0,j+off))
-def lead(*shape): return pl.BlockSpec((None,)+shape,lambda j:(j,)+(0,)*len(shape))
-
-def attention_forward(xn,w_qkv,gq,gk,cos,sin,qb,kb,sv,mats,groups=4):
+    return pl.BlockSpec(shape,lambda j,s:(0,)*n)
+def colb(rows,width): return pl.BlockSpec((rows,width),lambda j,s:(0,j))
+def lead(*shape): return pl.BlockSpec((None,)+shape,lambda j,s:(j,)+(0,)*len(shape))
+ANYWHERE=pl.BlockSpec(memory_space=pl.ANY)
+
+def attention_forward(place,xn,pieces,gq,gk,cos,sin,qb,kb,sv,mats):
     rows,ext=qb.shape[0],kb.shape[0]
     mean_mat,swap_mat,_,_=mats
-    n=groups*256
+    n=QUADS*256
+    at=lambda j,s:(0,position(j^s[0]))
     return pl.pallas_call(
-        fwd_kernel,grid=(groups,),
-        in_specs=[full(ext,D),colb(D,256),colb(D,256,groups),colb(D,256,2*groups),lead(1,256),lead(1,256),full(ext,LANES),full(ext,LANES),
-                  full(rows,LANES),full(ext,LANES),lead(8,LANES),full(2*LANES,LANES),full(2*LANES,LANES)],
-        out_specs=[colb(rows,256),colb(ext,256),colb(ext,256),colb(rows,256),colb(rows,256),lead(rows,LANES),lead(ext,LANES)],
+        fwd_kernel,
+        grid_spec=pltpu.PrefetchScalarGridSpec(
+            num_scalar_prefetch=1,grid=(QUADS,),
+            in_specs=[full(ext,D)]+[ANYWHERE]*7+[lead(1,256),lead(1,256),full(ext,LANES),full(ext,LANES),
+                      full(rows,LANES),full(ext,LANES),lead(8,LANES),full(2*LANES,LANES),full(2*LANES,LANES)],
+            out_specs=[colb(rows,256),colb(ext,256),colb(ext,256),colb(rows,256),colb(rows,256),lead(rows,LANES),lead(ext,LANES),
+                       pl.BlockSpec((D,256),at),pl.BlockSpec((D,512),at),colb(D,256)],
+            scratch_shapes=[pltpu.VMEM((QUADS,D,1024),BF),pltpu.SemaphoreType.DMA((7,))]),
         out_shape=[jax.ShapeDtypeStruct((rows,n),BF),jax.ShapeDtypeStruct((ext,n),BF),jax.ShapeDtypeStruct((ext,n),BF),
                    jax.ShapeDtypeStruct((rows,n),BF),jax.ShapeDtypeStruct((rows,n),F32),
-                   jax.ShapeDtypeStruct((groups,rows,LANES),F32),jax.ShapeDtypeStruct((groups,ext,LANES),F32)],
+                   jax.ShapeDtypeStruct((QUADS,rows,LANES),F32),jax.ShapeDtypeStruct((QUADS,ext,LANES),F32),
+                   jax.ShapeDtypeStruct((D,n),BF),jax.ShapeDtypeStruct((D,2*n),BF),jax.ShapeDtypeStruct((D,n),BF)],
         compiler_params=pltpu.CompilerParams(vmem_limit_bytes=56*2**20),
+        cost_estimate=pl.CostEstimate(flops=45 * 10**9, bytes_accessed=40 * 10**6, transcendentals=0),
         name="attention_forward",
-    )(xn,w_qkv,w_qkv,w_qkv,gq,gk,cos,sin,qb,kb,sv,mean_mat,swap_mat)
-
-def attention_backward(q,k,v,do,attn,lse,cq,ck,gq,gk,cos,sin,qb,kb,sv,mats,groups=4):
+    )(place,xn,*pieces,gq,gk,cos,sin,qb,kb,sv,mean_mat,swap_mat)
+
+def ffn_up_kernel(place_ref,x_ref,p0,p1,p2,p3,p4,p5,p6,out_ref,w_out,w_ref,sem):
+    await_quarter(place_ref,(p0,p1,p2,p3,p4,p5,p6),w_ref,sem)
+    step=pl.program_id(0)
+    w_out[...]=w_ref[step]
+    width=out_ref.shape[1]
+    for begin in range(0,width,256):
+        cols=slice(begin,min(begin+256,width))
+        out_ref[:,cols]=dot_nn(x_ref[...],w_ref[step,:,cols])
+
+def ffn_up(place,x,pieces):
+    rows=x.shape[0]; width=pieces[0].shape[1]
+    return pl.pallas_call(
+        ffn_up_kernel,
+        grid_spec=pltpu.PrefetchScalarGridSpec(
+            num_scalar_prefetch=1,grid=(QUADS,),
+            in_specs=[full(rows,D)]+[ANYWHERE]*7,
+            out_specs=[colb(rows,width),colb(D,width)],
+            scratch_shapes=[pltpu.VMEM((QUADS,D,width),BF),pltpu.SemaphoreType.DMA((7,))]),
+        out_shape=[jax.ShapeDtypeStruct((rows,QUADS*width),F32),jax.ShapeDtypeStruct((D,QUADS*width),BF)],
+        compiler_params=pltpu.CompilerParams(vmem_limit_bytes=56*2**20),
+        cost_estimate=pl.CostEstimate(flops=10 * 10**9, bytes_accessed=30 * 10**6, transcendentals=0),
+        name="ffn_up",
+    )(place,x,*pieces)
+
+def attention_backward(place,call,q,k,v,do,attn,lse,cq,ck,gq,gk,cos,sin,qb,kb,sv,mats):
     rows,ext=qb.shape[0],kb.shape[0]
-    n=groups*256
+    def quad(j,s): return s[0]^jnp.where(j==0,SEND_ORDER[2*call],SEND_ORDER[2*call+1])
+    def col(rows,width): return pl.BlockSpec((rows,width),lambda j,s:(0,quad(j,s)))
+    def led(*shape): return pl.BlockSpec((None,)+shape,lambda j,s:(quad(j,s),)+(0,)*len(shape))
     return pl.pallas_call(
-        bwd_kernel,grid=(groups,),
-        in_specs=[colb(rows,256),colb(ext,256),colb(ext,256),colb(rows,256),colb(rows,256),colb(rows,256),lead(rows,LANES),lead(ext,LANES),
-                  lead(1,256),lead(1,256),full(ext,LANES),full(ext,LANES),full(rows,LANES),full(ext,LANES),lead(8,LANES),
-                  full(2*LANES,LANES),full(2*LANES,LANES),full(2*LANES,LANES),full(2,2*LANES,LANES)],
-        out_specs=[colb(rows,256),colb(ext,256),colb(ext,256),lead(1,256),lead(1,256),lead(8,LANES)],
-        out_shape=[jax.ShapeDtypeStruct((rows,n),BF),jax.ShapeDtypeStruct((ext,n),BF),jax.ShapeDtypeStruct((ext,n),BF),
-                   jax.ShapeDtypeStruct((groups,1,256),F32),jax.ShapeDtypeStruct((groups,1,256),F32),jax.ShapeDtypeStruct((groups,8,LANES),F32)],
-        scratch_shapes=[pltpu.VMEM((ext,LANES),F32),pltpu.VMEM((ext,LANES),F32),pltpu.VMEM((ext,LANES),BF),pltpu.VMEM((ext,LANES),BF)],
+        bwd_kernel,
+        grid_spec=pltpu.PrefetchScalarGridSpec(
+            num_scalar_prefetch=1,grid=(2,),
+            in_specs=[col(rows,256),col(ext,256),col(ext,256),col(rows,256),col(rows,256),col(rows,256),led(rows,LANES),led(ext,LANES),
+                      led(1,256),led(1,256),full(ext,LANES),full(ext,LANES),full(rows,LANES),full(ext,LANES),led(8,LANES),
+                      full(2*LANES,LANES),full(2*LANES,LANES),full(2*LANES,LANES),full(2,2*LANES,LANES)],
+            out_specs=[colb(rows,256),colb(ext,512),led(1,256),led(1,256),led(8,LANES)],
+            scratch_shapes=[pltpu.VMEM((ext,LANES),F32),pltpu.VMEM((ext,LANES),F32),pltpu.VMEM((ext,LANES),BF),pltpu.VMEM((ext,LANES),BF)]),
+        out_shape=[jax.ShapeDtypeStruct((rows,512),BF),jax.ShapeDtypeStruct((ext,1024),BF),
+                   jax.ShapeDtypeStruct((QUADS,1,256),F32),jax.ShapeDtypeStruct((QUADS,1,256),F32),jax.ShapeDtypeStruct((QUADS,8,LANES),F32)],
         compiler_params=pltpu.CompilerParams(vmem_limit_bytes=56*2**20),
+        cost_estimate=pl.CostEstimate(flops=38 * 10**9, bytes_accessed=20 * 10**6, transcendentals=0),
         name="attention_backward",
-    )(q,k,v,do,attn,lse,cq,ck,gq,gk,cos,sin,qb,kb,sv,*mats)
+    )(place,q,k,v,do,attn,lse,cq,ck,gq,gk,cos,sin,qb,kb,sv,*mats)
 
 def features(query_doc,query_var,key_doc,key_var,key_obs,key_inside):
     lane=jnp.arange(HEAD)[None,:]
@@ -250,9 +319,87 @@
     return jnp.concatenate([c,c,c,c],axis=1),jnp.concatenate([-s,s,-s,s],axis=1)
 
 
+DIGITS = 34
+LOWEST = -7
+
+
+def tied(*values):
+    return lax.optimization_barrier(values)
+
+
+def permuted(shard, axis, flip):
+    return lax.ppermute(shard, axis, [(i, i ^ flip) for i in range(lax.axis_size(axis))])
+
+
 def shifted(shard, by):
     size = lax.axis_size("ctx")
     return lax.ppermute(shard, "ctx", [(i, i + by) for i in range(size) if 0 <= i + by < size])
+
+
+def neighbours(shard):
+    if lax.axis_size("ctx") != 4:
+        return shifted(shard, 1), shifted(shard, -1)
+    odd = lax.axis_index("ctx") % 2 == 1
+    near = permuted(shard, "ctx", 1)
+    far = lax.ppermute(near, "ctx", [(0, 2), (3, 1)])
+    return jnp.where(odd, near, far), jnp.where(odd, far, near)
+
+
+def returned(before, after):
+    if lax.axis_size("ctx") != 4:
+        return shifted(before, -1).astype(F32) + shifted(after, 1).astype(F32)
+    odd = lax.axis_index("ctx") % 2 == 1
+    far = lax.ppermute(jnp.where(odd, after, before), "ctx", [(1, 3), (2, 0)])
+    near = jnp.where(odd, before, after).astype(F32) + far.astype(F32)
+    return permuted(near.astype(BF), "ctx", 1).astype(F32)
+
+
+def ctx_spread(part):
+    size = lax.axis_size("ctx")
+    return lax.all_to_all(jnp.broadcast_to(part[None], (size,) + part.shape), "ctx", 0, 0)
+
+
+def halves_of(whole, core):
+    half = whole.shape[0] // 2
+    return lax.dynamic_slice_in_dim(whole, core * half, half, 0)
+
+
+def corner_of(near, up):
+    part = near.shape[0] // 2
+    return jnp.concatenate([permuted(near[:part], "ctx", 2), permuted(up[part:], "ctx", 1)], axis=0)
+
+
+def with_partner(piece):
+    return piece, permuted(piece, "fsdp", 1)
+
+
+def sides(left, core):
+    count = lax.axis_size("fsdp")
+    width = left.shape[1] // count
+    blocks = [left[:, i * width : (i + 1) * width] for i in range(count)]
+    even, odd = jnp.concatenate(blocks[0::2], axis=1), jnp.concatenate(blocks[1::2], axis=1)
+    return jnp.where(core == 0, even, odd), jnp.where(core == 0, odd, even)
+
+
+def added(*parts):
+    return sum(part.astype(F32) for part in parts).astype(BF)
+
+
+def joined(first, second):
+    return jnp.concatenate([first, second], axis=0)
+
+
+def core_scatter(total):
+    size = lax.axis_size("fsdp")
+    same_core = [[i for i in range(size) if i % 2 == core] for core in range(2)]
+    return lax.psum_scatter(total, "fsdp", scatter_dimension=0, axis_index_groups=same_core, tiled=True)
+
+
+def ctx_sum(part):
+    size = lax.axis_size("ctx")
+    parts = lax.all_to_all(part.reshape(size, part.shape[0] // size, part.shape[1]), "ctx", 0, 0)
+    total = jnp.sum(parts.astype(F32), axis=0).astype(BF)
+    return ctx_spread(total).reshape(part.shape)
 
 
 def document_ids(doc_lengths, positions):
@@ -268,6 +415,15 @@
     gate_part = gate_up[:, :FF]
     up_part = gate_up[:, FF:]
     return gate_part / (1.0 + jnp.exp(-gate_part)) * up_part
+
+
+def digits_of(value):
+    scaled = value * jnp.asarray(8.0 ** -(LOWEST + np.arange(DIGITS)), F32)
+    return jnp.floor(scaled) - 8.0 * jnp.floor(scaled / 8.0)
+
+
+def value_of(digits):
+    return jnp.sum(digits * jnp.asarray(8.0 ** (LOWEST + np.arange(DIGITS)), F32))
 
 
 def per_device(tokens, teacher, cotangent, lengths, variate, observed, norm_gains, var_bias, qkv_weight, out_weight, ffn_in, ffn_out):
@@ -279,22 +435,44 @@
     seq_len = observed.shape[1]
     gains_n = norm_gains.shape[1]
     bias_n = var_bias.shape[0]
-
+    shard_id = lax.axis_index("fsdp")
+    quartered = n_context == QUADS
+    me = lax.axis_index("ctx") if quartered else jnp.int32(0)
+    core = shard_id % 2 if quartered else jnp.int32(0)
+    place = jnp.stack([me, core]).astype(jnp.int32)
+
+    if quartered:
+        quarter = lambda a, width, begin=0: lax.dynamic_slice_in_dim(a, begin + me * width, width, 1)
+        shard = jnp.concatenate([quarter(qkv_weight, 256, i * D) for i in range(3)] + [quarter(out_weight, 256)], axis=1)
+        whole = lax.all_gather(shard, "fsdp", axis=0, tiled=True)
+        whole_in = lax.all_gather(quarter(ffn_in, FF // 2), "fsdp", axis=0, tiled=True)
+    else:
+        w_attention = jnp.concatenate([qkv_weight, out_weight], axis=1)
+        w_attention = lax.all_gather(w_attention, "fsdp", axis=0, tiled=True)
+        w_attention = jnp.swapaxes(w_attention.reshape(D, 4, QUADS, 256), 1, 2).reshape(D, QUADS, 1024)
+        w_in = lax.all_gather(ffn_in, "fsdp", axis=0, tiled=True).reshape(D, QUADS, FF // 2)
+    w_lower = lax.all_gather(ffn_out, "fsdp", axis=0, tiled=True)
+    before, behind = neighbours(tokens[0])
     own_count = jnp.sum(observed[0])
     small = jnp.zeros((16, gains_n), BF)
     small = small.at[:4].set(norm_gains).at[4, :bias_n].set(var_bias)
     small = small.at[5, 0].set((own_count // 256).astype(BF)).at[5, 1].set((own_count % 256).astype(BF))
-    before, after = shifted(tokens[0], 1), shifted(tokens[0], -1)
-    w_qkv = lax.all_gather(qkv_weight, "fsdp", axis=0, tiled=True)
-    small = lax.all_gather(small, "fsdp", axis=0)
-    w_attn = lax.all_gather(out_weight, "fsdp", axis=0, tiled=True)
-    w_upper = lax.all_gather(ffn_in, "fsdp", axis=0, tiled=True)
-    w_lower = lax.all_gather(ffn_out, "fsdp", axis=0, tiled=True)
+    small = lax.all_to_all(jnp.broadcast_to(small[None], (n_shards,) + small.shape), "fsdp", 0, 0)
+    if quartered:
+        mine = halves_of(whole, core)
+        near, up = permuted(mine, "ctx", 1), permuted(mine, "ctx", 2)
+        corner = corner_of(near, up)
+        whole_in, corner = tied(whole_in, corner)
+        pieces = (whole,) + with_partner(near) + with_partner(up) + with_partner(corner)
+        mine_in = halves_of(whole_in, core)
+        near_in, up_in = permuted(mine_in, "ctx", 1), permuted(mine_in, "ctx", 2)
+    else:
+        split = lambda w: (w[:, 0],) + tuple(w[i * D // 2 : (i + 1) * D // 2, j] for j in range(1, QUADS) for i in range(2))
+        pieces, pieces_in = split(w_attention), split(w_in)
 
     gains = jnp.moveaxis(small[:, :4], 0, 1).reshape(4, D).astype(F32)
     bias = small[:, 4, :bias_n].reshape(2 * HEADS).astype(F32)
     valid_total = jnp.sum(small[:, 5, 0].astype(F32) * 256.0 + small[:, 5, 1].astype(F32))
-
     key_pos = start - HALF + jnp.arange(ext, dtype=jnp.int32)
     inside = (key_pos >= 0) & (key_pos < seq_len)
     key_doc = document_ids(lengths[0], key_pos)
@@ -307,15 +485,21 @@
     mats = blockdiag()
     gain_q, gain_k = gains[2].reshape(-1, 1, 256), gains[3].reshape(-1, 1, 256)
 
-    inputs = jnp.concatenate([before, tokens[0], after], axis=0).astype(F32)
+    inputs = jnp.concatenate([before, tokens[0], behind], axis=0).astype(F32)
     inv = lax.rsqrt(jnp.mean(inputs * inputs, axis=-1, keepdims=True) + EPSILON)
     normed = (inputs * inv * gains[0]).astype(BF)
 
-    q, k, v, attn, lse, c_q, c_k = attention_forward(normed, w_qkv, gain_q, gain_k, cosine, sine, query_feat, key_feat, scales, mats)
+    q, k, v, attn, lse, c_q, c_k, w_q, w_kv, w_attn = attention_forward(
+        place, normed, pieces, gain_q, gain_k, cosine, sine, query_feat, key_feat, scales, mats
+    )
+    if quartered:
+        near_in, up_in, attn = tied(near_in, up_in, attn)
+        corner_in = corner_of(near_in, up_in)
+        pieces_in = (whole_in,) + with_partner(near_in) + with_partner(up_in) + with_partner(corner_in)
     mixed = tokens[0].astype(F32) + jnp.dot(attn, w_attn, preferred_element_type=F32)
-    normed_two_f, norm_two_pull = jax.vjp(rms_scale, mixed, gains[1])
+    normed_two_f, norm_two_pull = jax.vjp(lambda m: rms_scale(m, gains[1]), mixed)
     normed_two = normed_two_f.astype(BF)
-    gate_up = jnp.dot(normed_two, w_upper, preferred_element_type=F32)
+    gate_up, w_upper = ffn_up(place, normed_two, pieces_in)
     hidden_f, glu_pull = jax.vjp(gated_unit, gate_up)
     hidden = hidden_f.astype(BF)
     final = mixed + jnp.dot(hidden, w_lower, preferred_element_type=F32)
@@ -325,63 +509,128 @@
     all_tokens = rows * n_context * n_shards
     d_final = cotangent[0].astype(F32) + all_tokens * valid_col * distance / valid_total
     d_final_low = d_final.astype(BF)
-    grad_lower = dot_tn(hidden, d_final_low)
-    ffn_out_part = lax.psum_scatter(grad_lower.astype(BF), "fsdp", scatter_dimension=0, tiled=True)
+
+    low_grad = dot_tn(hidden, d_final_low).astype(BF)
+    d_final_low, low_grad = tied(d_final_low, low_grad)
+    low_part = lax.psum_scatter(low_grad, "fsdp", scatter_dimension=0, tiled=True)
     d_hidden = dot_nt(d_final_low, w_lower)
     (d_gate_up,) = glu_pull(d_hidden)
     d_gate_low = d_gate_up.astype(BF)
-    grad_upper = dot_tn(normed_two, d_gate_low)
-    ffn_in_part = lax.psum_scatter(grad_upper.astype(BF), "fsdp", scatter_dimension=0, tiled=True)
-    d_normed_two = dot_nt(d_gate_low, w_upper)
-    d_mixed_part, grad_norm_two = norm_two_pull(d_normed_two)
+    if quartered:
+        own_two, other_two = sides(normed_two, core)
+        theirs = dot_tn(other_two, d_gate_low).astype(BF)
+        d_gate_low, theirs = tied(d_gate_low, theirs)
+        swapped = permuted(theirs, "fsdp", 1)
+        d_normed_two = dot_nt(d_gate_low, w_upper)
+        d_gate_low, d_normed_two = tied(d_gate_low, d_normed_two)
+        in_chip = (dot_tn(own_two, d_gate_low) + swapped.astype(F32)).astype(BF)
+        part = lambda j: lax.dynamic_slice_in_dim(in_chip, (me ^ j) * (FF // 2), FF // 2, 1)
+        cut = in_chip.shape[0] // 2
+        last = part(3)
+    else:
+        d_normed_two = dot_nt(d_gate_low, w_upper)
+        in_part = lax.psum_scatter(dot_tn(normed_two, d_gate_low).astype(BF), "fsdp", scatter_dimension=0, tiled=True)
+        in_grad = lax.psum(in_part, "ctx").astype(F32)
+        last = in_part
+    (d_mixed_part,) = norm_two_pull(d_normed_two)
     d_mixed = d_final + d_mixed_part
     d_mixed_low = d_mixed.astype(BF)
+    out_grad = dot_tn(attn, d_mixed_low).astype(BF)
     d_attn = dot_nt(d_mixed_low, w_attn).astype(BF)
-    grad_attn = dot_tn(attn, d_mixed_low)
-    out_part = lax.psum_scatter(grad_attn.astype(BF), "fsdp", scatter_dimension=0, tiled=True)
-
-    d_q, d_k, d_v, d_gain_q, d_gain_k, d_bias = attention_backward(
-        q, k, v, d_attn, attn, lse, c_q, c_k, gain_q, gain_k, cosine, sine, query_feat, key_feat, scales, mats
-    )
-    grad_qkv = jnp.concatenate(
-        [dot_tn(normed[own], d_q).astype(BF), dot_tn(normed, d_k).astype(BF), dot_tn(normed, d_v).astype(BF)], axis=1
-    )
-    qkv_part = lax.psum_scatter(grad_qkv, "fsdp", scatter_dimension=0, tiled=True)
-    d_ext = dot_nt(d_k, w_qkv[:, D : 2 * D]) + dot_nt(d_v, w_qkv[:, 2 * D :])
-    from_next = shifted(d_ext[:HALF].astype(BF), -1)
-    from_prev = shifted(d_ext[HALF + rows :].astype(BF), 1)
-    d_own = d_ext[own] + dot_nt(d_q, w_qkv[:, :D])
-    unit = inputs * inv
-    grad_norm_one = (
-        jnp.sum(d_own * unit[own], axis=0)
-        + jnp.sum(d_ext[:HALF] * unit[:HALF], axis=0)
-        + jnp.sum(d_ext[HALF + rows :] * unit[HALF + rows :], axis=0)
-    )
-    d_own = d_own.at[rows - HALF :].add(from_next.astype(F32)).at[:HALF].add(from_prev.astype(F32))
-    scaled = d_own * gains[0]
-    input_grad = d_mixed + inv[own] * (scaled - unit[own] * jnp.mean(unit[own] * scaled, axis=-1, keepdims=True))
-
-    same = jnp.sum(d_bias[:, :4], axis=-1).reshape(HEADS)
-    sums = jnp.concatenate(
-        [grad_norm_one, grad_norm_two, d_gain_q.reshape(D), d_gain_k.reshape(D), same, jnp.full((LANES,), squared)]
-    )
-    sums = lax.psum(jnp.pad(sums, (0, -sums.shape[0] % (8 * LANES))).reshape(-1, LANES), ("ctx", "fsdp")).reshape(-1)
-    loss = sums[4 * D + HEADS] / (valid_total * D)
-    me = lax.axis_index("fsdp")
-    gains_grad = lax.dynamic_slice_in_dim(sums[: 4 * D].reshape(4, D), me * gains_n, gains_n, 1)
-    bias_sum = sums[4 * D : 4 * D + HEADS]
-    var_bias_grad = lax.dynamic_slice_in_dim(jnp.concatenate([bias_sum, -bias_sum]), me * bias_n, bias_n, 0)
-    qkv_grad, out_grad, in_grad, low_grad = lax.psum((qkv_part, out_part, ffn_in_part, ffn_out_part), "ctx")
+
+    d_attn, last, out_grad = tied(d_attn, last, out_grad)
+    out_part = lax.psum_scatter(out_grad, "fsdp", scatter_dimension=0, tiled=True)
+    if quartered:
+        last_near, last_up = permuted(last[:cut], "ctx", 1), permuted(last[cut:], "ctx", 2)
+    saved = (q, k, v, d_attn, attn, lse, c_q, c_k, gain_q, gain_k, cosine, sine, query_feat, key_feat, scales, mats)
+    d_q1, d_kv1, gain_q1, gain_k1, bias_1 = attention_backward(place, 0, *saved)
+    if quartered:
+        own_normed, other_normed = sides(normed, core)
+        theirs = [dot_tn(other_normed[own], d_q1).astype(BF), dot_tn(other_normed, d_kv1).astype(BF)]
+        last_near, last_up, theirs = tied(last_near, last_up, theirs)
+        swapped = [permuted(t, "fsdp", 1) for t in theirs]
+        one, two = part(1), part(2)
+        one, two = joined(one[:cut], added(one[cut:], last_up)), joined(added(two[:cut], last_near), two[cut:])
+        d_q1, d_kv1, one, two = tied(d_q1, d_kv1, one, two)
+        in_near, in_up = permuted(one, "ctx", 1), permuted(two, "ctx", 2)
+        first_q = (dot_tn(own_normed[own], d_q1) + swapped[0].astype(F32)).astype(BF)
+        first_kv = (dot_tn(own_normed, d_kv1) + swapped[1].astype(F32)).astype(BF)
+        quarters = {3: jnp.concatenate([first_q[:, :256], first_kv[:, :512]], axis=1), 1: jnp.concatenate([first_q[:, 256:], first_kv[:, 512:]], axis=1)}
+        d_attn, quarters, low_part = tied(d_attn, quarters, low_part)
+        last_near, last_up = permuted(quarters[3][:cut], "ctx", 1), permuted(quarters[3][cut:], "ctx", 2)
+        saved = saved[:3] + (d_attn,) + saved[4:]
+    d_q2, d_kv2, gain_q2, gain_k2, bias_2 = attention_backward(place, 1, *saved)
+    done_first = ((me ^ jnp.arange(QUADS)) % 2 == 1)[:, None, None]
+    d_gain_q = jnp.where(done_first, gain_q1, gain_q2).reshape(D)
+    d_gain_k = jnp.where(done_first, gain_k1, gain_k2).reshape(D)
+    same = jnp.sum(jnp.where(done_first, bias_1, bias_2)[:, :4], axis=-1).reshape(HEADS)
+    d_bias = jnp.concatenate([same, -same])
+
+    if quartered:
+        extra = jnp.zeros((n_shards, D // n_shards, LANES), F32)
+        extra = extra.at[:, 0, :gains_n].set(d_gain_q.reshape(n_shards, gains_n)).at[:, 1, :gains_n].set(d_gain_k.reshape(n_shards, gains_n))
+        extra = extra.at[:, 2, :bias_n].set(d_bias.reshape(n_shards, bias_n)).at[:, 3, :DIGITS].set(digits_of(squared)[None])
+        extra = extra.reshape(n_shards // 2, 2, D // n_shards, LANES).astype(BF)
+        own_extra = jnp.where(core == 0, extra[:, 0], extra[:, 1]).reshape(-1, LANES)
+        other_extra = jnp.where(core == 0, extra[:, 1], extra[:, 0]).reshape(-1, LANES)
+        theirs = [dot_tn(other_normed[own], d_q2).astype(BF), dot_tn(other_normed, d_kv2).astype(BF), other_extra]
+        theirs, in_near, in_up, out_part = tied(theirs, in_near, in_up, out_part)
+        swapped = [permuted(t, "fsdp", 1) for t in theirs]
+        in_total = added(part(0), in_near, in_up)
+        d_q2, d_kv2, in_total = tied(d_q2, d_kv2, in_total)
+        in_part = core_scatter(in_total)
+        second_q = (dot_tn(own_normed[own], d_q2) + swapped[0].astype(F32)).astype(BF)
+        second_kv = (dot_tn(own_normed, d_kv2) + swapped[1].astype(F32)).astype(BF)
+        quarters[2] = jnp.concatenate([second_q[:, :256], second_kv[:, :512]], axis=1)
+        quarters[0] = jnp.concatenate([second_q[:, 256:], second_kv[:, 512:]], axis=1)
+        one = joined(quarters[1][:cut], added(quarters[1][cut:], last_up))
+        two = joined(added(quarters[2][:cut], last_near), quarters[2][cut:])
+        d_kv2, d_q2, one, two = tied(d_kv2, d_q2, one, two)
+        near, up = permuted(one, "ctx", 1), permuted(two, "ctx", 2)
+    d_ext = dot_nt(d_kv1, w_kv[:, : 2 * 512]) + dot_nt(d_kv2, w_kv[:, 2 * 512 :])
+    from_others = returned(d_ext[:HALF].astype(BF), d_ext[HALF + rows :].astype(BF))
+    d_own = d_ext[own] + dot_nt(d_q1, w_q[:, : 2 * 256]) + dot_nt(d_q2, w_q[:, 2 * 256 :])
+    if quartered:
+        qkv_total = jnp.concatenate([added(quarters[0], near, up), added(own_extra, swapped[2])], axis=1)
+        qkv_part = core_scatter(qkv_total)
+        spread = ctx_spread(qkv_part)
+        qkv_grad = jnp.transpose(spread[:, :, : 3 * 256].reshape(QUADS, -1, 3, 256), (1, 2, 0, 3)).reshape(-1, 3 * D).astype(F32)
+        sums = jnp.sum(spread[:, :, 3 * 256 :].astype(F32), axis=0)
+        squared = value_of(sums[3, :DIGITS])
+        gain_rows, var_bias_grad = sums[:2, :gains_n], sums[2, :bias_n]
+        in_grad = jnp.swapaxes(ctx_spread(in_part), 0, 1).reshape(-1, 2 * FF).astype(F32)
+        other_grads = ctx_sum(joined(out_part, low_part)).astype(F32)
+    else:
+        order = [SEND_ORDER.index(j) for j in range(QUADS)]
+        natural = lambda first, second, width: jnp.concatenate([first, second], axis=1).reshape(-1, QUADS, width)[:, jnp.array(order)]
+        grad_q = dot_tn(normed[own], natural(d_q1, d_q2, 256).reshape(rows, D))
+        grad_kv = dot_tn(normed, jnp.swapaxes(natural(d_kv1, d_kv2, 512).reshape(ext, QUADS, 2, 256), 1, 2).reshape(ext, 2 * D))
+        grad_qkv = jnp.concatenate([grad_q, grad_kv], axis=1).astype(BF)
+        qkv_grad = lax.psum(lax.psum_scatter(grad_qkv, "fsdp", scatter_dimension=0, tiled=True), "ctx").astype(F32)
+        other_grads = lax.psum(joined(out_part, low_part), "ctx").astype(F32)
+        sums = jnp.concatenate([d_gain_q, d_gain_k, d_bias, squared[None]])
+        sums = lax.psum(jnp.pad(sums, (0, -sums.shape[0] % (8 * LANES))).reshape(-1, LANES), ("ctx", "fsdp")).reshape(-1)
+        gain_rows = lax.dynamic_slice_in_dim(sums[: 2 * D].reshape(2, D), shard_id * gains_n, gains_n, 1)
+        var_bias_grad = lax.dynamic_slice_in_dim(sums[2 * D : 2 * D + 2 * HEADS], shard_id * bias_n, bias_n, 0)
+        squared = sums[2 * D + 2 * HEADS]
+    loss = squared / (valid_total * D)
+    own_gains = norm_gains.astype(F32)
+    gain_one = jnp.sum(qkv_weight.astype(F32) * qkv_grad, axis=1) / own_gains[0]
+    gain_two = jnp.sum(ffn_in.astype(F32) * in_grad, axis=1) / own_gains[1]
+    gains_grad = jnp.concatenate([gain_one[None], gain_two[None], gain_rows], axis=0)
+    unit = inputs[own] * inv[own]
+    scaled = (d_own + from_others) * gains[0]
+    input_grad = d_mixed + inv[own] * (scaled - unit * jnp.mean(unit * scaled, axis=-1, keepdims=True))
     return (
         loss,
         final.astype(BF)[None],
         input_grad[None],
         gains_grad,
         var_bias_grad,
-        qkv_grad.astype(F32),
-        out_grad.astype(F32),
-        in_grad.astype(F32),
-        low_grad.astype(F32),
+        qkv_grad,
+        other_grads[: out_part.shape[0]],
+        in_grad,
+        other_grads[out_part.shape[0] :],
     )
 
 

time: 824 us -> 581 us (0.71)
  waiting for transfers between devices: 435 us -> 111 us
  blocking collectives: 53.4 us -> 0 us
  starting transfers between devices: 12.3 us -> 57.9 us
  other arithmetic: 53.5 us -> 91.5 us
  Pallas kernels: 107 us -> 142 us
  local copies, waits for them, and re-layouts: 27.6 us -> 51.3 us
    reduce_scatter x3 -> x4, waiting for transfers between devices: 220 us -> 0.04 us  [the longest x1 0.02 us: per_device(): lax.psum_scatter(low_grad, 'fsdp', scatter_dimension=0, tiled=True)]
    all_gather x3 -> x2, waiting for transfers between devices: 112 us -> 0.02 us  [the longest x1 0.02 us: per_device(): whole = lax.all_gather(shard, 'fsdp', axis=0, tiled=True)]
    ppermute x4 -> x32, waiting for transfers between devices: 0.01 us -> 103 us  [the longest x30 85.5 us: permuted(): lax.ppermute(shard, axis, [(i, i ^ flip) for i in range(lax.axis_size(axi...]
    all_gather x1, waiting for transfers between devices: 43.5 us -> 0.01 us  [per_device(): w_lower = lax.all_gather(ffn_out, 'fsdp', axis=0, tiled=True)]
    psum x1 -> x0, blocking collectives: 38.4 us -> none  [per_device(): lax.psum(jnp.pad(sums, (0, -sums.shape[0] % (8 * LANES))).reshape(-1, LAN...]
    pallas_call x2 -> x4, Pallas kernels: 107 us -> 142 us  [the longest x2 71.4 us: attention_backward(): pl.pallas_call(bwd_kernel, grid_spec=pltpu.PrefetchScalarGridSpec(num_sca...]
    psum x1 -> x0, waiting for transfers between devices: 34.8 us -> none  [per_device(): lax.psum((qkv_part, out_part, ffn_in_part, ffn_out_part), 'ctx')]
    convert_element_type x3 -> x18, other arithmetic: 4.99 us -> 31.7 us  [the longest x6 11.3 us: added(): return sum((part.astype(F32) for part in parts)).astype(BF)]
  transfers between devices with their start and end apart: 13 -> 44, of which waited for: 8 -> 11; matrix products, arithmetic and copies ran while one was open for 12% -> 35% of each run, Pallas kernels for 5% -> 25%
where the time goes in v2:
time: 581 us; the launch traced here: 574 us
  Pallas kernels  142 us (24%)
  waiting for transfers between devices  111 us (19%)
  matrix products  99.1 us (17%)
  other arithmetic  91.5 us (16%)
  starting transfers between devices  57.9 us (10%)
  local copies, waits for them, and re-layouts  51.3 us (9%)
  between operations  20.9 us (4%)
    ppermute x30, waiting for transfers between devices, permuted(): lax.ppermute(shard, axis, [(i, i ^ flip) for i in range(lax.axis_size(axi...  85.5 us
    pallas_call x2, Pallas kernels, attention_backward(): pl.pallas_call(bwd_kernel, grid_spec=pltpu.PrefetchScalarGridSpec(num_sca...  71.4 us
    pallas_call x1, Pallas kernels, attention_forward(): pl.pallas_call(fwd_kernel, grid_spec=pltpu.PrefetchScalarGridSpec(num_sca...  44.2 us
    dot_general x12, matrix products, dot_tn(): lax.dot_general(a, b, (((0,), (0,)), ((), ())), preferred_element_type=F32)  44 us
    dot_general x7, matrix products, dot_nt(): lax.dot_general(a, b, (((1,), (1,)), ((), ())), preferred_element_type=F32)  42.2 us
    ppermute x30, starting transfers between devices, permuted(): lax.ppermute(shard, axis, [(i, i ^ flip) for i in range(lax.axis_size(axi...  27.7 us
    pallas_call x1, Pallas kernels, ffn_up(): pl.pallas_call(ffn_up_kernel, grid_spec=pltpu.PrefetchScalarGridSpec(num_...  26.7 us
    unnamed x113, local copies, waits for them, and re-layouts  19 us
  transfers between devices with their start and end apart: 44, of which 11 were waited for; matrix products, arithmetic and copies ran while one was open for 35% of the time, Pallas kernels for 25%

profile of v2, /device:TPU:0, one launch (start us, length us, event | category | flops | bytes accessed | tf_op | source)
XLA Modules:
  0.0 574.1 jit_solution(15496831365016719060)
XLA Ops:
  15.2 6.3 %all-to-all-start = ((bf16[8,16,128]{2,1,0:T(8,128)(2,1)}), bf16[8,16,128]{2,1,0:T(8,128)(2,1)S(1)}, u32[]{:S(2)}, u32[]{:S(2)}) async-start(bf16[8,16,128]{2,1,0:T(8,128)(2,1)} %broadcast_in_dim.199), calls=%async_computation | async-start | bytes 65536 | tf_op jit(solution)/shard_map/all_to_all | solution.py:460
  26.3 2.8 fusion.43
  35.5 11.7 %collective-permute-done = bf16[512,1024]{1,0:T(8,128)(2,1)S(1)} collective-permute-done((bf16[512,1024]{1,0:T(8,128)(2,1)S(1)}, bf16[512,1024]{1,0:T(8,128)(2,1)S(1)}, u32[]{:S(2)}, u32[]{:S(2)}) %collective-permute-start) | collective-permute-done | bytes 1048608 | tf_op jit(solution)/shard_map/ppermute | solution.py:331
  47.2 4.6 collective-permute-start.1
  56.6 38.7 %collective-permute-done.4.p3 = bf16[512,1024]{1,0:T(8,128)(2,1)} collective-permute-done((bf16[512,1024]{1,0:T(8,128)(2,1)S(1)}, bf16[512,1024]{1,0:T(8,128)(2,1)}, u32[]{:S(2)}, u32[]{:S(2)}) %collective-permute-start.4) | collective-permute-done | bytes 1048608 | tf_op jit(solution)/shard_map/ppermute | solution.py:331
  96.4 2.6 collective-permute-start.7
  103.3 6.6 %collective-permute-done.7 = bf16[256,1024]{1,0:T(8,128)(2,1)S(1)} collective-permute-done((bf16[256,1024]{1,0:T(8,128)(2,1)S(1)}, bf16[256,1024]{1,0:T(8,128)(2,1)S(1)}, u32[]{:S(2)}, u32[]{:S(2)}) %collective-permute-start.7) | collective-permute-done | bytes 524320 | tf_op jit(solution)/shard_map/ppermute | solution.py:331
  109.9 2.6 collective-permute-done.6
  113.6 7.3 %multiply_convert_fusion.xn_ref = bf16[1536,1024]{1,0:T(8,128)(2,1)} fusion(f32[1024]{0:T(1024)S(1)} %bitcast.112, f32[1536]{0:T(1024)S(1)} %add_rsqrt_fusion, bf16[512,1024]{1,0:T(8,128)(2,1)S(1)} %get-tuple-element.303, bf16[512,1024]{1,0:T(8,128)(2,1)S(1)} %bitcast.101, bf16[512,1024]{1,0:T(8,128)(2,1)S(1)} %get-tuple-element.302), kind=kLoop, calls=%fused_computation.3 | loop fusion | flops 14155776 | bytes 6301696 | tf_op jit(solution)/shard_map/convert_element_type | solution.py:490
  123.1 44.2 %attention_forward.1 = (bf16[512,1024]{1,0:T(8,128)(2,1)}, bf16[1536,1024]{1,0:T(8,128)(2,1)}, bf16[1536,1024]{1,0:T(8,128)(2,1)}, bf16[512,1024]{1,0:T(8,128)(2...) custom-call(s32[2]{0:T(128)} %pad_add_fusion.place_ref, ...), custom_call_target="tpu_custom_call" | custom-call | flops 44999999488 | bytes 40000000 | tf_op jit(solution)/shard_map/attention_forward/pallas_call | solution.py:229
  173.7 12.9 %collective-permute-done.13 = bf16[256,1408]{1,0:T(8,128)(2,1)S(1)} collective-permute-done((bf16[256,1408]{1,0:T(8,128)(2,1)}, bf16[256,1408]{1,0:T(8,128)(2,1)S(1)}, u32[]{:S(2)}, u32[]{:S(2)}) %collective-permute-start.13) | collective-permute-done | bytes 720928 | tf_op jit(solution)/shard_map/ppermute | solution.py:331
  191.1 3.3 multiply_reduce_fusion.4
  195.6 26.7 %ffn_up.1 = (f32[512,5632]{1,0:T(8,128)}, bf16[1024,5632]{1,0:T(8,128)(2,1)}) custom-call(s32[2]{0:T(128)} %pad_add_fusion.place_ref, bf16[512,1024]{1,0:T(8,128)(2,1)} %copy-done.11, bf16[1024,1408]{1,0:T(8,128)(2,1)} %all-gather.6.cloned.1.call-done.p0, bf16[512,1408]{1,0:T(8,128)(2,1)} %copy-done.28, bf16[512,1408]{1,0:T(8,128)(2,1)} %collective-permute-done.11.p2, ...), custom_call_target="tpu_custom_call" | custom-call | flops 10000000000 | bytes 30000000 | tf_op jit(solution)/shard_map/ffn_up/pallas_call | solution.py:258
  222.3 6.3 %multiply_convert_fusion.1 = bf16[512,2816]{1,0:T(8,128)(2,1)} fusion(f32[512,5632]{1,0:T(8,128)} %get-tuple-element.176), kind=kLoop, calls=%fused_computation.7 | loop fusion | flops 7208960 | bytes 14417920 | tf_op jit(solution)/shard_map/convert_element_type | solution.py:504
  228.6 9.6 %fusion.64 = (bf16[512,1024]{1,0:T(8,128)(2,1)S(1)}, f32[512,1024]{1,0:T(8,128)}) fusion(f32[]{:T(128)} %add_reduce_fusion, bf16[1,512,1024]{2,1,0:T(8,128)(2,1)} %param.31, f32[512]{0:T(512)S(1)} %get-tuple-element.281, bf16[1,512,1024]{2,1,0:T(8,128)(2,1)} %param.32, f32[512,1024]{1,0:T(8,128)S(1)} %get-tuple-element.350, ...), kind=kOutput, calls=%fused_computation.220 | convolution fusion | flops 2956984320 | bytes 15992836 | tf_op jit(solution)/shard_map/dot_general | solution.py:505
  239.2 5.0 convolution_convert_fusion.1
  244.2 13.0 %fusion.16 = (f32[512,2816]{1,0:T(8,128)}, f32[512,2816]{1,0:T(8,128)}) fusion(f32[512,5632]{1,0:T(8,128)} %get-tuple-element.176, bf16[512,1024]{1,0:T(8,128)(2,1)} %copy-done.50, bf16[2816,1024]{1,0:T(8,128)(2,1)} %all-gather.8.cloned.1.call-done), kind=kOutput, calls=%fused_computation.71 | convolution fusion | flops 2972975104 | bytes 29884416 | tf_op jit(solution)/shard_map/dot_general | solution.py:22
  257.2 7.4 %add_convert_fusion.1 = bf16[512,5632]{1,0:T(8,128)(2,1)} fusion(f32[512,2816]{1,0:T(8,128)} %get-tuple-element.284, f32[512,2816]{1,0:T(8,128)} %get-tuple-element.283), kind=kLoop, calls=%fused_computation.1 | loop fusion | flops 5767168 | bytes 17301504 | tf_op jit(solution)/shard_map/convert_element_type | solution.py:518
  264.6 8.3 %convolution_convert_fusion = bf16[512,5632]{1,0:T(8,128)(2,1)} fusion(bf16[512,5632]{1,0:T(8,128)(2,1)} %add_convert_fusion.1, pred[]{:T(512)S(6)} %eq.178, bf16[512,128]{1,0:T(8,128)(2,1)S(1)} %get-tuple-element.311, bf16[512,128]{1,0:T(8,128)(2,1)S(1)} %get-tuple-element.312, bf16[512,128]{1,0:T(8,128)(2,1)S(1)} %get-tuple-element.313, ...), kind=kOutput, calls=%fused_computation.2 | convolution fusion | flops 2960130048 | bytes 12582913 | tf_op jit(solution)/shard_map/dot_general | solution.py:23
  274.9 2.6 fusion.67
  279.8 9.1 %fusion.80 = f32[512,1024]{1,0:T(8,128)S(1)} fusion(bf16[512,5632]{1,0:T(8,128)(2,1)S(1)} %bitcast.96, bf16[1024,5632]{1,0:T(8,128)(2,1)} %get-tuple-element.179), kind=kOutput, calls=%fused_computation.235 | convolution fusion | flops 5905580032 | bytes 19398656 | tf_op jit(solution)/shard_map/dot_general | solution.py:22
  291.1 3.8 fusion.1
  296.2 2.6 convolution_convert_fusion.2
  298.9 3.9 convolution_convert_fusion.5.do_ref
  302.8 8.0 %add_convert_fusion = bf16[512,5632]{1,0:T(8,128)(2,1)S(1)} fusion(bf16[512,5632]{1,0:T(8,128)(2,1)} %collective-permute-done.16, bf16[512,5632]{1,0:T(8,128)(2,1)} %add_convert_fusion.1, pred[]{:T(512)S(6)} %eq.178, bf16[512,128]{1,0:T(8,128)(2,1)S(1)} %get-tuple-element.311, bf16[512,128]{1,0:T(8,128)(2,1)S(1)} %get-tuple-element.312, ...), kind=kOutput, calls=%fused_computation | convolution fusion | flops 2965897216 | bytes 18350080 | tf_op jit(solution)/shard_map/dot_general | solution.py:23
  313.2 2.4 collective-permute-start.17
  315.7 2.4 collective-permute-start.18
  319.6 35.9 %attention_backward.2 = (bf16[512,512]{1,0:T(8,128)(2,1)}, bf16[1536,1024]{1,0:T(8,128)(2,1)}, f32[4,1,256]{2,1,0:T(1,128)}, f32[4,1,256]{2,1,0:T(1,128)}, f32[4,8,128]{2,1,0:T(8,128)}) custom-call(s32[2]{0:T(128)} %pad_add_fusion.place_ref, bf16[512,1024]{1,0:T(8,128)(2,1)} %get-tuple-element.167.q_ref, bf16[1536,1024]{1,0:T(8,128)(2,1)} %get-tuple-element.168.k_ref, ...), custom_call_target="tpu_custom_call" | custom-call | flops 38000001024 | bytes 20000000 | tf_op jit(solution)/shard_map/attention_backward/pallas_call | solution.py:276
  357.0 3.7 convolution_convert_fusion.4
  369.1 35.6 %attention_backward.3 = (bf16[512,512]{1,0:T(8,128)(2,1)}, bf16[1536,1024]{1,0:T(8,128)(2,1)}, f32[4,1,256]{2,1,0:T(1,128)}, f32[4,1,256]{2,1,0:T(1,128)}, f32[4,8,128]{2,1,0:T(8,128)}) custom-call(s32[2]{0:T(128)} %pad_add_fusion.place_ref, bf16[512,1024]{1,0:T(8,128)(2,1)} %get-tuple-element.167.q_ref, bf16[1536,1024]{1,0:T(8,128)(2,1)} %get-tuple-element.168.k_ref, ...), custom_call_target="tpu_custom_call" | custom-call | flops 38000001024 | bytes 20000000 | tf_op jit(solution)/shard_map/attention_backward/pallas_call | solution.py:276
  408.1 2.5 convolution_convert_fusion.6
  410.5 4.7 convolution_convert_fusion.3
  415.3 3.9 add_convert_fusion.2
  421.5 5.0 fusion.82
  431.9 3.5 all-to-all-start.3
  447.1 3.5 fusion.5
  450.6 5.6 fusion.79
  467.8 4.8 all-to-all-start.4
  476.6 17.6 %collective-permute-done.30 = bf16[512,1024]{1,0:T(8,128)(2,1)} collective-permute-done((bf16[512,1024]{1,0:T(8,128)(2,1)}, bf16[512,1024]{1,0:T(8,128)(2,1)}, u32[]{:S(2)}, u32[]{:S(2)}) %collective-permute-start.30) | collective-permute-done | bytes 1048608 | tf_op jit(solution)/shard_map/ppermute | solution.py:352
  494.2 3.5 add_convert_fusion.3
  498.7 3.5 maximum_convert_fusion
  504.4 4.3 all-to-all-start.2
  513.1 11.1 %collective-permute-done.31 = bf16[512,1024]{1,0:T(8,128)(2,1)} collective-permute-done((bf16[512,1024]{1,0:T(8,128)(2,1)}, bf16[512,1024]{1,0:T(8,128)(2,1)}, u32[]{:S(2)}, u32[]{:S(2)}) %collective-permute-start.31) | collective-permute-done | bytes 1048608 | tf_op jit(solution)/shard_map/ppermute | solution.py:331
  524.2 5.1 multiply_reduce_fusion.2
  531.2 6.5 %all-to-all-done.2 = bf16[4,128,1408]{2,1,0:T(8,128)(2,1)} async-done(((bf16[4,128,1408]{2,1,0:T(8,128)(2,1)}), bf16[4,128,1408]{2,1,0:T(8,128)(2,1)}, u32[]{:S(2)}, u32[]{:S(2)}) %all-to-all-start.2) | async-done | bytes 1441824 | tf_op jit(solution)/shard_map/all_to_all | solution.py:359
  539.6 4.9 all-to-all-start.1
  544.6 4.0 add_bitcast_fusion
  552.1 3.4 copy.123
  (327 shorter events, 126.1 us)
Async XLA Ops:
  7.2 44.5 %all-gather.4.cloned.1.call-start = ((), (), s32[]{:S(2)}) async-start(), calls=%async_computation.9 | async-start | bytes 2359296 | tf_op jit(solution)/shard_map/all_gather | solution.py:447
  9.1 104.4 %all-gather.6.cloned.1.call-start = ((), (), s32[]{:S(2)}) async-start(), calls=%async_computation.10 | async-start | bytes 3244032 | tf_op jit(solution)/shard_map/all_gather | solution.py:448
  15.2 20.2 %all-to-all-start = ((bf16[8,16,128]{2,1,0:T(8,128)(2,1)}), bf16[8,16,128]{2,1,0:T(8,128)(2,1)S(1)}, u32[]{:S(2)}, u32[]{:S(2)}) async-start(bf16[8,16,128]{2,1,0:T(8,128)(2,1)} %broadcast_in_dim.199), calls=%async_computation | async-start | bytes 65536 | tf_op jit(solution)/shard_map/all_to_all | solution.py:460
  21.5 207.1 %all-gather.8.cloned.1.call-start = ((), (), s32[]{:S(2)}) async-start(), calls=%async_computation.11 | async-start | bytes 6488064 | tf_op jit(solution)/shard_map/all_gather | solution.py:454
  21.6 25.6 %collective-permute-start = (bf16[512,1024]{1,0:T(8,128)(2,1)S(1)}, bf16[512,1024]{1,0:T(8,128)(2,1)S(1)}, u32[]{:S(2)}, u32[]{:S(2)}) collective-permute-start(bf16[512,1024]{1,0:T(8,128)(2,1)S(1)} %bitcast.99), channel_id=1, source_target_pairs={{0,8},{8,0},{16,24},{24,16},{1,9},{9,1},{17,25},{25,17},{2,10},{10... | collective-permute-start | bytes 3145736 | tf_op jit(solution)/shard_map/ppermute | solution.py:331
  23.2 346.0 %reduce-scatter.5.cloned.1.call-start = ((), (), s32[]{:S(2)}) async-start(), calls=%async_computation.12 | async-start | bytes 6488064 | tf_op jit(solution)/shard_map/reduce_scatter | solution.py:515
  47.2 52.9 %copy-start.26 = (bf16[512,1024]{1,0:T(8,128)(2,1)}, bf16[512,1024]{1,0:T(8,128)(2,1)S(1)}, u32[]{:S(2)}) copy-start(bf16[512,1024]{1,0:T(8,128)(2,1)S(1)} %collective-permute-done) | copy-start | bytes 3145732
  47.2 53.0 %collective-permute-start.1 = (bf16[512,1024]{1,0:T(8,128)(2,1)S(1)}, bf16[512,1024]{1,0:T(8,128)(2,1)}, u32[]{:S(2)}, u32[]{:S(2)}) collective-permute-start(bf16[512,1024]{1,0:T(8,128)(2,1)S(1)} %collective-permute-done), channel_id=1, source_target_pairs={{0,16},{24,8},{1,17},{25,9},{2,18},{26,10},{3,19},{27,11},{4,20},{... | collective-permute-start | bytes 3145736 | tf_op jit(solution)/shard_map/ppermute | solution.py:344
  53.2 45.8 %collective-permute-start.2 = (bf16[512,1024]{1,0:T(8,128)(2,1)S(1)}, bf16[512,1024]{1,0:T(8,128)(2,1)}, u32[]{:S(2)}, u32[]{:S(2)}) collective-permute-start(bf16[512,1024]{1,0:T(8,128)(2,1)S(1)} %constant_dynamic-slice_fusion.4), channel_id=1, source_target_pairs={{0,8},{8,0},{16,24},{24,16},{1,9},{9,1},{17,25},{25,17},{2,10},{10... | collective-permute-start | bytes 3145736 | tf_op jit(solution)/shard_map/ppermute | solution.py:331
  53.2 42.0 %collective-permute-start.4 = (bf16[512,1024]{1,0:T(8,128)(2,1)S(1)}, bf16[512,1024]{1,0:T(8,128)(2,1)}, u32[]{:S(2)}, u32[]{:S(2)}) collective-permute-start(bf16[512,1024]{1,0:T(8,128)(2,1)S(1)} %constant_dynamic-slice_fusion.4), channel_id=1, source_target_pairs={{0,16},{8,24},{16,0},{24,8},{1,17},{9,25},{17,1},{25,9},{2,18},{10... | collective-permute-start | bytes 3145736 | tf_op jit(solution)/shard_map/ppermute | solution.py:331
  56.6 57.0 %copy-start.32 = (f32[1,8,128]{2,0,1:T(1,128)}, f32[1,8,128]{2,0,1:T(1,128)S(1)}, u32[]{:S(2)}) copy-start(f32[1,8,128]{2,0,1:T(1,128)S(1)} %get-tuple-element.336) | copy-start | bytes 12292
  96.4 13.5 %collective-permute-start.7 = (bf16[256,1024]{1,0:T(8,128)(2,1)S(1)}, bf16[256,1024]{1,0:T(8,128)(2,1)S(1)}, u32[]{:S(2)}, u32[]{:S(2)}) collective-permute-start(bf16[256,1024]{1,0:T(8,128)(2,1)S(1)} %slice.517), channel_id=1, source_target_pairs={{0,8},{8,0},{16,24},{24,16},{1,9},{9,1},{17,25},{25,17},{2,10},{10... | collective-permute-start | bytes 1572872 | tf_op jit(solution)/shard_map/ppermute | solution.py:331
  100.1 12.4 %collective-permute-start.6 = (bf16[256,1024]{1,0:T(8,128)(2,1)S(1)}, bf16[256,1024]{1,0:T(8,128)(2,1)S(1)}, u32[]{:S(2)}, u32[]{:S(2)}) collective-permute-start(bf16[256,1024]{1,0:T(8,128)(2,1)S(1)} %slice.516), channel_id=1, source_target_pairs={{0,16},{8,24},{16,0},{24,8},{1,17},{9,25},{17,1},{25,9},{2,18},{10... | collective-permute-start | bytes 1572872 | tf_op jit(solution)/shard_map/ppermute | solution.py:331
  102.7 20.4 %collective-permute-start.3 = (bf16[512,1024]{1,0:T(8,128)(2,1)}, bf16[512,1024]{1,0:T(8,128)(2,1)}, u32[]{:S(2)}, u32[]{:S(2)}) collective-permute-start(bf16[512,1024]{1,0:T(8,128)(2,1)} %collective-permute-done.2.p1), channel_id=1, source_target_pairs={{0,1},{1,0},{2,3},{3,2},{4,5},{5,4},{6,7},{7,6},{8,9},{9,8},{10,11... | collective-permute-start | bytes 3145736 | tf_op jit(solution)/shard_map/ppermute | solution.py:331
  102.8 20.3 %collective-permute-start.5 = (bf16[512,1024]{1,0:T(8,128)(2,1)}, bf16[512,1024]{1,0:T(8,128)(2,1)}, u32[]{:S(2)}, u32[]{:S(2)}) collective-permute-start(bf16[512,1024]{1,0:T(8,128)(2,1)} %collective-permute-done.4.p3), channel_id=1, source_target_pairs={{0,1},{1,0},{2,3},{3,2},{4,5},{5,4},{6,7},{7,6},{8,9},{9,8},{10,11... | collective-permute-start | bytes 3145736 | tf_op jit(solution)/shard_map/ppermute | solution.py:331
  113.5 9.6 %collective-permute-start.8 = (bf16[512,1024]{1,0:T(8,128)(2,1)}, bf16[512,1024]{1,0:T(8,128)(2,1)}, u32[]{:S(2)}, u32[]{:S(2)}) collective-permute-start(bf16[512,1024]{1,0:T(8,128)(2,1)} %pad_maximum_fusion.4.p5), channel_id=1, source_target_pairs={{0,1},{1,0},{2,3},{3,2},{4,5},{5,4},{6,7},{7,6},{8,9},{9,8},{10,11... | collective-permute-start | bytes 3145736 | tf_op jit(solution)/shard_map/ppermute | solution.py:331
  121.0 46.4 %collective-permute-start.9 = (bf16[512,1408]{1,0:T(8,128)(2,1)S(1)}, bf16[512,1408]{1,0:T(8,128)(2,1)S(1)}, u32[]{:S(2)}, u32[]{:S(2)}) collective-permute-start(bf16[512,1408]{1,0:T(8,128)(2,1)S(1)} %constant_dynamic-slice_fusion.2), channel_id=1, source_target_pairs={{0,8},{8,0},{16,24},{24,16},{1,9},{9,1},{17,25},{25,17},{2,10},{10... | collective-permute-start | bytes 4325384 | tf_op jit(solution)/shard_map/ppermute | solution.py:331
  121.4 46.0 %collective-permute-start.10 = (bf16[512,1408]{1,0:T(8,128)(2,1)S(1)}, bf16[512,1408]{1,0:T(8,128)(2,1)S(1)}, u32[]{:S(2)}, u32[]{:S(2)}) collective-permute-start(bf16[512,1408]{1,0:T(8,128)(2,1)S(1)} %constant_dynamic-slice_fusion.2), channel_id=1, source_target_pairs={{0,16},{8,24},{16,0},{24,8},{1,17},{9,25},{17,1},{25,9},{2,18},{10... | collective-permute-start | bytes 4325384 | tf_op jit(solution)/shard_map/ppermute | solution.py:331
  168.4 18.2 %collective-permute-start.13 = (bf16[256,1408]{1,0:T(8,128)(2,1)}, bf16[256,1408]{1,0:T(8,128)(2,1)S(1)}, u32[]{:S(2)}, u32[]{:S(2)}) collective-permute-start(bf16[256,1408]{1,0:T(8,128)(2,1)} %slice.449), channel_id=1, source_target_pairs={{0,16},{8,24},{16,0},{24,8},{1,17},{9,25},{17,1},{25,9},{2,18},{10... | collective-permute-start | bytes 2162696 | tf_op jit(solution)/shard_map/ppermute | solution.py:331
  170.8 18.5 %collective-permute-start.14 = (bf16[256,1408]{1,0:T(8,128)(2,1)}, bf16[256,1408]{1,0:T(8,128)(2,1)S(1)}, u32[]{:S(2)}, u32[]{:S(2)}) collective-permute-start(bf16[256,1408]{1,0:T(8,128)(2,1)} %slice.450), channel_id=1, source_target_pairs={{0,8},{8,0},{16,24},{24,16},{1,9},{9,1},{17,25},{25,17},{2,10},{10... | collective-permute-start | bytes 2162696 | tf_op jit(solution)/shard_map/ppermute | solution.py:331
  173.2 21.6 %collective-permute-start.11 = (bf16[512,1408]{1,0:T(8,128)(2,1)}, bf16[512,1408]{1,0:T(8,128)(2,1)}, u32[]{:S(2)}, u32[]{:S(2)}) collective-permute-start(bf16[512,1408]{1,0:T(8,128)(2,1)} %copy-done.28), channel_id=1, source_target_pairs={{0,1},{1,0},{2,3},{3,2},{4,5},{5,4},{6,7},{7,6},{8,9},{9,8},{10,11... | collective-permute-start | bytes 4325384 | tf_op jit(solution)/shard_map/ppermute | solution.py:331
  173.2 21.6 %collective-permute-start.12 = (bf16[512,1408]{1,0:T(8,128)(2,1)}, bf16[512,1408]{1,0:T(8,128)(2,1)}, u32[]{:S(2)}, u32[]{:S(2)}) collective-permute-start(bf16[512,1408]{1,0:T(8,128)(2,1)} %copy-done.29), channel_id=1, source_target_pairs={{0,1},{1,0},{2,3},{3,2},{4,5},{5,4},{6,7},{7,6},{8,9},{9,8},{10,11... | collective-permute-start | bytes 4325384 | tf_op jit(solution)/shard_map/ppermute | solution.py:331
  190.2 4.7 collective-permute-start.15
  244.2 171.1 %reduce-scatter.7.cloned.1.call-start = ((), (), s32[]{:S(2)}) async-start(), calls=%async_computation.13 | async-start | bytes 2359296 | tf_op jit(solution)/shard_map/reduce_scatter | solution.py:542
  273.0 29.8 %collective-permute-start.16 = (bf16[512,5632]{1,0:T(8,128)(2,1)}, bf16[512,5632]{1,0:T(8,128)(2,1)}, u32[]{:S(2)}, u32[]{:S(2)}) collective-permute-start(bf16[512,5632]{1,0:T(8,128)(2,1)} %convolution_convert_fusion), channel_id=1, source_target_pairs={{0,1},{1,0},{2,3},{3,2},{4,5},{5,4},{6,7},{7,6},{8,9},{9,8},{10,11... | collective-permute-start | bytes 17301512 | tf_op jit(solution)/shard_map/ppermute | solution.py:331
  313.2 47.4 %collective-permute-start.17 = (bf16[256,1408]{1,0:T(8,128)(2,1)S(1)}, bf16[256,1408]{1,0:T(8,128)(2,1)S(1)}, u32[]{:S(2)}, u32[]{:S(2)}) collective-permute-start(bf16[256,1408]{1,0:T(8,128)(2,1)S(1)} %get-tuple-element.305), channel_id=1, source_target_pairs={{0,8},{8,0},{16,24},{24,16},{1,9},{9,1},{17,25},{25,17},{2,10},{10... | collective-permute-start | bytes 2162696 | tf_op jit(solution)/shard_map/ppermute | solution.py:331
  315.7 45.0 %collective-permute-start.18 = (bf16[256,1408]{1,0:T(8,128)(2,1)S(1)}, bf16[256,1408]{1,0:T(8,128)(2,1)S(1)}, u32[]{:S(2)}, u32[]{:S(2)}) collective-permute-start(bf16[256,1408]{1,0:T(8,128)(2,1)S(1)} %get-tuple-element.304), channel_id=1, source_target_pairs={{0,16},{8,24},{16,0},{24,8},{1,17},{9,25},{17,1},{25,9},{2,18},{10... | collective-permute-start | bytes 2162696 | tf_op jit(solution)/shard_map/ppermute | solution.py:331
  318.1 184.1 %reduce-scatter.11.cloned.1.call-start = ((), (), s32[]{:S(2)}) async-start(), calls=%async_computation.15 | async-start | bytes 1802240 | tf_op jit(solution)/shard_map/reduce_scatter | solution.py:395
  319.6 35.9 %copy-start.21 = (bf16[1536,512]{1,0:T(8,128)(2,1)S(1)}, bf16[1536,512]{1,0:T(8,128)(2,1)}, u32[]{:S(2)}) copy-start(bf16[1536,512]{1,0:T(8,128)(2,1)} %get-tuple-element.291) | copy-start | bytes 4718596
  364.8 3.6 collective-permute-start.20
  364.8 3.4 collective-permute-start.19
  365.3 49.9 %collective-permute-start.21 = (bf16[512,1408]{1,0:T(8,128)(2,1)}, bf16[512,1408]{1,0:T(8,128)(2,1)}, u32[]{:S(2)}, u32[]{:S(2)}) collective-permute-start(bf16[512,1408]{1,0:T(8,128)(2,1)} %pad_maximum_fusion.2), channel_id=1, source_target_pairs={{0,8},{8,0},{16,24},{24,16},{1,9},{9,1},{17,25},{25,17},{2,10},{10... | collective-permute-start | bytes 4325384 | tf_op jit(solution)/shard_map/ppermute | solution.py:331
  365.3 49.9 %collective-permute-start.22 = (bf16[512,1408]{1,0:T(8,128)(2,1)}, bf16[512,1408]{1,0:T(8,128)(2,1)}, u32[]{:S(2)}, u32[]{:S(2)}) collective-permute-start(bf16[512,1408]{1,0:T(8,128)(2,1)} %pad_maximum_fusion.3), channel_id=1, source_target_pairs={{0,16},{8,24},{16,0},{24,8},{1,17},{9,25},{17,1},{25,9},{2,18},{10... | collective-permute-start | bytes 4325384 | tf_op jit(solution)/shard_map/ppermute | solution.py:331
  369.1 36.4 %copy-start.38 = (f32[4,8,128]{2,1,0:T(8,128)S(1)}, f32[4,8,128]{2,1,0:T(8,128)}, u32[]{:S(2)}) copy-start(f32[4,8,128]{2,1,0:T(8,128)} %get-tuple-element.204) | copy-start | bytes 49156
  420.1 15.3 %collective-permute-start.25 = (bf16[256,768]{1,0:T(8,128)(2,1)}, bf16[256,768]{1,0:T(8,128)(2,1)}, u32[]{:S(2)}, u32[]{:S(2)}) collective-permute-start(bf16[256,768]{1,0:T(8,128)(2,1)} %get-tuple-element.319), channel_id=1, source_target_pairs={{0,16},{8,24},{16,0},{24,8},{1,17},{9,25},{17,1},{25,9},{2,18},{10... | collective-permute-start | bytes 1179656 | tf_op jit(solution)/shard_map/ppermute | solution.py:331
  421.5 16.0 %collective-permute-start.23 = (bf16[512,512]{1,0:T(8,128)(2,1)}, bf16[512,512]{1,0:T(8,128)(2,1)}, u32[]{:S(2)}, u32[]{:S(2)}) collective-permute-start(bf16[512,512]{1,0:T(8,128)(2,1)} %convolution_convert_fusion.6), channel_id=1, source_target_pairs={{0,1},{1,0},{2,3},{3,2},{4,5},{5,4},{6,7},{7,6},{8,9},{9,8},{10,11... | collective-permute-start | bytes 1572872 | tf_op jit(solution)/shard_map/ppermute | solution.py:331
  426.5 12.2 %collective-permute-start.24 = (bf16[512,1024]{1,0:T(8,128)(2,1)}, bf16[512,1024]{1,0:T(8,128)(2,1)}, u32[]{:S(2)}, u32[]{:S(2)}) collective-permute-start(bf16[512,1024]{1,0:T(8,128)(2,1)} %convolution_convert_fusion.3), channel_id=1, source_target_pairs={{0,1},{1,0},{2,3},{3,2},{4,5},{5,4},{6,7},{7,6},{8,9},{9,8},{10,11... | collective-permute-start | bytes 3145736 | tf_op jit(solution)/shard_map/ppermute | solution.py:331
  427.5 13.9 %collective-permute-start.26 = (bf16[256,768]{1,0:T(8,128)(2,1)}, bf16[256,768]{1,0:T(8,128)(2,1)}, u32[]{:S(2)}, u32[]{:S(2)}) collective-permute-start(bf16[256,768]{1,0:T(8,128)(2,1)} %get-tuple-element.318), channel_id=1, source_target_pairs={{0,8},{8,0},{16,24},{24,16},{1,9},{9,1},{17,25},{25,17},{2,10},{10... | collective-permute-start | bytes 1179656 | tf_op jit(solution)/shard_map/ppermute | solution.py:331
  431.9 34.6 %all-to-all-start.3 = ((bf16[4,120,1024]{2,1,0:T(8,128)(2,1)}), bf16[4,120,1024]{2,1,0:T(8,128)(2,1)S(1)}, u32[]{:S(2)}, u32[]{:S(2)}) async-start(bf16[4,120,1024]{2,1,0:T(8,128)(2,1)} %bitcast.103), calls=%async_computation.7 | async-start | bytes 1966080 | tf_op jit(solution)/shard_map/all_to_all | solution.py:400
  443.6 29.2 %collective-permute-start.28 = (bf16[512,768]{1,0:T(8,128)(2,1)}, bf16[512,768]{1,0:T(8,128)(2,1)}, u32[]{:S(2)}, u32[]{:S(2)}) collective-permute-start(bf16[512,768]{1,0:T(8,128)(2,1)} %fusion.18), channel_id=1, source_target_pairs={{0,16},{8,24},{16,0},{24,8},{1,17},{9,25},{17,1},{25,9},{2,18},{10... | collective-permute-start | bytes 2359304 | tf_op jit(solution)/shard_map/ppermute | solution.py:331
  445.6 27.2 %collective-permute-start.27 = (bf16[512,768]{1,0:T(8,128)(2,1)}, bf16[512,768]{1,0:T(8,128)(2,1)}, u32[]{:S(2)}, u32[]{:S(2)}) collective-permute-start(bf16[512,768]{1,0:T(8,128)(2,1)} %pad_maximum_fusion.11), channel_id=1, source_target_pairs={{0,8},{8,0},{16,24},{24,16},{1,9},{9,1},{17,25},{25,17},{2,10},{10... | collective-permute-start | bytes 2359304 | tf_op jit(solution)/shard_map/ppermute | solution.py:331
  459.1 35.2 %collective-permute-start.30 = (bf16[512,1024]{1,0:T(8,128)(2,1)}, bf16[512,1024]{1,0:T(8,128)(2,1)}, u32[]{:S(2)}, u32[]{:S(2)}) collective-permute-start(bf16[512,1024]{1,0:T(8,128)(2,1)} %broadcast_select_fusion.2), channel_id=1, source_target_pairs={{8,24},{16,0},{9,25},{17,1},{10,26},{18,2},{11,27},{19,3},{12,28},... | collective-permute-start | bytes 3145736 | tf_op jit(solution)/shard_map/ppermute | solution.py:352
  460.4 4.4 collective-permute-start.29
  467.8 34.4 %all-to-all-start.4 = ((bf16[4,120,1024]{2,1,0:T(8,128)(2,1)}), bf16[4,120,1024]{2,1,0:T(8,128)(2,1)S(1)}, u32[]{:S(2)}, u32[]{:S(2)}) async-start(bf16[4,120,1024]{2,1,0:T(8,128)(2,1)} %broadcast_in_dim.226), calls=%async_computation.8 | async-start | bytes 1966080 | tf_op jit(solution)/shard_map/all_to_all | solution.py:359
  472.5 56.7 %reduce-scatter.9.cloned.1.call-start = ((), (), s32[]{:S(2)}) async-start(), calls=%async_computation.14 | async-start | bytes 1146880 | tf_op jit(solution)/shard_map/reduce_scatter | solution.py:395
  497.7 26.4 %collective-permute-start.31 = (bf16[512,1024]{1,0:T(8,128)(2,1)}, bf16[512,1024]{1,0:T(8,128)(2,1)}, u32[]{:S(2)}, u32[]{:S(2)}) collective-permute-start(bf16[512,1024]{1,0:T(8,128)(2,1)} %add_convert_fusion.3), channel_id=1, source_target_pairs={{0,8},{8,0},{16,24},{24,16},{1,9},{9,1},{17,25},{25,17},{2,10},{10... | collective-permute-start | bytes 3145736 | tf_op jit(solution)/shard_map/ppermute | solution.py:331
  504.4 33.2 %all-to-all-start.2 = ((bf16[4,128,1408]{2,1,0:T(8,128)(2,1)}), bf16[4,128,1408]{2,1,0:T(8,128)(2,1)}, u32[]{:S(2)}, u32[]{:S(2)}) async-start(bf16[4,128,1408]{2,1,0:T(8,128)(2,1)} %broadcast_in_dim.225), calls=%async_computation.6 | async-start | bytes 2883584 | tf_op jit(solution)/shard_map/all_to_all | solution.py:359
  539.6 17.9 %all-to-all-start.1 = ((bf16[4,128,896]{1,2,0:T(8,128)(2,1)}), bf16[4,128,896]{1,2,0:T(8,128)(2,1)}, u32[]{:S(2)}, u32[]{:S(2)}) async-start(bf16[4,128,896]{1,2,0:T(8,128)(2,1)} %broadcast_in_dim.222), calls=%async_computation.4 | async-start | bytes 1835008 | tf_op jit(solution)/shard_map/all_to_all | solution.py:359
  (49 other events, 404.5 us)
Sparse Core Ops, SparseCore 0:
  10.2 32.9 all-gather.3
  45.4 35.1 all-gather.5
  82.2 59.2 all-gather.7
  244.3 67.2 reduce-scatter.4
  318.2 34.1 reduce-scatter.6
  429.8 31.5 reduce-scatter.10
  476.7 25.7 reduce-scatter.8

commit v3 on v2

--- a/solution.py
+++ b/solution.py
@@ -219,7 +219,7 @@
     return pl.BlockSpec(shape,lambda j,s:(0,)*n)
 def colb(rows,width): return pl.BlockSpec((rows,width),lambda j,s:(0,j))
 def lead(*shape): return pl.BlockSpec((None,)+shape,lambda j,s:(j,)+(0,)*len(shape))
-ANYWHERE=pl.BlockSpec(memory_space=pl.ANY)
+ANYWHERE=pl.BlockSpec(memory_space=pltpu.HBM)
 
 def attention_forward(place,xn,pieces,gq,gk,cos,sin,qb,kb,sv,mats):
     rows,ext=qb.shape[0],kb.shape[0]
@@ -240,33 +240,104 @@
                    jax.ShapeDtypeStruct((QUADS,rows,LANES),F32),jax.ShapeDtypeStruct((QUADS,ext,LANES),F32),
                    jax.ShapeDtypeStruct((D,n),BF),jax.ShapeDtypeStruct((D,2*n),BF),jax.ShapeDtypeStruct((D,n),BF)],
         compiler_params=pltpu.CompilerParams(vmem_limit_bytes=56*2**20),
-        cost_estimate=pl.CostEstimate(flops=45 * 10**9, bytes_accessed=40 * 10**6, transcendentals=0),
+        cost_estimate=pl.CostEstimate(flops=10**6, bytes_accessed=10**4, transcendentals=0),
         name="attention_forward",
     )(place,xn,*pieces,gq,gk,cos,sin,qb,kb,sv,mean_mat,swap_mat)
 
-def ffn_up_kernel(place_ref,x_ref,p0,p1,p2,p3,p4,p5,p6,out_ref,w_out,w_ref,sem):
-    await_quarter(place_ref,(p0,p1,p2,p3,p4,p5,p6),w_ref,sem)
-    step=pl.program_id(0)
-    w_out[...]=w_ref[step]
-    width=out_ref.shape[1]
-    for begin in range(0,width,256):
-        cols=slice(begin,min(begin+256,width))
-        out_ref[:,cols]=dot_nn(x_ref[...],w_ref[step,:,cols])
-
-def ffn_up(place,x,pieces):
+def feed_forward_kernel(place_ref,weight_ref,gain_ref,obs_ref,x_in,mixed_in,teacher_in,cot_in,low_in,attn_in,p0,p1,p2,p3,p4,p5,p6,
+                        hidden_out,d_up_out,act_out,d_low_out,d_mixed_out,d_mixed_low_out,d_attn_out,sum_ref,
+                        w_ref,low_ref,attn_ref,x_ref,mixed_ref,teacher_ref,cot_ref,gate_up_ref,hidden_ref,act_ref,d_low_ref,d_final_ref,acc_ref,
+                        in_sem,piece_sem,out_sem):
+    arrivals=[pltpu.make_async_copy(src,dst,in_sem.at[i]) for i,(src,dst) in enumerate(
+        [(x_in,x_ref),(mixed_in,mixed_ref),(low_in,low_ref),(teacher_in,teacher_ref),(cot_in,cot_ref),(attn_in,attn_ref)])]
+    pieces=piece_copies(place_ref,(p0,p1,p2,p3,p4,p5,p6),w_ref,piece_sem)
+    arrivals[0].start()
+    for group in pieces:
+        for copy in group: copy.start()
+    for copy in arrivals[1:]: copy.start()
+    sent=[]
+    def send(ref,out):
+        copy=pltpu.make_async_copy(ref,out,out_sem.at[len(sent)])
+        copy.start(); sent.append(copy)
+    arrivals[0].wait()
+    width=w_ref.shape[2]
+    tiles=[slice(begin,min(begin+256,width)) for begin in range(0,width,256)]
+    for half in range(2):
+        for quarter in (half,half+2):
+            slot=place_ref[0]^quarter
+            for i,group in enumerate(pieces):
+                @pl.when(slot==i)
+                def _(group=group):
+                    for copy in group: copy.wait()
+        for tile in tiles:
+            at=slice(half*width+tile.start,half*width+tile.stop); up_at=slice(FF+at.start,FF+at.stop)
+            gate=dot_nn(x_ref[...],w_ref[half,:,tile])
+            up=dot_nn(x_ref[...],w_ref[half+2,:,tile])
+            gate_up_ref[:,at]=gate.astype(BF)
+            gate_up_ref[:,up_at]=up.astype(BF)
+            hidden_ref[:,at]=(gate/(1.0+jnp.exp(-gate))*up).astype(BF)
+    send(hidden_ref,hidden_out)
+    for copy in arrivals[1:]: copy.wait()
+    total=jnp.zeros((1,256),F32)
+    for begin in range(0,D,256):
+        cols=slice(begin,begin+256)
+        final=mixed_ref[:,cols]+dot_nn(hidden_ref[...],low_ref[:,cols])
+        act_ref[:,cols]=final.astype(BF)
+        distance=final-teacher_ref[:,cols].astype(F32)
+        seen=obs_ref[...]*distance
+        total=total+jnp.sum(seen*distance,axis=0,keepdims=True)
+        d_final=cot_ref[:,cols].astype(F32)+weight_ref[0]*seen
+        d_final_ref[:,cols]=d_final
+        d_low_ref[:,cols]=d_final.astype(BF)
+    sum_ref[...]=total
+    send(act_ref,act_out)
+    send(d_low_ref,d_low_out)
+    for begin in range(0,FF,256):
+        cols=slice(begin,begin+256); ups=slice(FF+begin,FF+begin+256)
+        d_hidden=dot_nt(d_low_ref[...],low_ref[cols,:])
+        gate=gate_up_ref[:,cols].astype(F32); up=gate_up_ref[:,ups].astype(F32)
+        sig=1.0/(1.0+jnp.exp(-gate))
+        gate_up_ref[:,cols]=(d_hidden*up*(sig*(1.0+gate*(1.0-sig)))).astype(BF)
+        gate_up_ref[:,ups]=(d_hidden*(gate*sig)).astype(BF)
+    send(gate_up_ref,d_up_out)
+    for begin in range(0,D,256):
+        part=None
+        for quarter in range(QUADS):
+            one=dot_nt(gate_up_ref[:,quarter*width:(quarter+1)*width],w_ref[quarter,begin:begin+256,:])
+            part=one if part is None else part+one
+        acc_ref[:,begin:begin+256]=part
+    mixed=mixed_ref[...]
+    c=lax.rsqrt(jnp.mean(mixed*mixed,axis=1,keepdims=True)+EPSILON)
+    scaled=acc_ref[...]*gain_ref[...]
+    unit=mixed*c
+    d_mixed=d_final_ref[...]+c*(scaled-unit*jnp.mean(unit*scaled,axis=1,keepdims=True))
+    d_final_ref[...]=d_mixed
+    send(d_final_ref,d_mixed_out)
+    x_ref[...]=d_mixed.astype(BF)
+    send(x_ref,d_mixed_low_out)
+    for begin in range(0,D,256):
+        teacher_ref[:,begin:begin+256]=dot_nt(x_ref[...],attn_ref[begin:begin+256,:]).astype(BF)
+    send(teacher_ref,d_attn_out)
+    for copy in sent: copy.wait()
+
+def feed_forward(place,weight,gain,obs,x,mixed,teacher,cotangent,w_lower,w_attn,pieces):
     rows=x.shape[0]; width=pieces[0].shape[1]
+    low=jax.ShapeDtypeStruct((rows,D),BF)
+    smem=pl.BlockSpec(memory_space=pltpu.SMEM); vmem=pl.BlockSpec(memory_space=pltpu.VMEM)
+    square=pltpu.VMEM((rows,D),BF); wide=pltpu.VMEM((rows,D),F32)
     return pl.pallas_call(
-        ffn_up_kernel,
-        grid_spec=pltpu.PrefetchScalarGridSpec(
-            num_scalar_prefetch=1,grid=(QUADS,),
-            in_specs=[full(rows,D)]+[ANYWHERE]*7,
-            out_specs=[colb(rows,width),colb(D,width)],
-            scratch_shapes=[pltpu.VMEM((QUADS,D,width),BF),pltpu.SemaphoreType.DMA((7,))]),
-        out_shape=[jax.ShapeDtypeStruct((rows,QUADS*width),F32),jax.ShapeDtypeStruct((D,QUADS*width),BF)],
-        compiler_params=pltpu.CompilerParams(vmem_limit_bytes=56*2**20),
-        cost_estimate=pl.CostEstimate(flops=10 * 10**9, bytes_accessed=30 * 10**6, transcendentals=0),
-        name="ffn_up",
-    )(place,x,*pieces)
+        feed_forward_kernel,
+        in_specs=[smem,smem,vmem,vmem]+[ANYWHERE]*13,
+        out_specs=[ANYWHERE]*7+[vmem],
+        out_shape=[jax.ShapeDtypeStruct((rows,FF),BF),jax.ShapeDtypeStruct((rows,2*FF),BF),low,low,jax.ShapeDtypeStruct((rows,D),F32),low,low,
+                   jax.ShapeDtypeStruct((1,256),F32)],
+        scratch_shapes=[pltpu.VMEM((QUADS,D,width),BF),pltpu.VMEM((FF,D),BF),pltpu.VMEM((D,D),BF),square,wide,square,square,
+                        pltpu.VMEM((rows,2*FF),BF),pltpu.VMEM((rows,FF),BF),square,square,wide,wide,
+                        pltpu.SemaphoreType.DMA((6,)),pltpu.SemaphoreType.DMA((7,)),pltpu.SemaphoreType.DMA((7,))],
+        compiler_params=pltpu.CompilerParams(vmem_limit_bytes=58*2**20),
+        cost_estimate=pl.CostEstimate(flops=10**6, bytes_accessed=10**4, transcendentals=0),
+        name="feed_forward",
+    )(place,weight,gain,obs,x,mixed,teacher,cotangent,w_lower,w_attn,*pieces)
 
 def attention_backward(place,call,q,k,v,do,attn,lse,cq,ck,gq,gk,cos,sin,qb,kb,sv,mats):
     rows,ext=qb.shape[0],kb.shape[0]
@@ -285,9 +356,30 @@
         out_shape=[jax.ShapeDtypeStruct((rows,512),BF),jax.ShapeDtypeStruct((ext,1024),BF),
                    jax.ShapeDtypeStruct((QUADS,1,256),F32),jax.ShapeDtypeStruct((QUADS,1,256),F32),jax.ShapeDtypeStruct((QUADS,8,LANES),F32)],
         compiler_params=pltpu.CompilerParams(vmem_limit_bytes=56*2**20),
-        cost_estimate=pl.CostEstimate(flops=38 * 10**9, bytes_accessed=20 * 10**6, transcendentals=0),
+        cost_estimate=pl.CostEstimate(flops=10**6, bytes_accessed=10**4, transcendentals=0),
         name="attention_backward",
     )(place,q,k,v,do,attn,lse,cq,ck,gq,gk,cos,sin,qb,kb,sv,*mats)
+
+def finish_kernel(layout,spread_ref,weight_ref,grad_ref,sum_ref):
+    total=None
+    for quarter in range(QUADS):
+        for begin,width,base in layout:
+            at=slice(base+quarter*width,base+(quarter+1)*width)
+            grad=spread_ref[quarter,:,begin:begin+width].astype(F32)
+            grad_ref[:,at]=grad
+            part=jnp.sum(grad*weight_ref[:,at].astype(F32),axis=1,keepdims=True)
+            total=part if total is None else total+part
+    sum_ref[...]=total
+
+def finish(spread,weight,layout):
+    vmem=pl.BlockSpec(memory_space=pltpu.VMEM)
+    return pl.pallas_call(
+        lambda *refs: finish_kernel(layout,*refs),in_specs=[vmem]*2,out_specs=[vmem]*2,
+        out_shape=[jax.ShapeDtypeStruct(weight.shape,F32),jax.ShapeDtypeStruct((weight.shape[0],1),F32)],
+        compiler_params=pltpu.CompilerParams(vmem_limit_bytes=32*2**20),
+        cost_estimate=pl.CostEstimate(flops=10**6, bytes_accessed=10**4, transcendentals=0),
+        name="finish",
+    )(spread,weight)
 
 def features(query_doc,query_var,key_doc,key_var,key_obs,key_inside):
     lane=jnp.arange(HEAD)[None,:]
@@ -336,22 +428,14 @@
     return lax.ppermute(shard, "ctx", [(i, i + by) for i in range(size) if 0 <= i + by < size])
 
 
-def neighbours(shard):
-    if lax.axis_size("ctx") != 4:
-        return shifted(shard, 1), shifted(shard, -1)
+def returned_far(before, after):
     odd = lax.axis_index("ctx") % 2 == 1
-    near = permuted(shard, "ctx", 1)
-    far = lax.ppermute(near, "ctx", [(0, 2), (3, 1)])
-    return jnp.where(odd, near, far), jnp.where(odd, far, near)
-
-
-def returned(before, after):
-    if lax.axis_size("ctx") != 4:
-        return shifted(before, -1).astype(F32) + shifted(after, 1).astype(F32)
+    return lax.ppermute(jnp.where(odd, after, before), "ctx", [(1, 3), (2, 0)])
+
+
+def returned_near(before, after, far):
     odd = lax.axis_index("ctx") % 2 == 1
-    far = lax.ppermute(jnp.where(odd, after, before), "ctx", [(1, 3), (2, 0)])
-    near = jnp.where(odd, before, after).astype(F32) + far.astype(F32)
-    return permuted(near.astype(BF), "ctx", 1).astype(F32)
+    return permuted(added(jnp.where(odd, before, after), far), "ctx", 1)
 
 
 def ctx_spread(part):
@@ -395,11 +479,14 @@
     return lax.psum_scatter(total, "fsdp", scatter_dimension=0, axis_index_groups=same_core, tiled=True)
 
 
-def ctx_sum(part):
+def ctx_parts(part):
     size = lax.axis_size("ctx")
-    parts = lax.all_to_all(part.reshape(size, part.shape[0] // size, part.shape[1]), "ctx", 0, 0)
+    return lax.all_to_all(part.reshape(size, part.shape[0] // size, part.shape[1]), "ctx", 0, 0)
+
+
+def ctx_joined(parts):
     total = jnp.sum(parts.astype(F32), axis=0).astype(BF)
-    return ctx_spread(total).reshape(part.shape)
+    return ctx_spread(total).reshape(-1, parts.shape[2])
 
 
 def document_ids(doc_lengths, positions):
@@ -409,12 +496,6 @@
 
 def rms_scale(vector, scales):
     return vector * lax.rsqrt(jnp.mean(vector * vector, axis=-1, keepdims=True) + EPSILON) * scales
-
-
-def gated_unit(gate_up):
-    gate_part = gate_up[:, :FF]
-    up_part = gate_up[:, FF:]
-    return gate_part / (1.0 + jnp.exp(-gate_part)) * up_part
 
 
 def digits_of(value):
@@ -452,23 +533,26 @@
         w_attention = jnp.swapaxes(w_attention.reshape(D, 4, QUADS, 256), 1, 2).reshape(D, QUADS, 1024)
         w_in = lax.all_gather(ffn_in, "fsdp", axis=0, tiled=True).reshape(D, QUADS, FF // 2)
     w_lower = lax.all_gather(ffn_out, "fsdp", axis=0, tiled=True)
-    before, behind = neighbours(tokens[0])
     own_count = jnp.sum(observed[0])
     small = jnp.zeros((16, gains_n), BF)
     small = small.at[:4].set(norm_gains).at[4, :bias_n].set(var_bias)
     small = small.at[5, 0].set((own_count // 256).astype(BF)).at[5, 1].set((own_count % 256).astype(BF))
-    small = lax.all_to_all(jnp.broadcast_to(small[None], (n_shards,) + small.shape), "fsdp", 0, 0)
-    if quartered:
+    if quartered:
+        beside = permuted(tokens[0], "ctx", 1)
         mine = halves_of(whole, core)
+        mine, small, beside = tied(mine, small, beside)
+        across = lax.ppermute(beside, "ctx", [(0, 2), (3, 1)])
+        odd = me % 2 == 1
+        before, behind = jnp.where(odd, beside, across), jnp.where(odd, across, beside)
         near, up = permuted(mine, "ctx", 1), permuted(mine, "ctx", 2)
-        corner = corner_of(near, up)
-        whole_in, corner = tied(whole_in, corner)
-        pieces = (whole,) + with_partner(near) + with_partner(up) + with_partner(corner)
-        mine_in = halves_of(whole_in, core)
-        near_in, up_in = permuted(mine_in, "ctx", 1), permuted(mine_in, "ctx", 2)
     else:
+        before, behind = shifted(tokens[0], 1), shifted(tokens[0], -1)
         split = lambda w: (w[:, 0],) + tuple(w[i * D // 2 : (i + 1) * D // 2, j] for j in range(1, QUADS) for i in range(2))
         pieces, pieces_in = split(w_attention), split(w_in)
+
+    small = lax.all_to_all(jnp.broadcast_to(small[None], (n_shards,) + small.shape), "fsdp", 0, 0)
+
+    before, behind, small = tied(before, behind, small)
 
     gains = jnp.moveaxis(small[:, :4], 0, 1).reshape(4, D).astype(F32)
     bias = small[:, 4, :bias_n].reshape(2 * HEADS).astype(F32)
@@ -489,75 +573,69 @@
     inv = lax.rsqrt(jnp.mean(inputs * inputs, axis=-1, keepdims=True) + EPSILON)
     normed = (inputs * inv * gains[0]).astype(BF)
 
+    if quartered:
+        near, up, normed, whole_in = tied(near, up, normed, whole_in)
+        corner = corner_of(near, up)
+        mine_in = halves_of(whole_in, core)
+        in_by = [permuted(mine_in, "ctx", flip) for flip in (1, 2, 3)]
+        pieces = (whole,) + with_partner(near) + with_partner(up) + with_partner(corner)
+
     q, k, v, attn, lse, c_q, c_k, w_q, w_kv, w_attn = attention_forward(
         place, normed, pieces, gain_q, gain_k, cosine, sine, query_feat, key_feat, scales, mats
     )
     if quartered:
-        near_in, up_in, attn = tied(near_in, up_in, attn)
-        corner_in = corner_of(near_in, up_in)
-        pieces_in = (whole_in,) + with_partner(near_in) + with_partner(up_in) + with_partner(corner_in)
+        in_by, attn = tied(in_by, attn)
+        pieces_in = (whole_in,) + sum((with_partner(piece) for piece in in_by), ())
     mixed = tokens[0].astype(F32) + jnp.dot(attn, w_attn, preferred_element_type=F32)
-    normed_two_f, norm_two_pull = jax.vjp(lambda m: rms_scale(m, gains[1]), mixed)
-    normed_two = normed_two_f.astype(BF)
-    gate_up, w_upper = ffn_up(place, normed_two, pieces_in)
-    hidden_f, glu_pull = jax.vjp(gated_unit, gate_up)
-    hidden = hidden_f.astype(BF)
-    final = mixed + jnp.dot(hidden, w_lower, preferred_element_type=F32)
+    normed_two = rms_scale(mixed, gains[1]).astype(BF)
     valid_col = key_obs[own].astype(F32)[:, None]
-    distance = final - teacher[0].astype(F32)
-    squared = jnp.sum(valid_col * distance * distance)
     all_tokens = rows * n_context * n_shards
-    d_final = cotangent[0].astype(F32) + all_tokens * valid_col * distance / valid_total
-    d_final_low = d_final.astype(BF)
-
-    low_grad = dot_tn(hidden, d_final_low).astype(BF)
-    d_final_low, low_grad = tied(d_final_low, low_grad)
-    low_part = lax.psum_scatter(low_grad, "fsdp", scatter_dimension=0, tiled=True)
-    d_hidden = dot_nt(d_final_low, w_lower)
-    (d_gate_up,) = glu_pull(d_hidden)
-    d_gate_low = d_gate_up.astype(BF)
+    hidden, d_gate_low, activations, d_final_low, d_mixed, d_mixed_low, d_attn, squared = feed_forward(
+        place, (all_tokens / valid_total)[None], gains[1:2], valid_col, normed_two, mixed, teacher[0], cotangent[0], w_lower, w_attn, pieces_in
+    )
+    squared = jnp.sum(squared)
+
     if quartered:
         own_two, other_two = sides(normed_two, core)
         theirs = dot_tn(other_two, d_gate_low).astype(BF)
-        d_gate_low, theirs = tied(d_gate_low, theirs)
+        hidden, theirs = tied(hidden, theirs)
         swapped = permuted(theirs, "fsdp", 1)
-        d_normed_two = dot_nt(d_gate_low, w_upper)
-        d_gate_low, d_normed_two = tied(d_gate_low, d_normed_two)
+    low_grad = dot_tn(hidden, d_final_low).astype(BF)
+    d_mixed_low, low_grad = tied(d_mixed_low, low_grad)
+    low_part = lax.psum_scatter(low_grad, "fsdp", scatter_dimension=0, tiled=True)
+    out_grad = dot_tn(attn, d_mixed_low).astype(BF)
+    if quartered:
+        d_gate_low, out_grad = tied(d_gate_low, out_grad)
         in_chip = (dot_tn(own_two, d_gate_low) + swapped.astype(F32)).astype(BF)
         part = lambda j: lax.dynamic_slice_in_dim(in_chip, (me ^ j) * (FF // 2), FF // 2, 1)
         cut = in_chip.shape[0] // 2
         last = part(3)
+        d_attn, last = tied(d_attn, last)
+        last_near, last_up = permuted(last[:cut], "ctx", 1), permuted(last[cut:], "ctx", 2)
     else:
-        d_normed_two = dot_nt(d_gate_low, w_upper)
         in_part = lax.psum_scatter(dot_tn(normed_two, d_gate_low).astype(BF), "fsdp", scatter_dimension=0, tiled=True)
         in_grad = lax.psum(in_part, "ctx").astype(F32)
-        last = in_part
-    (d_mixed_part,) = norm_two_pull(d_normed_two)
-    d_mixed = d_final + d_mixed_part
-    d_mixed_low = d_mixed.astype(BF)
-    out_grad = dot_tn(attn, d_mixed_low).astype(BF)
-    d_attn = dot_nt(d_mixed_low, w_attn).astype(BF)
-
-    d_attn, last, out_grad = tied(d_attn, last, out_grad)
+
+    d_attn, out_grad = tied(d_attn, out_grad)
     out_part = lax.psum_scatter(out_grad, "fsdp", scatter_dimension=0, tiled=True)
-    if quartered:
-        last_near, last_up = permuted(last[:cut], "ctx", 1), permuted(last[cut:], "ctx", 2)
     saved = (q, k, v, d_attn, attn, lse, c_q, c_k, gain_q, gain_k, cosine, sine, query_feat, key_feat, scales, mats)
     d_q1, d_kv1, gain_q1, gain_k1, bias_1 = attention_backward(place, 0, *saved)
     if quartered:
+        d_q1, d_kv1, last_near, last_up = tied(d_q1, d_kv1, last_near, last_up)
+        d_q1, d_kv1, low_part = tied(d_q1, d_kv1, low_part)
         own_normed, other_normed = sides(normed, core)
         theirs = [dot_tn(other_normed[own], d_q1).astype(BF), dot_tn(other_normed, d_kv1).astype(BF)]
-        last_near, last_up, theirs = tied(last_near, last_up, theirs)
-        swapped = [permuted(t, "fsdp", 1) for t in theirs]
         one, two = part(1), part(2)
         one, two = joined(one[:cut], added(one[cut:], last_up)), joined(added(two[:cut], last_near), two[cut:])
-        d_q1, d_kv1, one, two = tied(d_q1, d_kv1, one, two)
+        theirs, d_q1, d_kv1, one, two = tied(theirs, d_q1, d_kv1, one, two)
+        swapped = [permuted(t, "fsdp", 1) for t in theirs]
         in_near, in_up = permuted(one, "ctx", 1), permuted(two, "ctx", 2)
         first_q = (dot_tn(own_normed[own], d_q1) + swapped[0].astype(F32)).astype(BF)
         first_kv = (dot_tn(own_normed, d_kv1) + swapped[1].astype(F32)).astype(BF)
-        quarters = {3: jnp.concatenate([first_q[:, :256], first_kv[:, :512]], axis=1), 1: jnp.concatenate([first_q[:, 256:], first_kv[:, 512:]], axis=1)}
-        d_attn, quarters, low_part = tied(d_attn, quarters, low_part)
-        last_near, last_up = permuted(quarters[3][:cut], "ctx", 1), permuted(quarters[3][cut:], "ctx", 2)
+        three = jnp.concatenate([first_q[:, :256], first_kv[:, :512]], axis=1)
+        one = jnp.concatenate([first_q[:, 256:], first_kv[:, 512:]], axis=1)
+        d_attn, three, one = tied(d_attn, three, one)
+        last_near, last_up = permuted(three[:cut], "ctx", 1), permuted(three[cut:], "ctx", 2)
         saved = saved[:3] + (d_attn,) + saved[4:]
     d_q2, d_kv2, gain_q2, gain_k2, bias_2 = attention_backward(place, 1, *saved)
     done_first = ((me ^ jnp.arange(QUADS)) % 2 == 1)[:, None, None]
@@ -573,34 +651,46 @@
         extra = extra.reshape(n_shards // 2, 2, D // n_shards, LANES).astype(BF)
         own_extra = jnp.where(core == 0, extra[:, 0], extra[:, 1]).reshape(-1, LANES)
         other_extra = jnp.where(core == 0, extra[:, 1], extra[:, 0]).reshape(-1, LANES)
-        theirs = [dot_tn(other_normed[own], d_q2).astype(BF), dot_tn(other_normed, d_kv2).astype(BF), other_extra]
-        theirs, in_near, in_up, out_part = tied(theirs, in_near, in_up, out_part)
-        swapped = [permuted(t, "fsdp", 1) for t in theirs]
+        d_q2, d_kv2, last_near, last_up = tied(d_q2, d_kv2, last_near, last_up)
+        d_q2, d_kv2, in_near, in_up, out_part = tied(d_q2, d_kv2, in_near, in_up, out_part)
         in_total = added(part(0), in_near, in_up)
         d_q2, d_kv2, in_total = tied(d_q2, d_kv2, in_total)
         in_part = core_scatter(in_total)
+        other_grads = ctx_parts(joined(out_part, low_part))
+    d_ext = dot_nt(d_kv1, w_kv[:, : 2 * 512]) + dot_nt(d_kv2, w_kv[:, 2 * 512 :])
+    to_before, to_behind = d_ext[:HALF].astype(BF), d_ext[HALF + rows :].astype(BF)
+    if quartered:
+        to_before, to_behind, d_q2, d_kv2 = tied(to_before, to_behind, d_q2, d_kv2)
+        far = returned_far(to_before, to_behind)
+        theirs = [dot_tn(other_normed[own], d_q2).astype(BF), dot_tn(other_normed, d_kv2).astype(BF), other_extra]
+        theirs, d_q2, d_kv2, other_grads = tied(theirs, d_q2, d_kv2, other_grads)
+        other_grads = ctx_joined(other_grads)
+        swapped = [permuted(t, "fsdp", 1) for t in theirs]
         second_q = (dot_tn(own_normed[own], d_q2) + swapped[0].astype(F32)).astype(BF)
         second_kv = (dot_tn(own_normed, d_kv2) + swapped[1].astype(F32)).astype(BF)
-        quarters[2] = jnp.concatenate([second_q[:, :256], second_kv[:, :512]], axis=1)
-        quarters[0] = jnp.concatenate([second_q[:, 256:], second_kv[:, 512:]], axis=1)
-        one = joined(quarters[1][:cut], added(quarters[1][cut:], last_up))
-        two = joined(added(quarters[2][:cut], last_near), quarters[2][cut:])
-        d_kv2, d_q2, one, two = tied(d_kv2, d_q2, one, two)
+        two = jnp.concatenate([second_q[:, :256], second_kv[:, :512]], axis=1)
+        one = joined(one[:cut], added(one[cut:], last_up))
+        two = joined(added(two[:cut], last_near), two[cut:])
+        one, two, far = tied(one, two, far)
         near, up = permuted(one, "ctx", 1), permuted(two, "ctx", 2)
-    d_ext = dot_nt(d_kv1, w_kv[:, : 2 * 512]) + dot_nt(d_kv2, w_kv[:, 2 * 512 :])
-    from_others = returned(d_ext[:HALF].astype(BF), d_ext[HALF + rows :].astype(BF))
-    d_own = d_ext[own] + dot_nt(d_q1, w_q[:, : 2 * 256]) + dot_nt(d_q2, w_q[:, 2 * 256 :])
-    if quartered:
-        qkv_total = jnp.concatenate([added(quarters[0], near, up), added(own_extra, swapped[2])], axis=1)
+        in_part, other_grads, far = tied(in_part, other_grads, far)
+        near, up, in_part, far = tied(near, up, in_part, far)
+        from_others = returned_near(to_before, to_behind, far)
+        in_spread = ctx_spread(in_part)
+        qkv_total = added(jnp.concatenate([second_q[:, 256:], second_kv[:, 512:]], axis=1), near, up)
+        qkv_total = jnp.concatenate([qkv_total, added(own_extra, swapped[2])], axis=1)
         qkv_part = core_scatter(qkv_total)
+        qkv_part, in_spread = tied(qkv_part, in_spread)
         spread = ctx_spread(qkv_part)
-        qkv_grad = jnp.transpose(spread[:, :, : 3 * 256].reshape(QUADS, -1, 3, 256), (1, 2, 0, 3)).reshape(-1, 3 * D).astype(F32)
+        from_others, spread = tied(from_others, spread)
+        from_others = from_others.astype(F32)
+        qkv_grad, gain_one = finish(spread, qkv_weight, tuple((i * 256, 256, i * D) for i in range(3)))
         sums = jnp.sum(spread[:, :, 3 * 256 :].astype(F32), axis=0)
         squared = value_of(sums[3, :DIGITS])
         gain_rows, var_bias_grad = sums[:2, :gains_n], sums[2, :bias_n]
-        in_grad = jnp.swapaxes(ctx_spread(in_part), 0, 1).reshape(-1, 2 * FF).astype(F32)
-        other_grads = ctx_sum(joined(out_part, low_part)).astype(F32)
+        in_grad, gain_two = finish(in_spread, ffn_in, ((0, FF // 2, 0),))
     else:
+        from_others = shifted(to_before, -1).astype(F32) + shifted(to_behind, 1).astype(F32)
         order = [SEND_ORDER.index(j) for j in range(QUADS)]
         natural = lambda first, second, width: jnp.concatenate([first, second], axis=1).reshape(-1, QUADS, width)[:, jnp.array(order)]
         grad_q = dot_tn(normed[own], natural(d_q1, d_q2, 256).reshape(rows, D))
@@ -613,17 +703,21 @@
         gain_rows = lax.dynamic_slice_in_dim(sums[: 2 * D].reshape(2, D), shard_id * gains_n, gains_n, 1)
         var_bias_grad = lax.dynamic_slice_in_dim(sums[2 * D : 2 * D + 2 * HEADS], shard_id * bias_n, bias_n, 0)
         squared = sums[2 * D + 2 * HEADS]
+    d_own = d_ext[own] + dot_nt(d_q1, w_q[:, : 2 * 256]) + dot_nt(d_q2, w_q[:, 2 * 256 :])
     loss = squared / (valid_total * D)
     own_gains = norm_gains.astype(F32)
-    gain_one = jnp.sum(qkv_weight.astype(F32) * qkv_grad, axis=1) / own_gains[0]
-    gain_two = jnp.sum(ffn_in.astype(F32) * in_grad, axis=1) / own_gains[1]
-    gains_grad = jnp.concatenate([gain_one[None], gain_two[None], gain_rows], axis=0)
+    if not quartered:
+        gain_one = jnp.sum(qkv_weight.astype(F32) * qkv_grad, axis=1)
+        gain_two = jnp.sum(ffn_in.astype(F32) * in_grad, axis=1)
+    gain_one, gain_two = gain_one.reshape(1, -1) / own_gains[:1], gain_two.reshape(1, -1) / own_gains[1:2]
+    gains_grad = jnp.concatenate([gain_one, gain_two, gain_rows], axis=0)
     unit = inputs[own] * inv[own]
     scaled = (d_own + from_others) * gains[0]
     input_grad = d_mixed + inv[own] * (scaled - unit * jnp.mean(unit * scaled, axis=-1, keepdims=True))
+    other_grads = other_grads.astype(F32)
     return (
         loss,
-        final.astype(BF)[None],
+        activations[None],
         input_grad[None],
         gains_grad,
         var_bias_grad,

time: 581 us -> 534 us (0.919)
  matrix products: 99.1 us -> 68.6 us
  other arithmetic: 91.5 us -> 64 us
  waiting for transfers between devices: 111 us -> 135 us
  local copies, waits for them, and re-layouts: 51.3 us -> 33.5 us
  Pallas kernels: 142 us -> 151 us
    ppermute x30 -> x29, waiting for transfers between devices: 85.5 us -> 44 us  [permuted(): lax.ppermute(shard, axis, [(i, i ^ flip) for i in range(lax.axis_size(axi...]
    all_to_all x3, waiting for transfers between devices: 7.79 us -> 39.2 us  [ctx_spread(): lax.all_to_all(jnp.broadcast_to(part[None], (size,) + part.shape), 'ctx',...]
    dot_general x7 -> x4, matrix products: 42.2 us -> 18.6 us  [dot_nt(): lax.dot_general(a, b, (((1,), (1,)), ((), ())), preferred_element_type=F32)]
    convert_element_type x11 -> x1, other arithmetic: 23.2 us -> 0.24 us  [per_device(): normed_two = rms_scale(mixed, gains[1]).astype(BF)]
    all_gather x1, waiting for transfers between devices: 0.02 us -> 20.1 us  [per_device(): whole = lax.all_gather(shard, 'fsdp', axis=0, tiled=True)]
    unnamed x113 -> x151, local copies, waits for them, and re-layouts: 19 us -> 6.91 us
    dot_general x1 -> x0, matrix products: 9.62 us -> none  [per_device(): final = mixed + jnp.dot(hidden, w_lower, preferred_element_type=F32)]
    ppermute x2, waiting for transfers between devices: 17.6 us -> 26.3 us  [the longest x1 16.1 us: returned_far(): return lax.ppermute(jnp.where(odd, after, before), 'ctx', [(1, 3), (2, 0)])]
  transfers between devices with their start and end apart: 44 -> 43, of which waited for: 11 -> 19; matrix products, arithmetic and copies ran while one was open for 35% -> 21% of each run, Pallas kernels for 25% -> 23%
where the time goes in v3:
time: 534 us; the launch traced here: 527 us
  Pallas kernels  151 us (28%)
  waiting for transfers between devices  135 us (25%)
  matrix products  68.6 us (13%)
  other arithmetic  64 us (12%)
  starting transfers between devices  52.8 us (10%)
  local copies, waits for them, and re-layouts  33.5 us (6%)
  between operations  21.6 us (4%)
    pallas_call x2, Pallas kernels, attention_backward(): pl.pallas_call(bwd_kernel, grid_spec=pltpu.PrefetchScalarGridSpec(num_sca...  72.3 us
    dot_general x12, matrix products, dot_tn(): lax.dot_general(a, b, (((0,), (0,)), ((), ())), preferred_element_type=F32)  46.7 us
    pallas_call x1, Pallas kernels, attention_forward(): pl.pallas_call(fwd_kernel, grid_spec=pltpu.PrefetchScalarGridSpec(num_sca...  44.6 us
    ppermute x29, waiting for transfers between devices, permuted(): lax.ppermute(shard, axis, [(i, i ^ flip) for i in range(lax.axis_size(axi...  44 us
    all_to_all x3, waiting for transfers between devices, ctx_spread(): lax.all_to_all(jnp.broadcast_to(part[None], (size,) + part.shape), 'ctx',...  39.2 us
    pallas_call x1, Pallas kernels, feed_forward(): pl.pallas_call(feed_forward_kernel, in_specs=[smem, smem, vmem, vmem] + [...  31.2 us
    ppermute x29, starting transfers between devices, permuted(): lax.ppermute(shard, axis, [(i, i ^ flip) for i in range(lax.axis_size(axi...  28.3 us
    all_gather x1, waiting for transfers between devices, per_device(): whole = lax.all_gather(shard, 'fsdp', axis=0, tiled=True)  20.1 us
  transfers between devices with their start and end apart: 43, of which 19 were waited for; matrix products, arithmetic and copies ran while one was open for 21% of the time, Pallas kernels for 23%

profile of v3, /device:TPU:0, one launch (start us, length us, event | category | flops | bytes accessed | tf_op | source)
XLA Modules:
  0.0 526.8 jit_solution(15550925722244160062)
XLA Ops:
  11.7 3.0 collective-permute-start
  21.9 20.1 %all-gather.4.cloned.1.call-done.p0 = bf16[1024,1024]{1,0:T(8,128)(2,1)} async-done(((bf16[128,1024]{1,0:T(8,128)(2,1)}), bf16[1024,1024]{1,0:T(8,128)(2,1)}) %all-gather.4.cloned.1.call-update) | async-done | bytes 2097168 | tf_op jit(solution)/shard_map/all_gather | solution.py:528
  42.0 2.3 constant_dynamic-slice_fusion.4
  44.3 4.4 collective-permute-start.3
  48.7 2.8 fusion.42
  57.4 3.3 all-to-all-start
  61.0 10.2 %collective-permute-done.3 = bf16[512,1024]{1,0:T(8,128)(2,1)} collective-permute-done((bf16[512,1024]{1,0:T(8,128)(2,1)S(1)}, bf16[512,1024]{1,0:T(8,128)(2,1)}, u32[]{:S(2)}, u32[]{:S(2)}) %collective-permute-start.3) | collective-permute-done | bytes 1048608 | tf_op jit(solution)/shard_map/ppermute | solution.py:544
  74.3 7.2 %multiply_convert_fusion.xn_ref = bf16[1536,1024]{1,0:T(8,128)(2,1)} fusion(f32[1024]{0:T(1024)S(1)} %bitcast.89, f32[1536]{0:T(1024)S(1)} %add_rsqrt_fusion, bf16[512,1024]{1,0:T(8,128)(2,1)S(1)} %get-tuple-element.217, bf16[512,1024]{1,0:T(8,128)(2,1)S(1)} %bitcast.73, bf16[512,1024]{1,0:T(8,128)(2,1)S(1)} %get-tuple-element.216), kind=kLoop, calls=%fused_computation.2 | loop fusion | flops 14155776 | bytes 6301696 | tf_op jit(solution)/shard_map/convert_element_type | solution.py:574
  81.5 11.6 %collective-permute-done.2.p3 = bf16[512,1024]{1,0:T(8,128)(2,1)} collective-permute-done((bf16[512,1024]{1,0:T(8,128)(2,1)}, bf16[512,1024]{1,0:T(8,128)(2,1)}, u32[]{:S(2)}, u32[]{:S(2)}) %collective-permute-start.2) | collective-permute-done | bytes 1048608 | tf_op jit(solution)/shard_map/ppermute | solution.py:423
  94.8 2.5 collective-permute-start.6
  105.0 5.2 collective-permute-done.6
  112.2 2.6 collective-permute-done.7
  120.0 44.6 %attention_forward.1 = (bf16[512,1024]{1,0:T(8,128)(2,1)}, bf16[1536,1024]{1,0:T(8,128)(2,1)}, bf16[1536,1024]{1,0:T(8,128)(2,1)}, bf16[512,1024]{1,0:T(8,128)(2...) custom-call(s32[2]{0:T(128)} %pad_add_fusion.place_ref, ...), custom_call_target="tpu_custom_call" | custom-call | flops 1000000 | bytes 10000 | tf_op jit(solution)/shard_map/attention_forward/pallas_call | solution.py:229
  164.6 7.3 %collective-permute-done.10.p3 = bf16[512,1408]{1,0:T(8,128)(2,1)} collective-permute-done((bf16[512,1408]{1,0:T(8,128)(2,1)S(1)}, bf16[512,1408]{1,0:T(8,128)(2,1)}, u32[]{:S(2)}, u32[]{:S(2)}) %collective-permute-start.10) | collective-permute-done | bytes 1441824 | tf_op jit(solution)/shard_map/ppermute | solution.py:423
  171.9 4.1 collective-permute-done.9.p1
  178.9 3.3 multiply_reduce_fusion.2
  183.8 31.2 %feed_forward.1 = (bf16[512,2816]{1,0:T(8,128)(2,1)}, bf16[512,5632]{1,0:T(8,128)(2,1)}, bf16[512,1024]{1,0:T(8,128)(2,1)}, bf16[512,1024]{1,0:T(8,128)(2,1)}, f...) custom-call(s32[2]{0:T(128)} %pad_add_fusion.place_ref, ...), custom_call_target="tpu_custom_call" | custom-call | flops 1000000 | bytes 10000 | tf_op jit(solution)/shard_map/feed_forward/pallas_call | solution.py:328
  215.1 8.3 %convolution_convert_fusion = bf16[512,5632]{1,0:T(8,128)(2,1)} fusion(bf16[512,5632]{1,0:T(8,128)(2,1)} %get-tuple-element.239, pred[]{:T(512)S(6)} %eq.181, bf16[512,128]{1,0:T(8,128)(2,1)S(1)} %get-tuple-element.346, bf16[512,128]{1,0:T(8,128)(2,1)S(1)} %get-tuple-element.347, bf16[512,128]{1,0:T(8,128)(2,1)S(1)} %get-tuple-element.348, ...), kind=kOutput, calls=%fused_computation.1 | convolution fusion | flops 2960130048 | bytes 12582913 | tf_op jit(solution)/shard_map/dot_general | solution.py:23
  223.5 5.1 convolution_convert_fusion.1
  233.5 2.6 convolution_convert_fusion.2
  236.2 2.8 collective-permute-done.15
  239.0 7.5 %add_convert_fusion = bf16[512,5632]{1,0:T(8,128)(2,1)S(1)} fusion(bf16[512,5632]{1,0:T(8,128)(2,1)} %collective-permute-done.15, bf16[512,5632]{1,0:T(8,128)(2,1)} %get-tuple-element.239, pred[]{:T(512)S(6)} %eq.181, bf16[512,128]{1,0:T(8,128)(2,1)S(1)} %copy-done.29, bf16[512,128]{1,0:T(8,128)(2,1)S(1)} %copy-done.31, bf16[512,128]{1,0:T(8,128)(2,1)S(1)} %copy-done.33, ...), kind=kOutput, calls=%fused_computation | convolution fusion | flops 2965897216 | bytes 18350080 | tf_op jit(solution)/shard_map/dot_general | solution.py:23
  250.0 3.7 collective-permute-start.16
  257.4 36.7 %attention_backward.2 = (bf16[512,512]{1,0:T(8,128)(2,1)}, bf16[1536,1024]{1,0:T(8,128)(2,1)}, f32[4,1,256]{2,1,0:T(1,128)}, f32[4,1,256]{2,1,0:T(1,128)}, f32[4,8,128]{2,1,0:T(8,128)}) custom-call(s32[2]{0:T(128)} %pad_add_fusion.place_ref, bf16[512,1024]{1,0:T(8,128)(2,1)} %get-tuple-element.222.q_ref, bf16[1536,1024]{1,0:T(8,128)(2,1)} %get-tuple-element.223.k_ref, ...), custom_call_target="tpu_custom_call" | custom-call | flops 1000000 | bytes 10000 | tf_op jit(solution)/shard_map/attention_backward/pallas_call | solution.py:347
  299.1 2.4 convolution_convert_fusion.6
  301.5 5.0 convolution_convert_fusion.4
  316.5 35.6 %attention_backward.3 = (bf16[512,512]{1,0:T(8,128)(2,1)}, bf16[1536,1024]{1,0:T(8,128)(2,1)}, f32[4,1,256]{2,1,0:T(1,128)}, f32[4,1,256]{2,1,0:T(1,128)}, f32[4,8,128]{2,1,0:T(8,128)}) custom-call(s32[2]{0:T(128)} %pad_add_fusion.place_ref, bf16[512,1024]{1,0:T(8,128)(2,1)} %get-tuple-element.222.q_ref, bf16[1536,1024]{1,0:T(8,128)(2,1)} %get-tuple-element.223.k_ref, ...), custom_call_target="tpu_custom_call" | custom-call | flops 1000000 | bytes 10000 | tf_op jit(solution)/shard_map/attention_backward/pallas_call | solution.py:347
  355.5 4.1 add_convert_fusion.1
  359.6 6.2 %fusion.3 = f32[1536,1024]{1,0:T(8,128)S(1)} fusion(bf16[1536,1024]{1,0:T(8,128)(2,1)} %get-tuple-element.294, bf16[1024,2048]{1,0:T(8,128)(2,1)} %get-tuple-element.258), kind=kOutput, calls=%fused_computation.17 | convolution fusion | flops 3221225472 | bytes 11534336 | tf_op jit(solution)/shard_map/dot_general | solution.py:22
  365.9 5.7 %fusion.78 = (bf16[1536,1024]{1,0:T(8,128)(2,1)S(1)}, f32[1536,1024]{1,0:T(8,128)}) fusion(f32[1536,1024]{1,0:T(8,128)S(1)} %fusion.3, bf16[1536,1024]{1,0:T(8,128)(2,1)S(1)} %copy-done.65, bf16[1024,2048]{1,0:T(8,128)(2,1)S(1)} %copy-done.63), kind=kOutput, calls=%fused_computation.212 | convolution fusion | flops 3224371200 | bytes 20971520 | tf_op jit(solution)/shard_map/dot_general | solution.py:22
  373.7 3.5 all-to-all-start.1
  377.3 2.5 convolution_convert_fusion.5
  379.7 5.1 convolution_convert_fusion.3
  384.9 4.5 all-to-all-done.1
  397.2 3.0 add_convert_fusion.3
  402.3 16.1 %collective-permute-done.26 = bf16[512,1024]{1,0:T(8,128)(2,1)} collective-permute-done((bf16[512,1024]{1,0:T(8,128)(2,1)}, bf16[512,1024]{1,0:T(8,128)(2,1)}, u32[]{:S(2)}, u32[]{:S(2)}) %collective-permute-start.26) | collective-permute-done | bytes 1048608 | tf_op jit(solution)/shard_map/ppermute | solution.py:433
  423.3 3.5 all-to-all-start.2
  429.3 18.5 %all-to-all-done.2 = bf16[4,120,1024]{2,1,0:T(8,128)(2,1)S(1)} async-done(((bf16[4,120,1024]{2,1,0:T(8,128)(2,1)}), bf16[4,120,1024]{2,1,0:T(8,128)(2,1)S(1)}, u32[]{:S(2)}, u32[]{:S(2)}) %all-to-all-start.2) | async-done | bytes 983072 | tf_op jit(solution)/shard_map/all_to_all | solution.py:443
  451.0 2.2 broadcast_in_dim.221
  453.2 3.9 all-to-all-start.3
  457.0 2.8 add_convert_fusion.2
  462.5 13.7 %all-to-all-done.3.refs_0_ = bf16[4,128,1408]{2,1,0:T(8,128)(2,1)S(1)} async-done(((bf16[4,128,1408]{2,1,0:T(8,128)(2,1)}), bf16[4,128,1408]{2,1,0:T(8,128)(2,1)S(1)}, u32[]{:S(2)}, u32[]{:S(2)}) %all-to-all-start.3) | async-done | bytes 1441824 | tf_op jit(solution)/shard_map/all_to_all | solution.py:443
  478.2 3.5 all-to-all-start.4
  481.8 5.2 maximum_convert_fusion
  493.2 5.6 %collective-permute-done.29 = bf16[512,1024]{1,0:T(8,128)(2,1)} collective-permute-done((bf16[512,1024]{1,0:T(8,128)(2,1)}, bf16[512,1024]{1,0:T(8,128)(2,1)}, u32[]{:S(2)}, u32[]{:S(2)}) %collective-permute-start.29) | collective-permute-done | bytes 1048608 | tf_op jit(solution)/shard_map/ppermute | solution.py:423
  498.8 7.0 %all-to-all-done.4.refs_0_ = bf16[4,128,896]{2,1,0:T(8,128)(2,1)S(1)} async-done(((bf16[4,128,896]{2,1,0:T(8,128)(2,1)}), bf16[4,128,896]{2,1,0:T(8,128)(2,1)S(1)}, u32[]{:S(2)}, u32[]{:S(2)}) %all-to-all-start.4) | async-done | bytes 917536 | tf_op jit(solution)/shard_map/all_to_all | solution.py:443
  507.8 4.7 multiply_reduce_fusion.1
  514.4 4.0 add_bitcast_fusion
  (345 shorter events, 104.5 us)
Async XLA Ops:
  7.2 34.8 %all-gather.4.cloned.1.call-start = ((), (), s32[]{:S(2)}) async-start(), calls=%async_computation.9 | async-start | bytes 2359296 | tf_op jit(solution)/shard_map/all_gather | solution.py:528
  9.1 84.0 %all-gather.6.cloned.1.call-start = ((), (), s32[]{:S(2)}) async-start(), calls=%async_computation.10 | async-start | bytes 3244032 | tf_op jit(solution)/shard_map/all_gather | solution.py:529
  10.9 172.7 %all-gather.8.cloned.1.call-start = ((), (), s32[]{:S(2)}) async-start(), calls=%async_computation.11 | async-start | bytes 6488064 | tf_op jit(solution)/shard_map/all_gather | solution.py:535
  11.7 32.6 %collective-permute-start = (bf16[512,1024]{1,0:T(8,128)(2,1)S(1)}, bf16[512,1024]{1,0:T(8,128)(2,1)S(1)}, u32[]{:S(2)}, u32[]{:S(2)}) collective-permute-start(bf16[512,1024]{1,0:T(8,128)(2,1)S(1)} %bitcast.71), channel_id=1, source_target_pairs={{0,8},{8,0},{16,24},{24,16},{1,9},{9,1},{17,25},{25,17},{2,10},{10... | collective-permute-start | bytes 3145736 | tf_op jit(solution)/shard_map/ppermute | solution.py:423
  44.3 26.9 %collective-permute-start.3 = (bf16[512,1024]{1,0:T(8,128)(2,1)S(1)}, bf16[512,1024]{1,0:T(8,128)(2,1)}, u32[]{:S(2)}, u32[]{:S(2)}) collective-permute-start(bf16[512,1024]{1,0:T(8,128)(2,1)S(1)} %collective-permute-done), channel_id=1, source_target_pairs={{0,16},{24,8},{1,17},{25,9},{2,18},{26,10},{3,19},{27,11},{4,20},{... | collective-permute-start | bytes 3145736 | tf_op jit(solution)/shard_map/ppermute | solution.py:544
  54.7 26.8 %collective-permute-start.1 = (bf16[512,1024]{1,0:T(8,128)(2,1)}, bf16[512,1024]{1,0:T(8,128)(2,1)}, u32[]{:S(2)}, u32[]{:S(2)}) collective-permute-start(bf16[512,1024]{1,0:T(8,128)(2,1)} %constant_dynamic-slice_fusion.4), channel_id=1, source_target_pairs={{0,8},{8,0},{16,24},{24,16},{1,9},{9,1},{17,25},{25,17},{2,10},{10... | collective-permute-start | bytes 3145736 | tf_op jit(solution)/shard_map/ppermute | solution.py:423
  54.7 38.4 %collective-permute-start.2 = (bf16[512,1024]{1,0:T(8,128)(2,1)}, bf16[512,1024]{1,0:T(8,128)(2,1)}, u32[]{:S(2)}, u32[]{:S(2)}) collective-permute-start(bf16[512,1024]{1,0:T(8,128)(2,1)} %constant_dynamic-slice_fusion.4), channel_id=1, source_target_pairs={{0,16},{8,24},{16,0},{24,8},{1,17},{9,25},{17,1},{25,9},{2,18},{10... | collective-permute-start | bytes 3145736 | tf_op jit(solution)/shard_map/ppermute | solution.py:423
  57.4 15.5 %all-to-all-start = ((bf16[8,16,128]{2,1,0:T(8,128)(2,1)}), bf16[8,16,128]{2,1,0:T(8,128)(2,1)S(1)}, u32[]{:S(2)}, u32[]{:S(2)}) async-start(bf16[8,16,128]{2,1,0:T(8,128)(2,1)} %broadcast_in_dim.196), calls=%async_computation | async-start | bytes 65536 | tf_op jit(solution)/shard_map/all_to_all | solution.py:553
  60.8 237.6 %reduce-scatter.5.cloned.1.call-start = ((), (), s32[]{:S(2)}) async-start(), calls=%async_computation.12 | async-start | bytes 6488064 | tf_op jit(solution)/shard_map/reduce_scatter | solution.py:605
  93.1 21.7 %collective-permute-start.4 = (bf16[512,1024]{1,0:T(8,128)(2,1)}, bf16[512,1024]{1,0:T(8,128)(2,1)S(1)}, u32[]{:S(2)}, u32[]{:S(2)}) collective-permute-start(bf16[512,1024]{1,0:T(8,128)(2,1)} %collective-permute-done.1.p1), channel_id=1, source_target_pairs={{0,1},{1,0},{2,3},{3,2},{4,5},{5,4},{6,7},{7,6},{8,9},{9,8},{10,11... | collective-permute-start | bytes 3145736 | tf_op jit(solution)/shard_map/ppermute | solution.py:423
  94.8 15.3 %collective-permute-start.6 = (bf16[256,1024]{1,0:T(8,128)(2,1)S(1)}, bf16[256,1024]{1,0:T(8,128)(2,1)S(1)}, u32[]{:S(2)}, u32[]{:S(2)}) collective-permute-start(bf16[256,1024]{1,0:T(8,128)(2,1)S(1)} %slice.426), channel_id=1, source_target_pairs={{0,16},{8,24},{16,0},{24,8},{1,17},{9,25},{17,1},{25,9},{2,18},{10... | collective-permute-start | bytes 1572872 | tf_op jit(solution)/shard_map/ppermute | solution.py:423
  99.9 14.8 %collective-permute-start.7 = (bf16[256,1024]{1,0:T(8,128)(2,1)S(1)}, bf16[256,1024]{1,0:T(8,128)(2,1)S(1)}, u32[]{:S(2)}, u32[]{:S(2)}) collective-permute-start(bf16[256,1024]{1,0:T(8,128)(2,1)S(1)} %slice.427), channel_id=1, source_target_pairs={{0,8},{8,0},{16,24},{24,16},{1,9},{9,1},{17,25},{25,17},{2,10},{10... | collective-permute-start | bytes 1572872 | tf_op jit(solution)/shard_map/ppermute | solution.py:423
  101.5 70.4 %collective-permute-start.10 = (bf16[512,1408]{1,0:T(8,128)(2,1)S(1)}, bf16[512,1408]{1,0:T(8,128)(2,1)}, u32[]{:S(2)}, u32[]{:S(2)}) collective-permute-start(bf16[512,1408]{1,0:T(8,128)(2,1)S(1)} %constant_dynamic-slice_fusion.2), channel_id=1, source_target_pairs={{0,16},{8,24},{16,0},{24,8},{1,17},{9,25},{17,1},{25,9},{2,18},{10... | collective-permute-start | bytes 4325384 | tf_op jit(solution)/shard_map/ppermute | solution.py:423
  103.5 68.4 %collective-permute-start.11 = (bf16[512,1408]{1,0:T(8,128)(2,1)S(1)}, bf16[512,1408]{1,0:T(8,128)(2,1)}, u32[]{:S(2)}, u32[]{:S(2)}) collective-permute-start(bf16[512,1408]{1,0:T(8,128)(2,1)S(1)} %constant_dynamic-slice_fusion.2), channel_id=1, source_target_pairs={{0,24},{8,16},{16,8},{24,0},{1,25},{9,17},{17,9},{25,1},{2,26},{10... | collective-permute-start | bytes 4325384 | tf_op jit(solution)/shard_map/ppermute | solution.py:423
  110.2 65.8 %collective-permute-start.9 = (bf16[512,1408]{1,0:T(8,128)(2,1)S(1)}, bf16[512,1408]{1,0:T(8,128)(2,1)}, u32[]{:S(2)}, u32[]{:S(2)}) collective-permute-start(bf16[512,1408]{1,0:T(8,128)(2,1)S(1)} %constant_dynamic-slice_fusion.2), channel_id=1, source_target_pairs={{0,8},{8,0},{16,24},{24,16},{1,9},{9,1},{17,25},{25,17},{2,10},{10... | collective-permute-start | bytes 4325384 | tf_op jit(solution)/shard_map/ppermute | solution.py:423
  114.7 2.9 collective-permute-start.5
  114.8 4.2 collective-permute-start.8
  175.9 7.6 %collective-permute-start.12 = (bf16[512,1408]{1,0:T(8,128)(2,1)}, bf16[512,1408]{1,0:T(8,128)(2,1)}, u32[]{:S(2)}, u32[]{:S(2)}) collective-permute-start(bf16[512,1408]{1,0:T(8,128)(2,1)} %collective-permute-done.9.p1), channel_id=1, source_target_pairs={{0,1},{1,0},{2,3},{3,2},{4,5},{5,4},{6,7},{7,6},{8,9},{9,8},{10,11... | collective-permute-start | bytes 4325384 | tf_op jit(solution)/shard_map/ppermute | solution.py:423
  175.9 7.6 %collective-permute-start.13 = (bf16[512,1408]{1,0:T(8,128)(2,1)}, bf16[512,1408]{1,0:T(8,128)(2,1)}, u32[]{:S(2)}, u32[]{:S(2)}) collective-permute-start(bf16[512,1408]{1,0:T(8,128)(2,1)} %collective-permute-done.10.p3), channel_id=1, source_target_pairs={{0,1},{1,0},{2,3},{3,2},{4,5},{5,4},{6,7},{7,6},{8,9},{9,8},{10,11... | collective-permute-start | bytes 4325384 | tf_op jit(solution)/shard_map/ppermute | solution.py:423
  176.4 7.2 %collective-permute-start.14 = (bf16[512,1408]{1,0:T(8,128)(2,1)}, bf16[512,1408]{1,0:T(8,128)(2,1)}, u32[]{:S(2)}, u32[]{:S(2)}) collective-permute-start(bf16[512,1408]{1,0:T(8,128)(2,1)} %collective-permute-done.11.p5), channel_id=1, source_target_pairs={{0,1},{1,0},{2,3},{3,2},{4,5},{5,4},{6,7},{7,6},{8,9},{9,8},{10,11... | collective-permute-start | bytes 4325384 | tf_op jit(solution)/shard_map/ppermute | solution.py:423
  228.6 126.9 %reduce-scatter.7.cloned.1.call-start = ((), (), s32[]{:S(2)}) async-start(), calls=%async_computation.13 | async-start | bytes 2359296 | tf_op jit(solution)/shard_map/reduce_scatter | solution.py:620
  229.0 10.0 %collective-permute-start.15 = (bf16[512,5632]{1,0:T(8,128)(2,1)}, bf16[512,5632]{1,0:T(8,128)(2,1)}, u32[]{:S(2)}, u32[]{:S(2)}) collective-permute-start(bf16[512,5632]{1,0:T(8,128)(2,1)} %convolution_convert_fusion), channel_id=1, source_target_pairs={{0,1},{1,0},{2,3},{3,2},{4,5},{5,4},{6,7},{7,6},{8,9},{9,8},{10,11... | collective-permute-start | bytes 17301512 | tf_op jit(solution)/shard_map/ppermute | solution.py:423
  250.0 44.3 %collective-permute-start.16 = (bf16[256,1408]{1,0:T(8,128)(2,1)}, bf16[256,1408]{1,0:T(8,128)(2,1)}, u32[]{:S(2)}, u32[]{:S(2)}) collective-permute-start(bf16[256,1408]{1,0:T(8,128)(2,1)} %get-tuple-element.340), channel_id=1, source_target_pairs={{0,8},{8,0},{16,24},{24,16},{1,9},{9,1},{17,25},{25,17},{2,10},{10... | collective-permute-start | bytes 2162696 | tf_op jit(solution)/shard_map/ppermute | solution.py:423
  253.6 40.7 %collective-permute-start.17 = (bf16[256,1408]{1,0:T(8,128)(2,1)}, bf16[256,1408]{1,0:T(8,128)(2,1)}, u32[]{:S(2)}, u32[]{:S(2)}) collective-permute-start(bf16[256,1408]{1,0:T(8,128)(2,1)} %get-tuple-element.339), channel_id=1, source_target_pairs={{0,16},{8,24},{16,0},{24,8},{1,17},{9,25},{17,1},{25,9},{2,18},{10... | collective-permute-start | bytes 2162696 | tf_op jit(solution)/shard_map/ppermute | solution.py:423
  257.4 54.3 %copy-start.23 = (bf16[1536,512]{1,0:T(8,128)(2,1)}, bf16[1536,512]{1,0:T(8,128)(2,1)S(1)}, u32[]{:S(2)}) copy-start(bf16[1536,512]{1,0:T(8,128)(2,1)S(1)} %get-tuple-element.328) | copy-start | bytes 4718596
  306.5 5.2 collective-permute-start.19
  306.5 3.5 collective-permute-start.18
  308.4 47.1 %collective-permute-start.22 = (bf16[512,1408]{1,0:T(8,128)(2,1)}, bf16[512,1408]{1,0:T(8,128)(2,1)}, u32[]{:S(2)}, u32[]{:S(2)}) collective-permute-start(bf16[512,1408]{1,0:T(8,128)(2,1)} %pad_maximum_fusion.2), channel_id=1, source_target_pairs={{0,8},{8,0},{16,24},{24,16},{1,9},{9,1},{17,25},{25,17},{2,10},{10... | collective-permute-start | bytes 4325384 | tf_op jit(solution)/shard_map/ppermute | solution.py:423
  308.5 47.0 %collective-permute-start.23 = (bf16[512,1408]{1,0:T(8,128)(2,1)}, bf16[512,1408]{1,0:T(8,128)(2,1)}, u32[]{:S(2)}, u32[]{:S(2)}) collective-permute-start(bf16[512,1408]{1,0:T(8,128)(2,1)} %pad_maximum_fusion.3), channel_id=1, source_target_pairs={{0,16},{8,24},{16,0},{24,8},{1,17},{9,25},{17,1},{25,9},{2,18},{10... | collective-permute-start | bytes 4325384 | tf_op jit(solution)/shard_map/ppermute | solution.py:423
  313.7 39.2 %copy-start.13 = (bf16[512,768]{1,0:T(8,128)(2,1)}, bf16[512,768]{1,0:T(8,128)(2,1)S(1)}, u32[]{:S(2)}) copy-start(bf16[512,768]{1,0:T(8,128)(2,1)S(1)} %pad_maximum_fusion.9) | copy-start | bytes 2359300
  313.8 41.6 %collective-permute-start.20 = (bf16[256,768]{1,0:T(8,128)(2,1)S(1)}, bf16[256,768]{1,0:T(8,128)(2,1)S(1)}, u32[]{:S(2)}, u32[]{:S(2)}) collective-permute-start(bf16[256,768]{1,0:T(8,128)(2,1)S(1)} %get-tuple-element.354), channel_id=1, source_target_pairs={{0,8},{8,0},{16,24},{24,16},{1,9},{9,1},{17,25},{25,17},{2,10},{10... | collective-permute-start | bytes 1179656 | tf_op jit(solution)/shard_map/ppermute | solution.py:423
  314.5 37.5 %copy-start.57 = (f32[4,1,256]{2,1,0:T(1,128)S(1)}, f32[4,1,256]{2,1,0:T(1,128)}, u32[]{:S(2)}) copy-start(f32[4,1,256]{2,1,0:T(1,128)} %get-tuple-element.283) | copy-start | bytes 12292
  314.5 37.5 %copy-start.58 = (f32[4,1,256]{2,1,0:T(1,128)S(1)}, f32[4,1,256]{2,1,0:T(1,128)}, u32[]{:S(2)}) copy-start(f32[4,1,256]{2,1,0:T(1,128)} %get-tuple-element.285) | copy-start | bytes 12292
  314.6 38.3 %copy-start.59 = (f32[4,8,128]{2,1,0:T(8,128)S(1)}, f32[4,8,128]{2,1,0:T(8,128)}, u32[]{:S(2)}) copy-start(f32[4,8,128]{2,1,0:T(8,128)} %get-tuple-element.287) | copy-start | bytes 49156
  314.6 40.9 %collective-permute-start.21 = (bf16[256,768]{1,0:T(8,128)(2,1)S(1)}, bf16[256,768]{1,0:T(8,128)(2,1)S(1)}, u32[]{:S(2)}, u32[]{:S(2)}) collective-permute-start(bf16[256,768]{1,0:T(8,128)(2,1)S(1)} %get-tuple-element.353), channel_id=1, source_target_pairs={{0,16},{8,24},{16,0},{24,8},{1,17},{9,25},{17,1},{25,9},{2,18},{10... | collective-permute-start | bytes 1179656 | tf_op jit(solution)/shard_map/ppermute | solution.py:423
  373.7 15.7 %all-to-all-start.1 = ((bf16[4,120,1024]{2,1,0:T(8,128)(2,1)}), bf16[4,120,1024]{2,1,0:T(8,128)(2,1)S(1)}, u32[]{:S(2)}, u32[]{:S(2)}) async-start(bf16[4,120,1024]{2,1,0:T(8,128)(2,1)} %bitcast.76), calls=%async_computation.3 | async-start | bytes 1966080 | tf_op jit(solution)/shard_map/all_to_all | solution.py:484
  377.2 70.6 %reduce-scatter.9.cloned.1.call-start = ((), (), s32[]{:S(2)}) async-start(), calls=%async_computation.14 | async-start | bytes 1802240 | tf_op jit(solution)/shard_map/reduce_scatter | solution.py:479
  389.4 7.8 %collective-permute-start.25 = (bf16[512,1024]{1,0:T(8,128)(2,1)}, bf16[512,1024]{1,0:T(8,128)(2,1)}, u32[]{:S(2)}, u32[]{:S(2)}) collective-permute-start(bf16[512,1024]{1,0:T(8,128)(2,1)} %convolution_convert_fusion.3), channel_id=1, source_target_pairs={{0,1},{1,0},{2,3},{3,2},{4,5},{5,4},{6,7},{7,6},{8,9},{9,8},{10,11... | collective-permute-start | bytes 3145736 | tf_op jit(solution)/shard_map/ppermute | solution.py:423
  389.4 5.4 %collective-permute-start.24 = (bf16[512,512]{1,0:T(8,128)(2,1)}, bf16[512,512]{1,0:T(8,128)(2,1)}, u32[]{:S(2)}, u32[]{:S(2)}) collective-permute-start(bf16[512,512]{1,0:T(8,128)(2,1)} %convolution_convert_fusion.5), channel_id=1, source_target_pairs={{0,1},{1,0},{2,3},{3,2},{4,5},{5,4},{6,7},{7,6},{8,9},{9,8},{10,11... | collective-permute-start | bytes 1572872 | tf_op jit(solution)/shard_map/ppermute | solution.py:423
  391.0 27.4 %collective-permute-start.26 = (bf16[512,1024]{1,0:T(8,128)(2,1)}, bf16[512,1024]{1,0:T(8,128)(2,1)}, u32[]{:S(2)}, u32[]{:S(2)}) collective-permute-start(bf16[512,1024]{1,0:T(8,128)(2,1)} %broadcast_select_fusion.2), channel_id=1, source_target_pairs={{8,24},{16,0},{9,25},{17,1},{10,26},{18,2},{11,27},{19,3},{12,28},... | collective-permute-start | bytes 3145736 | tf_op jit(solution)/shard_map/ppermute | solution.py:433
  418.4 29.4 %collective-permute-start.27 = (bf16[512,768]{1,0:T(8,128)(2,1)}, bf16[512,768]{1,0:T(8,128)(2,1)}, u32[]{:S(2)}, u32[]{:S(2)}) collective-permute-start(bf16[512,768]{1,0:T(8,128)(2,1)} %pad_maximum_fusion.10), channel_id=1, source_target_pairs={{0,8},{8,0},{16,24},{24,16},{1,9},{9,1},{17,25},{25,17},{2,10},{10... | collective-permute-start | bytes 2359304 | tf_op jit(solution)/shard_map/ppermute | solution.py:423
  418.4 29.4 %collective-permute-start.28 = (bf16[512,768]{1,0:T(8,128)(2,1)}, bf16[512,768]{1,0:T(8,128)(2,1)}, u32[]{:S(2)}, u32[]{:S(2)}) collective-permute-start(bf16[512,768]{1,0:T(8,128)(2,1)} %fusion.15), channel_id=1, source_target_pairs={{0,16},{8,24},{16,0},{24,8},{1,17},{9,25},{17,1},{25,9},{2,18},{10... | collective-permute-start | bytes 2359304 | tf_op jit(solution)/shard_map/ppermute | solution.py:423
  423.3 24.4 %all-to-all-start.2 = ((bf16[4,120,1024]{2,1,0:T(8,128)(2,1)}), bf16[4,120,1024]{2,1,0:T(8,128)(2,1)S(1)}, u32[]{:S(2)}, u32[]{:S(2)}) async-start(bf16[4,120,1024]{2,1,0:T(8,128)(2,1)} %broadcast_in_dim.220), calls=%async_computation.5 | async-start | bytes 1966080 | tf_op jit(solution)/shard_map/all_to_all | solution.py:443
  426.9 49.4 %reduce-scatter.11.cloned.1.call-start = ((), (), s32[]{:S(2)}) async-start(), calls=%async_computation.15 | async-start | bytes 1146880 | tf_op jit(solution)/shard_map/reduce_scatter | solution.py:479
  426.9 1.4 collective-permute-start.30
  453.2 23.1 %all-to-all-start.3 = ((bf16[4,128,1408]{2,1,0:T(8,128)(2,1)}), bf16[4,128,1408]{2,1,0:T(8,128)(2,1)S(1)}, u32[]{:S(2)}, u32[]{:S(2)}) async-start(bf16[4,128,1408]{2,1,0:T(8,128)(2,1)} %broadcast_in_dim.221), calls=%async_computation.7 | async-start | bytes 2883584 | tf_op jit(solution)/shard_map/all_to_all | solution.py:443
  459.9 39.0 %collective-permute-start.29 = (bf16[512,1024]{1,0:T(8,128)(2,1)}, bf16[512,1024]{1,0:T(8,128)(2,1)}, u32[]{:S(2)}, u32[]{:S(2)}) collective-permute-start(bf16[512,1024]{1,0:T(8,128)(2,1)} %add_convert_fusion.2), channel_id=1, source_target_pairs={{0,8},{8,0},{16,24},{24,16},{1,9},{9,1},{17,25},{25,17},{2,10},{10... | collective-permute-start | bytes 3145736 | tf_op jit(solution)/shard_map/ppermute | solution.py:423
  478.2 27.6 %all-to-all-start.4 = ((bf16[4,128,896]{2,1,0:T(8,128)(2,1)}), bf16[4,128,896]{2,1,0:T(8,128)(2,1)S(1)}, u32[]{:S(2)}, u32[]{:S(2)}) async-start(bf16[4,128,896]{2,1,0:T(8,128)(2,1)} %broadcast_in_dim.222), calls=%async_computation.8 | async-start | bytes 1835008 | tf_op jit(solution)/shard_map/all_to_all | solution.py:443
  (71 other events, 717.5 us)
Sparse Core Ops, SparseCore 0:
  10.2 31.7 all-gather.3
  44.2 36.3 all-gather.5
  82.3 59.2 all-gather.7
  228.7 66.9 reduce-scatter.4
  298.4 34.0 reduce-scatter.6
  392.6 33.8 reduce-scatter.8
  451.1 23.7 reduce-scatter.10

commit v4 on v3

--- a/solution.py
+++ b/solution.py
@@ -540,7 +540,7 @@
     if quartered:
         beside = permuted(tokens[0], "ctx", 1)
         mine = halves_of(whole, core)
-        mine, small, beside = tied(mine, small, beside)
+        mine, small = tied(mine, small)
         across = lax.ppermute(beside, "ctx", [(0, 2), (3, 1)])
         odd = me % 2 == 1
         before, behind = jnp.where(odd, beside, across), jnp.where(odd, across, beside)
@@ -660,21 +660,19 @@
     d_ext = dot_nt(d_kv1, w_kv[:, : 2 * 512]) + dot_nt(d_kv2, w_kv[:, 2 * 512 :])
     to_before, to_behind = d_ext[:HALF].astype(BF), d_ext[HALF + rows :].astype(BF)
     if quartered:
-        to_before, to_behind, d_q2, d_kv2 = tied(to_before, to_behind, d_q2, d_kv2)
+        to_before, to_behind, d_q2, d_kv2, other_grads = tied(to_before, to_behind, d_q2, d_kv2, other_grads)
         far = returned_far(to_before, to_behind)
         theirs = [dot_tn(other_normed[own], d_q2).astype(BF), dot_tn(other_normed, d_kv2).astype(BF), other_extra]
-        theirs, d_q2, d_kv2, other_grads = tied(theirs, d_q2, d_kv2, other_grads)
-        other_grads = ctx_joined(other_grads)
+        theirs, d_q2, d_kv2, far, in_part = tied(theirs, d_q2, d_kv2, far, in_part)
         swapped = [permuted(t, "fsdp", 1) for t in theirs]
         second_q = (dot_tn(own_normed[own], d_q2) + swapped[0].astype(F32)).astype(BF)
         second_kv = (dot_tn(own_normed, d_kv2) + swapped[1].astype(F32)).astype(BF)
         two = jnp.concatenate([second_q[:, :256], second_kv[:, :512]], axis=1)
         one = joined(one[:cut], added(one[cut:], last_up))
         two = joined(added(two[:cut], last_near), two[cut:])
-        one, two, far = tied(one, two, far)
         near, up = permuted(one, "ctx", 1), permuted(two, "ctx", 2)
-        in_part, other_grads, far = tied(in_part, other_grads, far)
-        near, up, in_part, far = tied(near, up, in_part, far)
+        other_grads = ctx_joined(other_grads)
+        near, up, in_part, far, other_grads = tied(near, up, in_part, far, other_grads)
         from_others = returned_near(to_before, to_behind, far)
         in_spread = ctx_spread(in_part)
         qkv_total = added(jnp.concatenate([second_q[:, 256:], second_kv[:, 512:]], axis=1), near, up)

time: 534 us -> 525 us (0.983)
    ppermute x29, waiting for transfers between devices: 44 us -> 65.2 us  [permuted(): lax.ppermute(shard, axis, [(i, i ^ flip) for i in range(lax.axis_size(axi...]
    all_gather x1, waiting for transfers between devices: 20.1 us -> 0.01 us  [per_device(): whole = lax.all_gather(shard, 'fsdp', axis=0, tiled=True)]
  transfers between devices with their start and end apart: 43 -> 43, of which waited for: 19 -> 21; matrix products, arithmetic and copies ran while one was open for 21% -> 24% of each run, Pallas kernels for 23% -> 23%
where the time goes in v4:
time: 525 us; the launch traced here: 519 us
  Pallas kernels  151 us (29%)
  waiting for transfers between devices  131 us (25%)
  other arithmetic  64.9 us (12%)
  matrix products  63.6 us (12%)
  starting transfers between devices  54 us (10%)
  local copies, waits for them, and re-layouts  32.3 us (6%)
  between operations  21.6 us (4%)
    pallas_call x2, Pallas kernels, attention_backward(): pl.pallas_call(bwd_kernel, grid_spec=pltpu.PrefetchScalarGridSpec(num_sca...  72.2 us
    ppermute x29, waiting for transfers between devices, permuted(): lax.ppermute(shard, axis, [(i, i ^ flip) for i in range(lax.axis_size(axi...  65.2 us
    pallas_call x1, Pallas kernels, attention_forward(): pl.pallas_call(fwd_kernel, grid_spec=pltpu.PrefetchScalarGridSpec(num_sca...  44.5 us
    dot_general x12, matrix products, dot_tn(): lax.dot_general(a, b, (((0,), (0,)), ((), ())), preferred_element_type=F32)  41.6 us
    all_to_all x3, waiting for transfers between devices, ctx_spread(): lax.all_to_all(jnp.broadcast_to(part[None], (size,) + part.shape), 'ctx',...  37.1 us
    pallas_call x1, Pallas kernels, feed_forward(): pl.pallas_call(feed_forward_kernel, in_specs=[smem, smem, vmem, vmem] + [...  31.2 us
    ppermute x29, starting transfers between devices, permuted(): lax.ppermute(shard, axis, [(i, i ^ flip) for i in range(lax.axis_size(axi...  27.4 us
    ppermute x1, waiting for transfers between devices, returned_far(): return lax.ppermute(jnp.where(odd, after, before), 'ctx', [(1, 3), (2, 0)])  19.6 us
  transfers between devices with their start and end apart: 43, of which 21 were waited for; matrix products, arithmetic and copies ran while one was open for 24% of the time, Pallas kernels for 23%

profile of v4, /device:TPU:0, one launch (start us, length us, event | category | flops | bytes accessed | tf_op | source)
XLA Modules:
  0.0 518.6 jit_solution(442421199301087173)
XLA Ops:
  11.7 3.0 collective-permute-start.2
  21.9 15.9 %collective-permute-done.2 = bf16[512,1024]{1,0:T(8,128)(2,1)S(1)} collective-permute-done((bf16[512,1024]{1,0:T(8,128)(2,1)S(1)}, bf16[512,1024]{1,0:T(8,128)(2,1)S(1)}, u32[]{:S(2)}, u32[]{:S(2)}) %collective-permute-start.2) | collective-permute-done | bytes 1048608 | tf_op jit(solution)/shard_map/ppermute | solution.py:423
  37.8 4.6 collective-permute-start.3
  42.5 2.8 fusion.40
  48.5 2.3 constant_dynamic-slice_fusion.4
  51.4 4.9 all-to-all-start
  56.5 6.6 %collective-permute-done.3 = bf16[512,1024]{1,0:T(8,128)(2,1)} collective-permute-done((bf16[512,1024]{1,0:T(8,128)(2,1)S(1)}, bf16[512,1024]{1,0:T(8,128)(2,1)}, u32[]{:S(2)}, u32[]{:S(2)}) %collective-permute-start.3) | collective-permute-done | bytes 1048608 | tf_op jit(solution)/shard_map/ppermute | solution.py:544
  64.8 2.7 collective-permute-start
  69.0 7.2 %multiply_convert_fusion.xn_ref = bf16[1536,1024]{1,0:T(8,128)(2,1)} fusion(f32[1024]{0:T(1024)S(1)} %bitcast.88, f32[1536]{0:T(1024)S(1)} %add_rsqrt_fusion, bf16[512,1024]{1,0:T(8,128)(2,1)S(1)} %get-tuple-element.212, bf16[512,1024]{1,0:T(8,128)(2,1)S(1)} %bitcast.73, bf16[512,1024]{1,0:T(8,128)(2,1)S(1)} %get-tuple-element.211), kind=kLoop, calls=%fused_computation.2 | loop fusion | flops 14155776 | bytes 6301696 | tf_op jit(solution)/shard_map/convert_element_type | solution.py:574
  76.2 13.0 %collective-permute-done.p1 = bf16[512,1024]{1,0:T(8,128)(2,1)} collective-permute-done((bf16[512,1024]{1,0:T(8,128)(2,1)}, bf16[512,1024]{1,0:T(8,128)(2,1)}, u32[]{:S(2)}, u32[]{:S(2)}) %collective-permute-start) | collective-permute-done | bytes 1048608 | tf_op jit(solution)/shard_map/ppermute | solution.py:423
  100.5 6.7 %collective-permute-done.6 = bf16[256,1024]{1,0:T(8,128)(2,1)S(1)} collective-permute-done((bf16[256,1024]{1,0:T(8,128)(2,1)S(1)}, bf16[256,1024]{1,0:T(8,128)(2,1)S(1)}, u32[]{:S(2)}, u32[]{:S(2)}) %collective-permute-start.6) | collective-permute-done | bytes 524320 | tf_op jit(solution)/shard_map/ppermute | solution.py:423
  107.7 2.6 collective-permute-done.7
  115.4 44.5 %attention_forward.1 = (bf16[512,1024]{1,0:T(8,128)(2,1)}, bf16[1536,1024]{1,0:T(8,128)(2,1)}, bf16[1536,1024]{1,0:T(8,128)(2,1)}, bf16[512,1024]{1,0:T(8,128)(2...) custom-call(s32[2]{0:T(128)} %pad_add_fusion.place_ref, ...), custom_call_target="tpu_custom_call" | custom-call | flops 1000000 | bytes 10000 | tf_op jit(solution)/shard_map/attention_forward/pallas_call | solution.py:229
  159.9 8.8 %collective-permute-done.10.p3 = bf16[512,1408]{1,0:T(8,128)(2,1)} collective-permute-done((bf16[512,1408]{1,0:T(8,128)(2,1)S(1)}, bf16[512,1408]{1,0:T(8,128)(2,1)}, u32[]{:S(2)}, u32[]{:S(2)}) %collective-permute-start.10) | collective-permute-done | bytes 1441824 | tf_op jit(solution)/shard_map/ppermute | solution.py:423
  168.7 2.8 collective-permute-done.9.p1
  174.5 3.3 multiply_reduce_fusion.2
  179.4 31.2 %feed_forward.1 = (bf16[512,2816]{1,0:T(8,128)(2,1)}, bf16[512,5632]{1,0:T(8,128)(2,1)}, bf16[512,1024]{1,0:T(8,128)(2,1)}, bf16[512,1024]{1,0:T(8,128)(2,1)}, f...) custom-call(s32[2]{0:T(128)} %pad_add_fusion.place_ref, ...), custom_call_target="tpu_custom_call" | custom-call | flops 1000000 | bytes 10000 | tf_op jit(solution)/shard_map/feed_forward/pallas_call | solution.py:328
  210.7 8.3 %convolution_convert_fusion = bf16[512,5632]{1,0:T(8,128)(2,1)} fusion(bf16[512,5632]{1,0:T(8,128)(2,1)} %get-tuple-element.234, pred[]{:T(512)S(6)} %eq.181, bf16[512,128]{1,0:T(8,128)(2,1)S(1)} %get-tuple-element.338, bf16[512,128]{1,0:T(8,128)(2,1)S(1)} %get-tuple-element.339, bf16[512,128]{1,0:T(8,128)(2,1)S(1)} %get-tuple-element.340, ...), kind=kOutput, calls=%fused_computation.1 | convolution fusion | flops 2960130048 | bytes 12582913 | tf_op jit(solution)/shard_map/dot_general | solution.py:23
  219.0 5.1 convolution_convert_fusion.1
  229.1 2.6 convolution_convert_fusion.2
  231.7 2.8 collective-permute-done.15
  234.6 7.5 %add_convert_fusion = bf16[512,5632]{1,0:T(8,128)(2,1)S(1)} fusion(bf16[512,5632]{1,0:T(8,128)(2,1)} %collective-permute-done.15, bf16[512,5632]{1,0:T(8,128)(2,1)} %get-tuple-element.234, pred[]{:T(512)S(6)} %eq.181, bf16[512,128]{1,0:T(8,128)(2,1)S(1)} %copy-done.29, bf16[512,128]{1,0:T(8,128)(2,1)S(1)} %copy-done.31, bf16[512,128]{1,0:T(8,128)(2,1)S(1)} %copy-done.33, ...), kind=kOutput, calls=%fused_computation | convolution fusion | flops 2965897216 | bytes 18350080 | tf_op jit(solution)/shard_map/dot_general | solution.py:23
  245.5 4.9 collective-permute-start.16
  252.9 36.7 %attention_backward.2 = (bf16[512,512]{1,0:T(8,128)(2,1)}, bf16[1536,1024]{1,0:T(8,128)(2,1)}, f32[4,1,256]{2,1,0:T(1,128)}, f32[4,1,256]{2,1,0:T(1,128)}, f32[4,8,128]{2,1,0:T(8,128)}) custom-call(s32[2]{0:T(128)} %pad_add_fusion.place_ref, bf16[512,1024]{1,0:T(8,128)(2,1)} %get-tuple-element.217.q_ref, bf16[1536,1024]{1,0:T(8,128)(2,1)} %get-tuple-element.218.k_ref, ...), custom_call_target="tpu_custom_call" | custom-call | flops 1000000 | bytes 10000 | tf_op jit(solution)/shard_map/attention_backward/pallas_call | solution.py:347
  294.6 2.3 convolution_convert_fusion.6
  296.9 4.8 convolution_convert_fusion.4
  307.1 3.0 add_convert_fusion.4
  313.8 35.5 %attention_backward.3 = (bf16[512,512]{1,0:T(8,128)(2,1)}, bf16[1536,1024]{1,0:T(8,128)(2,1)}, f32[4,1,256]{2,1,0:T(1,128)}, f32[4,1,256]{2,1,0:T(1,128)}, f32[4,8,128]{2,1,0:T(8,128)}) custom-call(s32[2]{0:T(128)} %pad_add_fusion.place_ref, bf16[512,1024]{1,0:T(8,128)(2,1)} %get-tuple-element.217.q_ref, bf16[1536,1024]{1,0:T(8,128)(2,1)} %get-tuple-element.218.k_ref, ...), custom_call_target="tpu_custom_call" | custom-call | flops 1000000 | bytes 10000 | tf_op jit(solution)/shard_map/attention_backward/pallas_call | solution.py:347
  353.6 3.5 all-to-all-start.1
  357.2 3.9 add_convert_fusion.1
  361.1 6.2 %fusion.3 = f32[1536,1024]{1,0:T(8,128)S(1)} fusion(bf16[1536,1024]{1,0:T(8,128)(2,1)} %get-tuple-element.290, bf16[1024,2048]{1,0:T(8,128)(2,1)} %get-tuple-element.253), kind=kOutput, calls=%fused_computation.17 | convolution fusion | flops 3221225472 | bytes 11534336 | tf_op jit(solution)/shard_map/dot_general | solution.py:22
  367.3 5.8 %fusion.76 = (bf16[1536,1024]{1,0:T(8,128)(2,1)S(1)}, f32[1536,1024]{1,0:T(8,128)}) fusion(f32[1536,1024]{1,0:T(8,128)S(1)} %fusion.3, bf16[1536,1024]{1,0:T(8,128)(2,1)S(1)} %copy-done.65, bf16[1024,2048]{1,0:T(8,128)(2,1)S(1)} %copy-done.63), kind=kOutput, calls=%fused_computation.212 | convolution fusion | flops 3224371200 | bytes 20971520 | tf_op jit(solution)/shard_map/dot_general | solution.py:22
  377.4 2.8 convolution_convert_fusion.3
  380.2 19.6 %collective-permute-done.25 = bf16[512,1024]{1,0:T(8,128)(2,1)} collective-permute-done((bf16[512,1024]{1,0:T(8,128)(2,1)S(1)}, bf16[512,1024]{1,0:T(8,128)(2,1)}, u32[]{:S(2)}, u32[]{:S(2)}) %collective-permute-start.25) | collective-permute-done | bytes 1048608 | tf_op jit(solution)/shard_map/ppermute | solution.py:433
  408.5 2.3 collective-permute-start.28
  413.7 3.5 all-to-all-start.2
  419.7 3.6 collective-permute-done.24
  423.3 15.6 %all-to-all-done.2 = bf16[4,120,1024]{2,1,0:T(8,128)(2,1)S(1)} async-done(((bf16[4,120,1024]{2,1,0:T(8,128)(2,1)}), bf16[4,120,1024]{2,1,0:T(8,128)(2,1)S(1)}, u32[]{:S(2)}, u32[]{:S(2)}) %all-to-all-start.2) | async-done | bytes 983072 | tf_op jit(solution)/shard_map/all_to_all | solution.py:443
  442.1 2.2 broadcast_in_dim.221
  444.3 3.7 all-to-all-start.3
  448.0 2.8 add_convert_fusion.2
  453.5 13.8 %all-to-all-done.3.refs_0_ = bf16[4,128,1408]{2,1,0:T(8,128)(2,1)S(1)} async-done(((bf16[4,128,1408]{2,1,0:T(8,128)(2,1)}), bf16[4,128,1408]{2,1,0:T(8,128)(2,1)S(1)}, u32[]{:S(2)}, u32[]{:S(2)}) %all-to-all-start.3) | async-done | bytes 1441824 | tf_op jit(solution)/shard_map/all_to_all | solution.py:443
  470.8 3.9 all-to-all-start.4
  474.7 5.2 %maximum_convert_fusion = f32[1536,1024]{1,0:T(8,128)} fusion(bf16[512,1024]{1,0:T(8,128)(2,1)S(1)} %copy-done.5, bf16[512,1024]{1,0:T(8,128)(2,1)} %bitcast.70, bf16[512,1024]{1,0:T(8,128)(2,1)} %copy-done.6), kind=kLoop, calls=%fused_computation.6 | loop fusion | flops 9437184 | bytes 9437184 | tf_op jit(solution)/shard_map/convert_element_type | solution.py:572
  486.1 3.7 collective-permute-done.29
  489.9 7.8 %all-to-all-done.4.refs_0_ = bf16[4,128,896]{2,1,0:T(8,128)(2,1)S(1)} async-done(((bf16[4,128,896]{2,1,0:T(8,128)(2,1)}), bf16[4,128,896]{2,1,0:T(8,128)(2,1)S(1)}, u32[]{:S(2)}, u32[]{:S(2)}) %all-to-all-start.4) | async-done | bytes 917536 | tf_op jit(solution)/shard_map/all_to_all | solution.py:443
  499.6 4.7 multiply_reduce_fusion.1
  506.2 4.0 add_bitcast_fusion
  (347 shorter events, 101.8 us)
Async XLA Ops:
  7.2 41.2 %all-gather.4.cloned.1.call-start = ((), (), s32[]{:S(2)}) async-start(), calls=%async_computation.9 | async-start | bytes 2359296 | tf_op jit(solution)/shard_map/all_gather | solution.py:528
  9.1 81.6 %all-gather.6.cloned.1.call-start = ((), (), s32[]{:S(2)}) async-start(), calls=%async_computation.10 | async-start | bytes 3244032 | tf_op jit(solution)/shard_map/all_gather | solution.py:529
  10.9 168.3 %all-gather.8.cloned.1.call-start = ((), (), s32[]{:S(2)}) async-start(), calls=%async_computation.11 | async-start | bytes 6488064 | tf_op jit(solution)/shard_map/all_gather | solution.py:535
  11.7 26.2 %collective-permute-start.2 = (bf16[512,1024]{1,0:T(8,128)(2,1)S(1)}, bf16[512,1024]{1,0:T(8,128)(2,1)S(1)}, u32[]{:S(2)}, u32[]{:S(2)}) collective-permute-start(bf16[512,1024]{1,0:T(8,128)(2,1)S(1)} %bitcast.71), channel_id=1, source_target_pairs={{0,8},{8,0},{16,24},{24,16},{1,9},{9,1},{17,25},{25,17},{2,10},{10... | collective-permute-start | bytes 3145736 | tf_op jit(solution)/shard_map/ppermute | solution.py:423
  37.8 25.3 %collective-permute-start.3 = (bf16[512,1024]{1,0:T(8,128)(2,1)S(1)}, bf16[512,1024]{1,0:T(8,128)(2,1)}, u32[]{:S(2)}, u32[]{:S(2)}) collective-permute-start(bf16[512,1024]{1,0:T(8,128)(2,1)S(1)} %collective-permute-done.2), channel_id=1, source_target_pairs={{0,16},{24,8},{1,17},{25,9},{2,18},{26,10},{3,19},{27,11},{4,20},{... | collective-permute-start | bytes 3145736 | tf_op jit(solution)/shard_map/ppermute | solution.py:544
  51.4 16.3 %all-to-all-start = ((bf16[8,16,128]{2,1,0:T(8,128)(2,1)}), bf16[8,16,128]{2,1,0:T(8,128)(2,1)S(1)}, u32[]{:S(2)}, u32[]{:S(2)}) async-start(bf16[8,16,128]{2,1,0:T(8,128)(2,1)} %broadcast_in_dim.196), calls=%async_computation | async-start | bytes 65536 | tf_op jit(solution)/shard_map/all_to_all | solution.py:553
  56.2 237.6 %reduce-scatter.5.cloned.1.call-start = ((), (), s32[]{:S(2)}) async-start(), calls=%async_computation.12 | async-start | bytes 6488064 | tf_op jit(solution)/shard_map/reduce_scatter | solution.py:605
  64.8 24.4 %collective-permute-start = (bf16[512,1024]{1,0:T(8,128)(2,1)}, bf16[512,1024]{1,0:T(8,128)(2,1)}, u32[]{:S(2)}, u32[]{:S(2)}) collective-permute-start(bf16[512,1024]{1,0:T(8,128)(2,1)} %constant_dynamic-slice_fusion.4), channel_id=1, source_target_pairs={{0,8},{8,0},{16,24},{24,16},{1,9},{9,1},{17,25},{25,17},{2,10},{10... | collective-permute-start | bytes 3145736 | tf_op jit(solution)/shard_map/ppermute | solution.py:423
  67.5 23.2 %collective-permute-start.1 = (bf16[512,1024]{1,0:T(8,128)(2,1)}, bf16[512,1024]{1,0:T(8,128)(2,1)}, u32[]{:S(2)}, u32[]{:S(2)}) collective-permute-start(bf16[512,1024]{1,0:T(8,128)(2,1)} %constant_dynamic-slice_fusion.4), channel_id=1, source_target_pairs={{0,16},{8,24},{16,0},{24,8},{1,17},{9,25},{17,1},{25,9},{2,18},{10... | collective-permute-start | bytes 3145736 | tf_op jit(solution)/shard_map/ppermute | solution.py:423
  90.7 19.6 %collective-permute-start.4 = (bf16[512,1024]{1,0:T(8,128)(2,1)}, bf16[512,1024]{1,0:T(8,128)(2,1)S(1)}, u32[]{:S(2)}, u32[]{:S(2)}) collective-permute-start(bf16[512,1024]{1,0:T(8,128)(2,1)} %collective-permute-done.p1), channel_id=1, source_target_pairs={{0,1},{1,0},{2,3},{3,2},{4,5},{5,4},{6,7},{7,6},{8,9},{9,8},{10,11... | collective-permute-start | bytes 3145736 | tf_op jit(solution)/shard_map/ppermute | solution.py:423
  92.4 14.8 %collective-permute-start.6 = (bf16[256,1024]{1,0:T(8,128)(2,1)S(1)}, bf16[256,1024]{1,0:T(8,128)(2,1)S(1)}, u32[]{:S(2)}, u32[]{:S(2)}) collective-permute-start(bf16[256,1024]{1,0:T(8,128)(2,1)S(1)} %slice.426), channel_id=1, source_target_pairs={{0,16},{8,24},{16,0},{24,8},{1,17},{9,25},{17,1},{25,9},{2,18},{10... | collective-permute-start | bytes 1572872 | tf_op jit(solution)/shard_map/ppermute | solution.py:423
  95.4 14.8 %collective-permute-start.7 = (bf16[256,1024]{1,0:T(8,128)(2,1)S(1)}, bf16[256,1024]{1,0:T(8,128)(2,1)S(1)}, u32[]{:S(2)}, u32[]{:S(2)}) collective-permute-start(bf16[256,1024]{1,0:T(8,128)(2,1)S(1)} %slice.427), channel_id=1, source_target_pairs={{0,8},{8,0},{16,24},{24,16},{1,9},{9,1},{17,25},{25,17},{2,10},{10... | collective-permute-start | bytes 1572872 | tf_op jit(solution)/shard_map/ppermute | solution.py:423
  98.6 70.1 %collective-permute-start.10 = (bf16[512,1408]{1,0:T(8,128)(2,1)S(1)}, bf16[512,1408]{1,0:T(8,128)(2,1)}, u32[]{:S(2)}, u32[]{:S(2)}) collective-permute-start(bf16[512,1408]{1,0:T(8,128)(2,1)S(1)} %constant_dynamic-slice_fusion.2), channel_id=1, source_target_pairs={{0,16},{8,24},{16,0},{24,8},{1,17},{9,25},{17,1},{25,9},{2,18},{10... | collective-permute-start | bytes 4325384 | tf_op jit(solution)/shard_map/ppermute | solution.py:423
  99.1 69.7 %collective-permute-start.11 = (bf16[512,1408]{1,0:T(8,128)(2,1)S(1)}, bf16[512,1408]{1,0:T(8,128)(2,1)}, u32[]{:S(2)}, u32[]{:S(2)}) collective-permute-start(bf16[512,1408]{1,0:T(8,128)(2,1)S(1)} %constant_dynamic-slice_fusion.2), channel_id=1, source_target_pairs={{0,24},{8,16},{16,8},{24,0},{1,25},{9,17},{17,9},{25,1},{2,26},{10... | collective-permute-start | bytes 4325384 | tf_op jit(solution)/shard_map/ppermute | solution.py:423
  107.2 64.3 %collective-permute-start.9 = (bf16[512,1408]{1,0:T(8,128)(2,1)S(1)}, bf16[512,1408]{1,0:T(8,128)(2,1)}, u32[]{:S(2)}, u32[]{:S(2)}) collective-permute-start(bf16[512,1408]{1,0:T(8,128)(2,1)S(1)} %constant_dynamic-slice_fusion.2), channel_id=1, source_target_pairs={{0,8},{8,0},{16,24},{24,16},{1,9},{9,1},{17,25},{25,17},{2,10},{10... | collective-permute-start | bytes 4325384 | tf_op jit(solution)/shard_map/ppermute | solution.py:423
  110.3 3.1 collective-permute-start.5
  110.3 4.1 collective-permute-start.8
  171.5 7.6 %collective-permute-start.12 = (bf16[512,1408]{1,0:T(8,128)(2,1)}, bf16[512,1408]{1,0:T(8,128)(2,1)}, u32[]{:S(2)}, u32[]{:S(2)}) collective-permute-start(bf16[512,1408]{1,0:T(8,128)(2,1)} %collective-permute-done.9.p1), channel_id=1, source_target_pairs={{0,1},{1,0},{2,3},{3,2},{4,5},{5,4},{6,7},{7,6},{8,9},{9,8},{10,11... | collective-permute-start | bytes 4325384 | tf_op jit(solution)/shard_map/ppermute | solution.py:423
  171.5 7.6 %collective-permute-start.13 = (bf16[512,1408]{1,0:T(8,128)(2,1)}, bf16[512,1408]{1,0:T(8,128)(2,1)}, u32[]{:S(2)}, u32[]{:S(2)}) collective-permute-start(bf16[512,1408]{1,0:T(8,128)(2,1)} %collective-permute-done.10.p3), channel_id=1, source_target_pairs={{0,1},{1,0},{2,3},{3,2},{4,5},{5,4},{6,7},{7,6},{8,9},{9,8},{10,11... | collective-permute-start | bytes 4325384 | tf_op jit(solution)/shard_map/ppermute | solution.py:423
  172.0 7.2 %collective-permute-start.14 = (bf16[512,1408]{1,0:T(8,128)(2,1)}, bf16[512,1408]{1,0:T(8,128)(2,1)}, u32[]{:S(2)}, u32[]{:S(2)}) collective-permute-start(bf16[512,1408]{1,0:T(8,128)(2,1)} %collective-permute-done.11.p5), channel_id=1, source_target_pairs={{0,1},{1,0},{2,3},{3,2},{4,5},{5,4},{6,7},{7,6},{8,9},{9,8},{10,11... | collective-permute-start | bytes 4325384 | tf_op jit(solution)/shard_map/ppermute | solution.py:423
  224.2 127.2 %reduce-scatter.7.cloned.1.call-start = ((), (), s32[]{:S(2)}) async-start(), calls=%async_computation.13 | async-start | bytes 2359296 | tf_op jit(solution)/shard_map/reduce_scatter | solution.py:620
  224.6 9.9 %collective-permute-start.15 = (bf16[512,5632]{1,0:T(8,128)(2,1)}, bf16[512,5632]{1,0:T(8,128)(2,1)}, u32[]{:S(2)}, u32[]{:S(2)}) collective-permute-start(bf16[512,5632]{1,0:T(8,128)(2,1)} %convolution_convert_fusion), channel_id=1, source_target_pairs={{0,1},{1,0},{2,3},{3,2},{4,5},{5,4},{6,7},{7,6},{8,9},{9,8},{10,11... | collective-permute-start | bytes 17301512 | tf_op jit(solution)/shard_map/ppermute | solution.py:423
  245.5 44.2 %collective-permute-start.16 = (bf16[256,1408]{1,0:T(8,128)(2,1)}, bf16[256,1408]{1,0:T(8,128)(2,1)}, u32[]{:S(2)}, u32[]{:S(2)}) collective-permute-start(bf16[256,1408]{1,0:T(8,128)(2,1)} %get-tuple-element.332), channel_id=1, source_target_pairs={{0,8},{8,0},{16,24},{24,16},{1,9},{9,1},{17,25},{25,17},{2,10},{10... | collective-permute-start | bytes 2162696 | tf_op jit(solution)/shard_map/ppermute | solution.py:423
  250.5 39.2 %collective-permute-start.17 = (bf16[256,1408]{1,0:T(8,128)(2,1)}, bf16[256,1408]{1,0:T(8,128)(2,1)}, u32[]{:S(2)}, u32[]{:S(2)}) collective-permute-start(bf16[256,1408]{1,0:T(8,128)(2,1)} %get-tuple-element.331), channel_id=1, source_target_pairs={{0,16},{8,24},{16,0},{24,8},{1,17},{9,25},{17,1},{25,9},{2,18},{10... | collective-permute-start | bytes 2162696 | tf_op jit(solution)/shard_map/ppermute | solution.py:423
  252.8 54.3 %copy-start.22 = (bf16[1536,512]{1,0:T(8,128)(2,1)}, bf16[1536,512]{1,0:T(8,128)(2,1)S(1)}, u32[]{:S(2)}) copy-start(bf16[1536,512]{1,0:T(8,128)(2,1)S(1)} %get-tuple-element.320) | copy-start | bytes 4718596
  252.8 36.7 %slice-start = ((s8[5767168]{0:T(1024)(128)(4,1)}), s8[1572864]{0:T(1024)(128)(4,1)S(1)}, s32[]{:S(2)}) async-start(s8[5767168]{0:T(1024)(128)(4,1)} %bitcast.68), calls=%async_computation.16 | async-start | bytes 3145728
  252.8 36.7 %slice-start.1 = ((s8[5767168]{0:T(1024)(128)(4,1)}), s8[4194304]{0:T(1024)(128)(4,1)S(1)}, s32[]{:S(2)}) async-start(s8[5767168]{0:T(1024)(128)(4,1)} %bitcast.68), calls=%async_computation.17 | async-start | bytes 8388608
  301.7 5.4 %collective-permute-start.19 = (bf16[512,1024]{1,0:T(8,128)(2,1)}, bf16[512,1024]{1,0:T(8,128)(2,1)}, u32[]{:S(2)}, u32[]{:S(2)}) collective-permute-start(bf16[512,1024]{1,0:T(8,128)(2,1)} %convolution_convert_fusion.4), channel_id=1, source_target_pairs={{0,1},{1,0},{2,3},{3,2},{4,5},{5,4},{6,7},{7,6},{8,9},{9,8},{10,11... | collective-permute-start | bytes 3145736 | tf_op jit(solution)/shard_map/ppermute | solution.py:423
  301.7 3.8 collective-permute-start.18
  303.7 47.7 %collective-permute-start.22 = (bf16[512,1408]{1,0:T(8,128)(2,1)}, bf16[512,1408]{1,0:T(8,128)(2,1)}, u32[]{:S(2)}, u32[]{:S(2)}) collective-permute-start(bf16[512,1408]{1,0:T(8,128)(2,1)} %pad_maximum_fusion.2), channel_id=1, source_target_pairs={{0,8},{8,0},{16,24},{24,16},{1,9},{9,1},{17,25},{25,17},{2,10},{10... | collective-permute-start | bytes 4325384 | tf_op jit(solution)/shard_map/ppermute | solution.py:423
  303.9 47.5 %collective-permute-start.23 = (bf16[512,1408]{1,0:T(8,128)(2,1)}, bf16[512,1408]{1,0:T(8,128)(2,1)}, u32[]{:S(2)}, u32[]{:S(2)}) collective-permute-start(bf16[512,1408]{1,0:T(8,128)(2,1)} %pad_maximum_fusion.3), channel_id=1, source_target_pairs={{0,16},{8,24},{16,0},{24,8},{1,17},{9,25},{17,1},{25,9},{2,18},{10... | collective-permute-start | bytes 4325384 | tf_op jit(solution)/shard_map/ppermute | solution.py:423
  311.3 40.0 %collective-permute-start.20 = (bf16[256,768]{1,0:T(8,128)(2,1)S(1)}, bf16[256,768]{1,0:T(8,128)(2,1)S(1)}, u32[]{:S(2)}, u32[]{:S(2)}) collective-permute-start(bf16[256,768]{1,0:T(8,128)(2,1)S(1)} %get-tuple-element.346), channel_id=1, source_target_pairs={{0,8},{8,0},{16,24},{24,16},{1,9},{9,1},{17,25},{25,17},{2,10},{10... | collective-permute-start | bytes 1179656 | tf_op jit(solution)/shard_map/ppermute | solution.py:423
  313.4 36.7 %copy-start.59 = (f32[4,8,128]{2,1,0:T(8,128)S(1)}, f32[4,8,128]{2,1,0:T(8,128)}, u32[]{:S(2)}) copy-start(f32[4,8,128]{2,1,0:T(8,128)} %get-tuple-element.284) | copy-start | bytes 49156
  313.4 38.1 %copy-start.47 = (bf16[352,1024]{1,0:T(8,128)(2,1)S(1)}, bf16[352,1024]{1,0:T(8,128)(2,1)}, u32[]{:S(2)}) copy-start(bf16[352,1024]{1,0:T(8,128)(2,1)} %reduce-scatter.5.cloned.1.call-done) | copy-start | bytes 2162692
  313.4 38.0 %collective-permute-start.21 = (bf16[256,768]{1,0:T(8,128)(2,1)S(1)}, bf16[256,768]{1,0:T(8,128)(2,1)S(1)}, u32[]{:S(2)}, u32[]{:S(2)}) collective-permute-start(bf16[256,768]{1,0:T(8,128)(2,1)S(1)} %get-tuple-element.345), channel_id=1, source_target_pairs={{0,16},{8,24},{16,0},{24,8},{1,17},{9,25},{17,1},{25,9},{2,18},{10... | collective-permute-start | bytes 1179656 | tf_op jit(solution)/shard_map/ppermute | solution.py:423
  353.6 19.7 %all-to-all-start.1 = ((bf16[4,120,1024]{2,1,0:T(8,128)(2,1)}), bf16[4,120,1024]{2,1,0:T(8,128)(2,1)S(1)}, u32[]{:S(2)}, u32[]{:S(2)}) async-start(bf16[4,120,1024]{2,1,0:T(8,128)(2,1)} %bitcast.21), calls=%async_computation.3 | async-start | bytes 1966080 | tf_op jit(solution)/shard_map/all_to_all | solution.py:484
  357.1 42.7 %reduce-scatter.9.cloned.1.call-start = ((), (), s32[]{:S(2)}) async-start(), calls=%async_computation.14 | async-start | bytes 1802240 | tf_op jit(solution)/shard_map/reduce_scatter | solution.py:479
  373.4 26.3 %collective-permute-start.25 = (bf16[512,1024]{1,0:T(8,128)(2,1)S(1)}, bf16[512,1024]{1,0:T(8,128)(2,1)}, u32[]{:S(2)}, u32[]{:S(2)}) collective-permute-start(bf16[512,1024]{1,0:T(8,128)(2,1)S(1)} %broadcast_select_fusion.2), channel_id=1, source_target_pairs={{8,24},{16,0},{9,25},{17,1},{10,26},{18,2},{11,27},{19,3},{12,28},... | collective-permute-start | bytes 3145736 | tf_op jit(solution)/shard_map/ppermute | solution.py:433
  399.8 4.8 collective-permute-start.27
  399.8 3.6 collective-permute-start.26
  402.6 20.7 %collective-permute-start.24 = (bf16[512,768]{1,0:T(8,128)(2,1)}, bf16[512,768]{1,0:T(8,128)(2,1)}, u32[]{:S(2)}, u32[]{:S(2)}) collective-permute-start(bf16[512,768]{1,0:T(8,128)(2,1)} %pad_maximum_fusion.10), channel_id=1, source_target_pairs={{0,8},{8,0},{16,24},{24,16},{1,9},{9,1},{17,25},{25,17},{2,10},{10... | collective-permute-start | bytes 2359304 | tf_op jit(solution)/shard_map/ppermute | solution.py:423
  408.5 30.4 %collective-permute-start.28 = (bf16[512,768]{1,0:T(8,128)(2,1)}, bf16[512,768]{1,0:T(8,128)(2,1)}, u32[]{:S(2)}, u32[]{:S(2)}) collective-permute-start(bf16[512,768]{1,0:T(8,128)(2,1)} %fusion.16), channel_id=1, source_target_pairs={{0,16},{8,24},{16,0},{24,8},{1,17},{9,25},{17,1},{25,9},{2,18},{10... | collective-permute-start | bytes 2359304 | tf_op jit(solution)/shard_map/ppermute | solution.py:423
  413.7 25.2 %all-to-all-start.2 = ((bf16[4,120,1024]{2,1,0:T(8,128)(2,1)}), bf16[4,120,1024]{2,1,0:T(8,128)(2,1)S(1)}, u32[]{:S(2)}, u32[]{:S(2)}) async-start(bf16[4,120,1024]{2,1,0:T(8,128)(2,1)} %broadcast_in_dim.220), calls=%async_computation.5 | async-start | bytes 1966080 | tf_op jit(solution)/shard_map/all_to_all | solution.py:443
  417.2 51.6 %reduce-scatter.11.cloned.1.call-start = ((), (), s32[]{:S(2)}) async-start(), calls=%async_computation.15 | async-start | bytes 1146880 | tf_op jit(solution)/shard_map/reduce_scatter | solution.py:479
  417.3 1.4 collective-permute-start.30
  444.3 23.0 %all-to-all-start.3 = ((bf16[4,128,1408]{2,1,0:T(8,128)(2,1)}), bf16[4,128,1408]{2,1,0:T(8,128)(2,1)S(1)}, u32[]{:S(2)}, u32[]{:S(2)}) async-start(bf16[4,128,1408]{2,1,0:T(8,128)(2,1)} %broadcast_in_dim.221), calls=%async_computation.7 | async-start | bytes 2883584 | tf_op jit(solution)/shard_map/all_to_all | solution.py:443
  450.8 39.0 %collective-permute-start.29 = (bf16[512,1024]{1,0:T(8,128)(2,1)}, bf16[512,1024]{1,0:T(8,128)(2,1)}, u32[]{:S(2)}, u32[]{:S(2)}) collective-permute-start(bf16[512,1024]{1,0:T(8,128)(2,1)} %add_convert_fusion.2), channel_id=1, source_target_pairs={{0,8},{8,0},{16,24},{24,16},{1,9},{9,1},{17,25},{25,17},{2,10},{10... | collective-permute-start | bytes 3145736 | tf_op jit(solution)/shard_map/ppermute | solution.py:423
  470.8 26.9 %all-to-all-start.4 = ((bf16[4,128,896]{2,1,0:T(8,128)(2,1)}), bf16[4,128,896]{2,1,0:T(8,128)(2,1)S(1)}, u32[]{:S(2)}, u32[]{:S(2)}) async-start(bf16[4,128,896]{2,1,0:T(8,128)(2,1)} %broadcast_in_dim.222), calls=%async_computation.8 | async-start | bytes 1835008 | tf_op jit(solution)/shard_map/all_to_all | solution.py:443
  (72 other events, 738.8 us)
Sparse Core Ops, SparseCore 0:
  10.2 31.7 all-gather.3
  44.3 36.3 all-gather.5
  82.3 59.2 all-gather.7
  224.3 68.7 reduce-scatter.4
  295.8 34.1 reduce-scatter.6
  361.2 35.0 reduce-scatter.8
  442.2 26.5 reduce-scatter.10

commit v5 on v4

--- a/solution.py
+++ b/solution.py
@@ -583,11 +583,11 @@
     q, k, v, attn, lse, c_q, c_k, w_q, w_kv, w_attn = attention_forward(
         place, normed, pieces, gain_q, gain_k, cosine, sine, query_feat, key_feat, scales, mats
     )
-    if quartered:
-        in_by, attn = tied(in_by, attn)
-        pieces_in = (whole_in,) + sum((with_partner(piece) for piece in in_by), ())
     mixed = tokens[0].astype(F32) + jnp.dot(attn, w_attn, preferred_element_type=F32)
     normed_two = rms_scale(mixed, gains[1]).astype(BF)
+    if quartered:
+        in_by, normed_two, mixed = tied(in_by, normed_two, mixed)
+        pieces_in = (whole_in,) + sum((with_partner(piece) for piece in in_by), ())
     valid_col = key_obs[own].astype(F32)[:, None]
     all_tokens = rows * n_context * n_shards
     hidden, d_gate_low, activations, d_final_low, d_mixed, d_mixed_low, d_attn, squared = feed_forward(
@@ -680,7 +680,6 @@
         qkv_part = core_scatter(qkv_total)
         qkv_part, in_spread = tied(qkv_part, in_spread)
         spread = ctx_spread(qkv_part)
-        from_others, spread = tied(from_others, spread)
         from_others = from_others.astype(F32)
         qkv_grad, gain_one = finish(spread, qkv_weight, tuple((i * 256, 256, i * D) for i in range(3)))
         sums = jnp.sum(spread[:, :, 3 * 256 :].astype(F32), axis=0)

time: 525 us -> 517 us (0.985)
    all_to_all x3, waiting for transfers between devices: 37.1 us -> 18.9 us  [ctx_spread(): lax.all_to_all(jnp.broadcast_to(part[None], (size,) + part.shape), 'ctx',...]
    ppermute x29, waiting for transfers between devices: 65.2 us -> 78.7 us  [permuted(): lax.ppermute(shard, axis, [(i, i ^ flip) for i in range(lax.axis_size(axi...]
  transfers between devices with their start and end apart: 43 -> 43, of which waited for: 21 -> 21; matrix products, arithmetic and copies ran while one was open for 24% -> 25% of each run, Pallas kernels for 23% -> 23%
where the time goes in v5:
time: 517 us; the launch traced here: 510 us
  Pallas kernels  151 us (29%)
  waiting for transfers between devices  127 us (25%)
  matrix products  63.8 us (12%)
  other arithmetic  63.2 us (12%)
  starting transfers between devices  53.2 us (10%)
  local copies, waits for them, and re-layouts  30.3 us (6%)
  between operations  21.7 us (4%)
    ppermute x29, waiting for transfers between devices, permuted(): lax.ppermute(shard, axis, [(i, i ^ flip) for i in range(lax.axis_size(axi...  78.7 us
    pallas_call x2, Pallas kernels, attention_backward(): pl.pallas_call(bwd_kernel, grid_spec=pltpu.PrefetchScalarGridSpec(num_sca...  72.2 us
    pallas_call x1, Pallas kernels, attention_forward(): pl.pallas_call(fwd_kernel, grid_spec=pltpu.PrefetchScalarGridSpec(num_sca...  44.5 us
    dot_general x12, matrix products, dot_tn(): lax.dot_general(a, b, (((0,), (0,)), ((), ())), preferred_element_type=F32)  41.8 us
    pallas_call x1, Pallas kernels, feed_forward(): pl.pallas_call(feed_forward_kernel, in_specs=[smem, smem, vmem, vmem] + [...  31.3 us
    ppermute x29, starting transfers between devices, permuted(): lax.ppermute(shard, axis, [(i, i ^ flip) for i in range(lax.axis_size(axi...  26.9 us
    ppermute x1, waiting for transfers between devices, returned_far(): return lax.ppermute(jnp.where(odd, after, before), 'ctx', [(1, 3), (2, 0)])  19.9 us
    all_to_all x3, waiting for transfers between devices, ctx_spread(): lax.all_to_all(jnp.broadcast_to(part[None], (size,) + part.shape), 'ctx',...  18.9 us
  transfers between devices with their start and end apart: 43, of which 21 were waited for; matrix products, arithmetic and copies ran while one was open for 25% of the time, Pallas kernels for 23%

profile of v5, /device:TPU:0, one launch (start us, length us, event | category | flops | bytes accessed | tf_op | source)
XLA Modules:
  0.0 510.0 jit_solution(8562079716651091731)
XLA Ops:
  11.0 3.0 collective-permute-start.2
  23.9 13.2 %collective-permute-done.2 = bf16[512,1024]{1,0:T(8,128)(2,1)S(1)} collective-permute-done((bf16[512,1024]{1,0:T(8,128)(2,1)S(1)}, bf16[512,1024]{1,0:T(8,128)(2,1)S(1)}, u32[]{:S(2)}, u32[]{:S(2)}) %collective-permute-start.2) | collective-permute-done | bytes 1048608 | tf_op jit(solution)/shard_map/ppermute | solution.py:423
  37.1 4.7 collective-permute-start.3
  41.8 2.8 fusion.40
  47.7 2.3 constant_dynamic-slice_fusion.4
  50.6 4.9 all-to-all-start
  55.8 6.7 %collective-permute-done.3 = bf16[512,1024]{1,0:T(8,128)(2,1)} collective-permute-done((bf16[512,1024]{1,0:T(8,128)(2,1)S(1)}, bf16[512,1024]{1,0:T(8,128)(2,1)}, u32[]{:S(2)}, u32[]{:S(2)}) %collective-permute-start.3) | collective-permute-done | bytes 1048608 | tf_op jit(solution)/shard_map/ppermute | solution.py:544
  64.2 2.6 collective-permute-start
  68.3 7.2 %multiply_convert_fusion.xn_ref = bf16[1536,1024]{1,0:T(8,128)(2,1)} fusion(f32[1024]{0:T(1024)S(1)} %bitcast.88, f32[1536]{0:T(1024)S(1)} %add_rsqrt_fusion, bf16[512,1024]{1,0:T(8,128)(2,1)S(1)} %get-tuple-element.211, bf16[512,1024]{1,0:T(8,128)(2,1)S(1)} %bitcast.73, bf16[512,1024]{1,0:T(8,128)(2,1)S(1)} %get-tuple-element.210), kind=kLoop, calls=%fused_computation.2 | loop fusion | flops 14155776 | bytes 6301696 | tf_op jit(solution)/shard_map/convert_element_type | solution.py:574
  75.5 13.1 %collective-permute-done.p1 = bf16[512,1024]{1,0:T(8,128)(2,1)} collective-permute-done((bf16[512,1024]{1,0:T(8,128)(2,1)}, bf16[512,1024]{1,0:T(8,128)(2,1)}, u32[]{:S(2)}, u32[]{:S(2)}) %collective-permute-start) | collective-permute-done | bytes 1048608 | tf_op jit(solution)/shard_map/ppermute | solution.py:423
  95.7 6.5 %collective-permute-done.6 = bf16[256,1024]{1,0:T(8,128)(2,1)S(1)} collective-permute-done((bf16[256,1024]{1,0:T(8,128)(2,1)S(1)}, bf16[256,1024]{1,0:T(8,128)(2,1)S(1)}, u32[]{:S(2)}, u32[]{:S(2)}) %collective-permute-start.6) | collective-permute-done | bytes 524320 | tf_op jit(solution)/shard_map/ppermute | solution.py:423
  109.7 44.5 %attention_forward.1 = (bf16[512,1024]{1,0:T(8,128)(2,1)}, bf16[1536,1024]{1,0:T(8,128)(2,1)}, bf16[1536,1024]{1,0:T(8,128)(2,1)}, bf16[512,1024]{1,0:T(8,128)(2...) custom-call(s32[2]{0:T(128)} %pad_add_fusion.place_ref, ...), custom_call_target="tpu_custom_call" | custom-call | flops 1000000 | bytes 10000 | tf_op jit(solution)/shard_map/attention_forward/pallas_call | solution.py:229
  154.3 3.3 multiply_reduce_fusion.2
  159.1 10.0 %collective-permute-done.10.p3 = bf16[512,1408]{1,0:T(8,128)(2,1)} collective-permute-done((bf16[512,1408]{1,0:T(8,128)(2,1)S(1)}, bf16[512,1408]{1,0:T(8,128)(2,1)}, u32[]{:S(2)}, u32[]{:S(2)}) %collective-permute-start.10) | collective-permute-done | bytes 1441824 | tf_op jit(solution)/shard_map/ppermute | solution.py:423
  173.6 2.2 collective-permute-done.12.p2
  175.9 2.1 collective-permute-done.14.p6
  178.0 31.3 %feed_forward.1 = (bf16[512,2816]{1,0:T(8,128)(2,1)}, bf16[512,5632]{1,0:T(8,128)(2,1)}, bf16[512,1024]{1,0:T(8,128)(2,1)}, bf16[512,1024]{1,0:T(8,128)(2,1)}, f...) custom-call(s32[2]{0:T(128)} %pad_add_fusion.place_ref, ...), custom_call_target="tpu_custom_call" | custom-call | flops 1000000 | bytes 10000 | tf_op jit(solution)/shard_map/feed_forward/pallas_call | solution.py:328
  209.4 8.3 %convolution_convert_fusion = bf16[512,5632]{1,0:T(8,128)(2,1)} fusion(bf16[512,5632]{1,0:T(8,128)(2,1)} %get-tuple-element.234, pred[]{:T(512)S(6)} %eq.180, bf16[512,128]{1,0:T(8,128)(2,1)S(1)} %get-tuple-element.336, bf16[512,128]{1,0:T(8,128)(2,1)S(1)} %get-tuple-element.337, bf16[512,128]{1,0:T(8,128)(2,1)S(1)} %get-tuple-element.338, ...), kind=kOutput, calls=%fused_computation.1 | convolution fusion | flops 2960130048 | bytes 12582913 | tf_op jit(solution)/shard_map/dot_general | solution.py:23
  217.7 5.1 convolution_convert_fusion.1
  227.5 2.6 convolution_convert_fusion.2
  230.2 3.0 collective-permute-done.15
  233.2 7.5 %add_convert_fusion = bf16[512,5632]{1,0:T(8,128)(2,1)S(1)} fusion(bf16[512,5632]{1,0:T(8,128)(2,1)} %collective-permute-done.15, bf16[512,5632]{1,0:T(8,128)(2,1)} %get-tuple-element.234, pred[]{:T(512)S(6)} %eq.180, bf16[512,128]{1,0:T(8,128)(2,1)S(1)} %copy-done.36, bf16[512,128]{1,0:T(8,128)(2,1)S(1)} %copy-done.38, bf16[512,128]{1,0:T(8,128)(2,1)S(1)} %copy-done.40, ...), kind=kOutput, calls=%fused_computation | convolution fusion | flops 2965897216 | bytes 18350080 | tf_op jit(solution)/shard_map/dot_general | solution.py:23
  244.1 4.6 collective-permute-start.16
  251.4 36.7 %attention_backward.2 = (bf16[512,512]{1,0:T(8,128)(2,1)}, bf16[1536,1024]{1,0:T(8,128)(2,1)}, f32[4,1,256]{2,1,0:T(1,128)}, f32[4,1,256]{2,1,0:T(1,128)}, f32[4,8,128]{2,1,0:T(8,128)}) custom-call(s32[2]{0:T(128)} %pad_add_fusion.place_ref, bf16[512,1024]{1,0:T(8,128)(2,1)} %get-tuple-element.216.q_ref, bf16[1536,1024]{1,0:T(8,128)(2,1)} %get-tuple-element.217.k_ref, ...), custom_call_target="tpu_custom_call" | custom-call | flops 1000000 | bytes 10000 | tf_op jit(solution)/shard_map/attention_backward/pallas_call | solution.py:347
  293.1 2.3 convolution_convert_fusion.6
  295.5 4.8 convolution_convert_fusion.4
  306.0 3.0 add_convert_fusion.4
  313.3 35.5 %attention_backward.3 = (bf16[512,512]{1,0:T(8,128)(2,1)}, bf16[1536,1024]{1,0:T(8,128)(2,1)}, f32[4,1,256]{2,1,0:T(1,128)}, f32[4,1,256]{2,1,0:T(1,128)}, f32[4,8,128]{2,1,0:T(8,128)}) custom-call(s32[2]{0:T(128)} %pad_add_fusion.place_ref, bf16[512,1024]{1,0:T(8,128)(2,1)} %get-tuple-element.216.q_ref, bf16[1536,1024]{1,0:T(8,128)(2,1)} %get-tuple-element.217.k_ref, ...), custom_call_target="tpu_custom_call" | custom-call | flops 1000000 | bytes 10000 | tf_op jit(solution)/shard_map/attention_backward/pallas_call | solution.py:347
  350.9 2.2 pad_maximum_fusion.4
  353.1 3.5 all-to-all-start.1
  356.7 3.4 add_convert_fusion.1
  360.1 6.2 %fusion.3 = f32[1536,1024]{1,0:T(8,128)S(1)} fusion(bf16[1536,1024]{1,0:T(8,128)(2,1)} %get-tuple-element.288, bf16[1024,2048]{1,0:T(8,128)(2,1)} %get-tuple-element.253), kind=kOutput, calls=%fused_computation.17 | convolution fusion | flops 3221225472 | bytes 11534336 | tf_op jit(solution)/shard_map/dot_general | solution.py:22
  366.4 5.8 %fusion.76 = (bf16[1536,1024]{1,0:T(8,128)(2,1)S(1)}, f32[1536,1024]{1,0:T(8,128)}) fusion(f32[1536,1024]{1,0:T(8,128)S(1)} %fusion.3, bf16[1536,1024]{1,0:T(8,128)(2,1)S(1)} %copy-done.75, bf16[1024,2048]{1,0:T(8,128)(2,1)S(1)} %copy-done.73), kind=kOutput, calls=%fused_computation.212 | convolution fusion | flops 3224371200 | bytes 20971520 | tf_op jit(solution)/shard_map/dot_general | solution.py:22
  376.5 2.8 convolution_convert_fusion.3
  379.3 19.9 %collective-permute-done.24 = bf16[512,1024]{1,0:T(8,128)(2,1)} collective-permute-done((bf16[512,1024]{1,0:T(8,128)(2,1)S(1)}, bf16[512,1024]{1,0:T(8,128)(2,1)}, u32[]{:S(2)}, u32[]{:S(2)}) %collective-permute-start.24) | collective-permute-done | bytes 1048608 | tf_op jit(solution)/shard_map/ppermute | solution.py:433
  410.3 3.5 all-to-all-start.2
  415.4 7.0 %collective-permute-done.27 = bf16[512,768]{1,0:T(8,128)(2,1)} collective-permute-done((bf16[512,768]{1,0:T(8,128)(2,1)}, bf16[512,768]{1,0:T(8,128)(2,1)}, u32[]{:S(2)}, u32[]{:S(2)}) %collective-permute-start.27) | collective-permute-done | bytes 786464 | tf_op jit(solution)/shard_map/ppermute | solution.py:423
  422.4 15.3 %all-to-all-done.2 = bf16[4,120,1024]{2,1,0:T(8,128)(2,1)S(1)} async-done(((bf16[4,120,1024]{2,1,0:T(8,128)(2,1)}), bf16[4,120,1024]{2,1,0:T(8,128)(2,1)S(1)}, u32[]{:S(2)}, u32[]{:S(2)}) %all-to-all-start.2) | async-done | bytes 983072 | tf_op jit(solution)/shard_map/all_to_all | solution.py:443
  442.0 3.7 all-to-all-start.3
  445.7 3.3 add_convert_fusion.2
  452.3 4.9 maximum_convert_fusion
  457.2 2.1 fusion.13
  461.4 3.6 all-to-all-done.3.refs_0_
  465.0 2.2 reduce-scatter.11.cloned.1.call-done
  469.2 3.6 all-to-all-start.4
  472.8 14.8 %collective-permute-done.30 = bf16[512,1024]{1,0:T(8,128)(2,1)} collective-permute-done((bf16[512,1024]{1,0:T(8,128)(2,1)}, bf16[512,1024]{1,0:T(8,128)(2,1)}, u32[]{:S(2)}, u32[]{:S(2)}) %collective-permute-start.30) | collective-permute-done | bytes 1048608 | tf_op jit(solution)/shard_map/ppermute | solution.py:423
  487.6 4.7 multiply_reduce_fusion.1
  492.3 3.5 add_bitcast_fusion
  (367 shorter events, 98.5 us)
Async XLA Ops:
  7.2 40.5 %all-gather.4.cloned.1.call-start = ((), (), s32[]{:S(2)}) async-start(), calls=%async_computation.9 | async-start | bytes 2359296 | tf_op jit(solution)/shard_map/all_gather | solution.py:528
  9.1 81.0 %all-gather.6.cloned.1.call-start = ((), (), s32[]{:S(2)}) async-start(), calls=%async_computation.10 | async-start | bytes 3244032 | tf_op jit(solution)/shard_map/all_gather | solution.py:529
  10.9 167.1 %all-gather.8.cloned.1.call-start = ((), (), s32[]{:S(2)}) async-start(), calls=%async_computation.11 | async-start | bytes 6488064 | tf_op jit(solution)/shard_map/all_gather | solution.py:535
  11.0 26.2 %collective-permute-start.2 = (bf16[512,1024]{1,0:T(8,128)(2,1)S(1)}, bf16[512,1024]{1,0:T(8,128)(2,1)S(1)}, u32[]{:S(2)}, u32[]{:S(2)}) collective-permute-start(bf16[512,1024]{1,0:T(8,128)(2,1)S(1)} %bitcast.71), channel_id=1, source_target_pairs={{0,8},{8,0},{16,24},{24,16},{1,9},{9,1},{17,25},{25,17},{2,10},{10... | collective-permute-start | bytes 3145736 | tf_op jit(solution)/shard_map/ppermute | solution.py:423
  37.1 25.3 %collective-permute-start.3 = (bf16[512,1024]{1,0:T(8,128)(2,1)S(1)}, bf16[512,1024]{1,0:T(8,128)(2,1)}, u32[]{:S(2)}, u32[]{:S(2)}) collective-permute-start(bf16[512,1024]{1,0:T(8,128)(2,1)S(1)} %collective-permute-done.2), channel_id=1, source_target_pairs={{0,16},{24,8},{1,17},{25,9},{2,18},{26,10},{3,19},{27,11},{4,20},{... | collective-permute-start | bytes 3145736 | tf_op jit(solution)/shard_map/ppermute | solution.py:544
  50.6 16.2 %all-to-all-start = ((bf16[8,16,128]{2,1,0:T(8,128)(2,1)}), bf16[8,16,128]{2,1,0:T(8,128)(2,1)S(1)}, u32[]{:S(2)}, u32[]{:S(2)}) async-start(bf16[8,16,128]{2,1,0:T(8,128)(2,1)} %broadcast_in_dim.196), calls=%async_computation | async-start | bytes 65536 | tf_op jit(solution)/shard_map/all_to_all | solution.py:553
  55.5 236.9 %reduce-scatter.5.cloned.1.call-start = ((), (), s32[]{:S(2)}) async-start(), calls=%async_computation.12 | async-start | bytes 6488064 | tf_op jit(solution)/shard_map/reduce_scatter | solution.py:605
  64.2 24.4 %collective-permute-start = (bf16[512,1024]{1,0:T(8,128)(2,1)}, bf16[512,1024]{1,0:T(8,128)(2,1)}, u32[]{:S(2)}, u32[]{:S(2)}) collective-permute-start(bf16[512,1024]{1,0:T(8,128)(2,1)} %constant_dynamic-slice_fusion.4), channel_id=1, source_target_pairs={{0,8},{8,0},{16,24},{24,16},{1,9},{9,1},{17,25},{25,17},{2,10},{10... | collective-permute-start | bytes 3145736 | tf_op jit(solution)/shard_map/ppermute | solution.py:423
  66.8 23.3 %collective-permute-start.1 = (bf16[512,1024]{1,0:T(8,128)(2,1)}, bf16[512,1024]{1,0:T(8,128)(2,1)}, u32[]{:S(2)}, u32[]{:S(2)}) collective-permute-start(bf16[512,1024]{1,0:T(8,128)(2,1)} %constant_dynamic-slice_fusion.4), channel_id=1, source_target_pairs={{0,16},{8,24},{16,0},{24,8},{1,17},{9,25},{17,1},{25,9},{2,18},{10... | collective-permute-start | bytes 3145736 | tf_op jit(solution)/shard_map/ppermute | solution.py:423
  91.3 10.9 %collective-permute-start.6 = (bf16[256,1024]{1,0:T(8,128)(2,1)S(1)}, bf16[256,1024]{1,0:T(8,128)(2,1)S(1)}, u32[]{:S(2)}, u32[]{:S(2)}) collective-permute-start(bf16[256,1024]{1,0:T(8,128)(2,1)S(1)} %slice.427), channel_id=1, source_target_pairs={{0,16},{8,24},{16,0},{24,8},{1,17},{9,25},{17,1},{25,9},{2,18},{10... | collective-permute-start | bytes 1572872 | tf_op jit(solution)/shard_map/ppermute | solution.py:423
  92.9 10.9 %collective-permute-start.7 = (bf16[256,1024]{1,0:T(8,128)(2,1)S(1)}, bf16[256,1024]{1,0:T(8,128)(2,1)S(1)}, u32[]{:S(2)}, u32[]{:S(2)}) collective-permute-start(bf16[256,1024]{1,0:T(8,128)(2,1)S(1)} %slice.428), channel_id=1, source_target_pairs={{0,8},{8,0},{16,24},{24,16},{1,9},{9,1},{17,25},{25,17},{2,10},{10... | collective-permute-start | bytes 1572872 | tf_op jit(solution)/shard_map/ppermute | solution.py:423
  94.6 12.4 %collective-permute-start.4 = (bf16[512,1024]{1,0:T(8,128)(2,1)}, bf16[512,1024]{1,0:T(8,128)(2,1)S(1)}, u32[]{:S(2)}, u32[]{:S(2)}) collective-permute-start(bf16[512,1024]{1,0:T(8,128)(2,1)} %collective-permute-done.p1), channel_id=1, source_target_pairs={{0,1},{1,0},{2,3},{3,2},{4,5},{5,4},{6,7},{7,6},{8,9},{9,8},{10,11... | collective-permute-start | bytes 3145736 | tf_op jit(solution)/shard_map/ppermute | solution.py:423
  95.2 13.2 %collective-permute-start.5 = (bf16[512,1024]{1,0:T(8,128)(2,1)}, bf16[512,1024]{1,0:T(8,128)(2,1)S(1)}, u32[]{:S(2)}, u32[]{:S(2)}) collective-permute-start(bf16[512,1024]{1,0:T(8,128)(2,1)} %collective-permute-done.1.p3), channel_id=1, source_target_pairs={{0,1},{1,0},{2,3},{3,2},{4,5},{5,4},{6,7},{7,6},{8,9},{9,8},{10,11... | collective-permute-start | bytes 3145736 | tf_op jit(solution)/shard_map/ppermute | solution.py:423
  103.8 4.6 collective-permute-start.8
  104.1 65.0 %collective-permute-start.10 = (bf16[512,1408]{1,0:T(8,128)(2,1)S(1)}, bf16[512,1408]{1,0:T(8,128)(2,1)}, u32[]{:S(2)}, u32[]{:S(2)}) collective-permute-start(bf16[512,1408]{1,0:T(8,128)(2,1)S(1)} %constant_dynamic-slice_fusion.2), channel_id=1, source_target_pairs={{0,16},{8,24},{16,0},{24,8},{1,17},{9,25},{17,1},{25,9},{2,18},{10... | collective-permute-start | bytes 4325384 | tf_op jit(solution)/shard_map/ppermute | solution.py:423
  105.5 63.6 %collective-permute-start.11 = (bf16[512,1408]{1,0:T(8,128)(2,1)S(1)}, bf16[512,1408]{1,0:T(8,128)(2,1)}, u32[]{:S(2)}, u32[]{:S(2)}) collective-permute-start(bf16[512,1408]{1,0:T(8,128)(2,1)S(1)} %constant_dynamic-slice_fusion.2), channel_id=1, source_target_pairs={{0,24},{8,16},{16,8},{24,0},{1,25},{9,17},{17,9},{25,1},{2,26},{10... | collective-permute-start | bytes 4325384 | tf_op jit(solution)/shard_map/ppermute | solution.py:423
  107.0 63.3 %collective-permute-start.9 = (bf16[512,1408]{1,0:T(8,128)(2,1)S(1)}, bf16[512,1408]{1,0:T(8,128)(2,1)}, u32[]{:S(2)}, u32[]{:S(2)}) collective-permute-start(bf16[512,1408]{1,0:T(8,128)(2,1)S(1)} %constant_dynamic-slice_fusion.2), channel_id=1, source_target_pairs={{0,8},{8,0},{16,24},{24,16},{1,9},{9,1},{17,25},{25,17},{2,10},{10... | collective-permute-start | bytes 4325384 | tf_op jit(solution)/shard_map/ppermute | solution.py:423
  170.3 5.5 %collective-permute-start.12 = (bf16[512,1408]{1,0:T(8,128)(2,1)}, bf16[512,1408]{1,0:T(8,128)(2,1)S(1)}, u32[]{:S(2)}, u32[]{:S(2)}) collective-permute-start(bf16[512,1408]{1,0:T(8,128)(2,1)} %collective-permute-done.9.p1), channel_id=1, source_target_pairs={{0,1},{1,0},{2,3},{3,2},{4,5},{5,4},{6,7},{7,6},{8,9},{9,8},{10,11... | collective-permute-start | bytes 4325384 | tf_op jit(solution)/shard_map/ppermute | solution.py:423
  170.3 5.6 %collective-permute-start.13 = (bf16[512,1408]{1,0:T(8,128)(2,1)}, bf16[512,1408]{1,0:T(8,128)(2,1)}, u32[]{:S(2)}, u32[]{:S(2)}) collective-permute-start(bf16[512,1408]{1,0:T(8,128)(2,1)} %collective-permute-done.10.p3), channel_id=1, source_target_pairs={{0,1},{1,0},{2,3},{3,2},{4,5},{5,4},{6,7},{7,6},{8,9},{9,8},{10,11... | collective-permute-start | bytes 4325384 | tf_op jit(solution)/shard_map/ppermute | solution.py:423
  170.8 7.2 %collective-permute-start.14 = (bf16[512,1408]{1,0:T(8,128)(2,1)}, bf16[512,1408]{1,0:T(8,128)(2,1)}, u32[]{:S(2)}, u32[]{:S(2)}) collective-permute-start(bf16[512,1408]{1,0:T(8,128)(2,1)} %collective-permute-done.11.p5), channel_id=1, source_target_pairs={{0,1},{1,0},{2,3},{3,2},{4,5},{5,4},{6,7},{7,6},{8,9},{9,8},{10,11... | collective-permute-start | bytes 4325384 | tf_op jit(solution)/shard_map/ppermute | solution.py:423
  222.9 128.0 %reduce-scatter.7.cloned.1.call-start = ((), (), s32[]{:S(2)}) async-start(), calls=%async_computation.13 | async-start | bytes 2359296 | tf_op jit(solution)/shard_map/reduce_scatter | solution.py:620
  223.3 9.8 %collective-permute-start.15 = (bf16[512,5632]{1,0:T(8,128)(2,1)}, bf16[512,5632]{1,0:T(8,128)(2,1)}, u32[]{:S(2)}, u32[]{:S(2)}) collective-permute-start(bf16[512,5632]{1,0:T(8,128)(2,1)} %convolution_convert_fusion), channel_id=1, source_target_pairs={{0,1},{1,0},{2,3},{3,2},{4,5},{5,4},{6,7},{7,6},{8,9},{9,8},{10,11... | collective-permute-start | bytes 17301512 | tf_op jit(solution)/shard_map/ppermute | solution.py:423
  244.1 44.1 %collective-permute-start.16 = (bf16[256,1408]{1,0:T(8,128)(2,1)}, bf16[256,1408]{1,0:T(8,128)(2,1)}, u32[]{:S(2)}, u32[]{:S(2)}) collective-permute-start(bf16[256,1408]{1,0:T(8,128)(2,1)} %get-tuple-element.330), channel_id=1, source_target_pairs={{0,8},{8,0},{16,24},{24,16},{1,9},{9,1},{17,25},{25,17},{2,10},{10... | collective-permute-start | bytes 2162696 | tf_op jit(solution)/shard_map/ppermute | solution.py:423
  248.7 39.5 %collective-permute-start.17 = (bf16[256,1408]{1,0:T(8,128)(2,1)}, bf16[256,1408]{1,0:T(8,128)(2,1)}, u32[]{:S(2)}, u32[]{:S(2)}) collective-permute-start(bf16[256,1408]{1,0:T(8,128)(2,1)} %get-tuple-element.329), channel_id=1, source_target_pairs={{0,16},{8,24},{16,0},{24,8},{1,17},{9,25},{17,1},{25,9},{2,18},{10... | collective-permute-start | bytes 2162696 | tf_op jit(solution)/shard_map/ppermute | solution.py:423
  251.4 54.6 %copy-start.28 = (bf16[1536,512]{1,0:T(8,128)(2,1)}, bf16[1536,512]{1,0:T(8,128)(2,1)S(1)}, u32[]{:S(2)}) copy-start(bf16[1536,512]{1,0:T(8,128)(2,1)S(1)} %get-tuple-element.318) | copy-start | bytes 4718596
  251.4 36.7 %slice-start = ((s8[5767168]{0:T(1024)(128)(4,1)}), s8[1572864]{0:T(1024)(128)(4,1)S(1)}, s32[]{:S(2)}) async-start(s8[5767168]{0:T(1024)(128)(4,1)} %bitcast.68), calls=%async_computation.16 | async-start | bytes 3145728
  251.4 36.7 %slice-start.1 = ((s8[5767168]{0:T(1024)(128)(4,1)}), s8[4194304]{0:T(1024)(128)(4,1)S(1)}, s32[]{:S(2)}) async-start(s8[5767168]{0:T(1024)(128)(4,1)} %bitcast.68), calls=%async_computation.17 | async-start | bytes 8388608
  300.3 5.7 %collective-permute-start.19 = (bf16[512,1024]{1,0:T(8,128)(2,1)}, bf16[512,1024]{1,0:T(8,128)(2,1)}, u32[]{:S(2)}, u32[]{:S(2)}) collective-permute-start(bf16[512,1024]{1,0:T(8,128)(2,1)} %convolution_convert_fusion.4), channel_id=1, source_target_pairs={{0,1},{1,0},{2,3},{3,2},{4,5},{5,4},{6,7},{7,6},{8,9},{9,8},{10,11... | collective-permute-start | bytes 3145736 | tf_op jit(solution)/shard_map/ppermute | solution.py:423
  300.3 3.9 collective-permute-start.18
  302.2 48.7 %collective-permute-start.22 = (bf16[512,1408]{1,0:T(8,128)(2,1)}, bf16[512,1408]{1,0:T(8,128)(2,1)S(1)}, u32[]{:S(2)}, u32[]{:S(2)}) collective-permute-start(bf16[512,1408]{1,0:T(8,128)(2,1)} %pad_maximum_fusion.2), channel_id=1, source_target_pairs={{0,8},{8,0},{16,24},{24,16},{1,9},{9,1},{17,25},{25,17},{2,10},{10... | collective-permute-start | bytes 4325384 | tf_op jit(solution)/shard_map/ppermute | solution.py:423
  302.3 48.6 %collective-permute-start.23 = (bf16[512,1408]{1,0:T(8,128)(2,1)}, bf16[512,1408]{1,0:T(8,128)(2,1)}, u32[]{:S(2)}, u32[]{:S(2)}) collective-permute-start(bf16[512,1408]{1,0:T(8,128)(2,1)} %pad_maximum_fusion.3), channel_id=1, source_target_pairs={{0,16},{8,24},{16,0},{24,8},{1,17},{9,25},{17,1},{25,9},{2,18},{10... | collective-permute-start | bytes 4325384 | tf_op jit(solution)/shard_map/ppermute | solution.py:423
  311.1 39.8 %collective-permute-start.20 = (bf16[256,768]{1,0:T(8,128)(2,1)}, bf16[256,768]{1,0:T(8,128)(2,1)S(1)}, u32[]{:S(2)}, u32[]{:S(2)}) collective-permute-start(bf16[256,768]{1,0:T(8,128)(2,1)} %get-tuple-element.344), channel_id=1, source_target_pairs={{0,8},{8,0},{16,24},{24,16},{1,9},{9,1},{17,25},{25,17},{2,10},{10... | collective-permute-start | bytes 1179656 | tf_op jit(solution)/shard_map/ppermute | solution.py:423
  312.6 37.0 %copy-start.69 = (f32[4,8,128]{2,1,0:T(8,128)S(1)}, f32[4,8,128]{2,1,0:T(8,128)}, u32[]{:S(2)}) copy-start(f32[4,8,128]{2,1,0:T(8,128)} %get-tuple-element.280) | copy-start | bytes 49156
  312.6 38.3 %copy-start.53 = (bf16[352,1024]{1,0:T(8,128)(2,1)S(1)}, bf16[352,1024]{1,0:T(8,128)(2,1)}, u32[]{:S(2)}) copy-start(bf16[352,1024]{1,0:T(8,128)(2,1)} %reduce-scatter.5.cloned.1.call-done) | copy-start | bytes 2162692
  312.6 38.2 %collective-permute-start.21 = (bf16[256,768]{1,0:T(8,128)(2,1)}, bf16[256,768]{1,0:T(8,128)(2,1)S(1)}, u32[]{:S(2)}, u32[]{:S(2)}) collective-permute-start(bf16[256,768]{1,0:T(8,128)(2,1)} %get-tuple-element.343), channel_id=1, source_target_pairs={{0,16},{8,24},{16,0},{24,8},{1,17},{9,25},{17,1},{25,9},{2,18},{10... | collective-permute-start | bytes 1179656 | tf_op jit(solution)/shard_map/ppermute | solution.py:423
  353.1 19.3 %all-to-all-start.1 = ((bf16[4,120,1024]{2,1,0:T(8,128)(2,1)}), bf16[4,120,1024]{2,1,0:T(8,128)(2,1)S(1)}, u32[]{:S(2)}, u32[]{:S(2)}) async-start(bf16[4,120,1024]{2,1,0:T(8,128)(2,1)} %bitcast.21), calls=%async_computation.3 | async-start | bytes 1966080 | tf_op jit(solution)/shard_map/all_to_all | solution.py:484
  356.6 42.5 %reduce-scatter.9.cloned.1.call-start = ((), (), s32[]{:S(2)}) async-start(), calls=%async_computation.14 | async-start | bytes 1802240 | tf_op jit(solution)/shard_map/reduce_scatter | solution.py:479
  372.6 26.6 %collective-permute-start.24 = (bf16[512,1024]{1,0:T(8,128)(2,1)S(1)}, bf16[512,1024]{1,0:T(8,128)(2,1)}, u32[]{:S(2)}, u32[]{:S(2)}) collective-permute-start(bf16[512,1024]{1,0:T(8,128)(2,1)S(1)} %broadcast_select_fusion.2), channel_id=1, source_target_pairs={{8,24},{16,0},{9,25},{17,1},{10,26},{18,2},{11,27},{19,3},{12,28},... | collective-permute-start | bytes 3145736 | tf_op jit(solution)/shard_map/ppermute | solution.py:433
  399.2 4.1 collective-permute-start.26
  399.2 3.6 collective-permute-start.25
  401.7 20.7 %collective-permute-start.27 = (bf16[512,768]{1,0:T(8,128)(2,1)}, bf16[512,768]{1,0:T(8,128)(2,1)}, u32[]{:S(2)}, u32[]{:S(2)}) collective-permute-start(bf16[512,768]{1,0:T(8,128)(2,1)} %pad_maximum_fusion.10), channel_id=1, source_target_pairs={{0,8},{8,0},{16,24},{24,16},{1,9},{9,1},{17,25},{25,17},{2,10},{10... | collective-permute-start | bytes 2359304 | tf_op jit(solution)/shard_map/ppermute | solution.py:423
  407.4 30.3 %collective-permute-start.28 = (bf16[512,768]{1,0:T(8,128)(2,1)}, bf16[512,768]{1,0:T(8,128)(2,1)}, u32[]{:S(2)}, u32[]{:S(2)}) collective-permute-start(bf16[512,768]{1,0:T(8,128)(2,1)} %fusion.16), channel_id=1, source_target_pairs={{0,16},{8,24},{16,0},{24,8},{1,17},{9,25},{17,1},{25,9},{2,18},{10... | collective-permute-start | bytes 2359304 | tf_op jit(solution)/shard_map/ppermute | solution.py:423
  410.3 27.4 %all-to-all-start.2 = ((bf16[4,120,1024]{2,1,0:T(8,128)(2,1)}), bf16[4,120,1024]{2,1,0:T(8,128)(2,1)S(1)}, u32[]{:S(2)}, u32[]{:S(2)}) async-start(bf16[4,120,1024]{2,1,0:T(8,128)(2,1)} %broadcast_in_dim.220), calls=%async_computation.5 | async-start | bytes 1966080 | tf_op jit(solution)/shard_map/all_to_all | solution.py:443
  413.9 53.4 %reduce-scatter.11.cloned.1.call-start = ((), (), s32[]{:S(2)}) async-start(), calls=%async_computation.15 | async-start | bytes 1146880 | tf_op jit(solution)/shard_map/reduce_scatter | solution.py:479
  413.9 1.4 collective-permute-start.29
  442.0 23.0 %all-to-all-start.3 = ((bf16[4,128,1408]{2,1,0:T(8,128)(2,1)}), bf16[4,128,1408]{2,1,0:T(8,128)(2,1)S(1)}, u32[]{:S(2)}, u32[]{:S(2)}) async-start(bf16[4,128,1408]{2,1,0:T(8,128)(2,1)} %broadcast_in_dim.221), calls=%async_computation.7 | async-start | bytes 2883584 | tf_op jit(solution)/shard_map/all_to_all | solution.py:443
  449.0 38.6 %collective-permute-start.30 = (bf16[512,1024]{1,0:T(8,128)(2,1)}, bf16[512,1024]{1,0:T(8,128)(2,1)}, u32[]{:S(2)}, u32[]{:S(2)}) collective-permute-start(bf16[512,1024]{1,0:T(8,128)(2,1)} %add_convert_fusion.2), channel_id=1, source_target_pairs={{0,8},{8,0},{16,24},{24,16},{1,9},{9,1},{17,25},{25,17},{2,10},{10... | collective-permute-start | bytes 3145736 | tf_op jit(solution)/shard_map/ppermute | solution.py:423
  469.2 28.6 %all-to-all-start.4 = ((bf16[4,128,896]{2,1,0:T(8,128)(2,1)}), bf16[4,128,896]{2,1,0:T(8,128)(2,1)S(1)}, u32[]{:S(2)}, u32[]{:S(2)}) async-start(bf16[4,128,896]{2,1,0:T(8,128)(2,1)} %broadcast_in_dim.222), calls=%async_computation.8 | async-start | bytes 1835008 | tf_op jit(solution)/shard_map/all_to_all | solution.py:443
  (82 other events, 824.9 us)
Sparse Core Ops, SparseCore 0:
  10.2 31.7 all-gather.3
  44.3 36.3 all-gather.5
  82.3 59.2 all-gather.7
  223.0 68.1 reduce-scatter.4
  293.9 34.1 reduce-scatter.6
  360.2 34.8 reduce-scatter.8
  440.9 26.2 reduce-scatter.10

commit v6 on v5

--- a/solution.py
+++ b/solution.py
@@ -553,6 +553,8 @@
     small = lax.all_to_all(jnp.broadcast_to(small[None], (n_shards,) + small.shape), "fsdp", 0, 0)
 
     before, behind, small = tied(before, behind, small)
+    if quartered:
+        before, behind, near = tied(before, behind, near)
 
     gains = jnp.moveaxis(small[:, :4], 0, 1).reshape(4, D).astype(F32)
     bias = small[:, 4, :bias_n].reshape(2 * HEADS).astype(F32)

time: 517 us -> 518 us (level)
  transfers between devices with their start and end apart: 43 -> 43, of which waited for: 21 -> 21; matrix products, arithmetic and copies ran while one was open for 25% -> 26% of each run, Pallas kernels for 23% -> 23%
where the time goes in v6:
time: 518 us; the launch traced here: 509 us
  Pallas kernels  151 us (29%)
  waiting for transfers between devices  124 us (24%)
  other arithmetic  66.1 us (13%)
  matrix products  63.9 us (12%)
  starting transfers between devices  52.6 us (10%)
  local copies, waits for them, and re-layouts  30.3 us (6%)
  between operations  21.7 us (4%)
    ppermute x29, waiting for transfers between devices, permuted(): lax.ppermute(shard, axis, [(i, i ^ flip) for i in range(lax.axis_size(axi...  80.1 us
    pallas_call x2, Pallas kernels, attention_backward(): pl.pallas_call(bwd_kernel, grid_spec=pltpu.PrefetchScalarGridSpec(num_sca...  72.2 us
    pallas_call x1, Pallas kernels, attention_forward(): pl.pallas_call(fwd_kernel, grid_spec=pltpu.PrefetchScalarGridSpec(num_sca...  44.5 us
    dot_general x12, matrix products, dot_tn(): lax.dot_general(a, b, (((0,), (0,)), ((), ())), preferred_element_type=F32)  41.8 us
    pallas_call x1, Pallas kernels, feed_forward(): pl.pallas_call(feed_forward_kernel, in_specs=[smem, smem, vmem, vmem] + [...  31.2 us
    ppermute x29, starting transfers between devices, permuted(): lax.ppermute(shard, axis, [(i, i ^ flip) for i in range(lax.axis_size(axi...  26.3 us
    ppermute x1, waiting for transfers between devices, returned_far(): return lax.ppermute(jnp.where(odd, after, before), 'ctx', [(1, 3), (2, 0)])  19.6 us
    all_to_all x3, waiting for transfers between devices, ctx_spread(): lax.all_to_all(jnp.broadcast_to(part[None], (size,) + part.shape), 'ctx',...  18.9 us
  transfers between devices with their start and end apart: 43, of which 21 were waited for; matrix products, arithmetic and copies ran while one was open for 26% of the time, Pallas kernels for 23%

profile of v6, /device:TPU:0, one launch (start us, length us, event | category | flops | bytes accessed | tf_op | source)
XLA Modules:
  0.0 509.4 jit_solution(17010684874677152490)
XLA Ops:
  11.0 3.0 collective-permute-start
  18.0 4.2 fusion.40
  22.1 15.1 %collective-permute-done = bf16[512,1024]{1,0:T(8,128)(2,1)} collective-permute-done((bf16[512,1024]{1,0:T(8,128)(2,1)S(1)}, bf16[512,1024]{1,0:T(8,128)(2,1)}, u32[]{:S(2)}, u32[]{:S(2)}) %collective-permute-start) | collective-permute-done | bytes 1048608 | tf_op jit(solution)/shard_map/ppermute | solution.py:423
  37.2 4.7 collective-permute-start.1
  48.7 2.3 constant_dynamic-slice_fusion.4
  51.6 3.0 pad_maximum_fusion.7.sin_ref
  55.3 4.9 all-to-all-start
  60.2 2.5 collective-permute-done.1
  64.5 2.6 collective-permute-start.3
  67.7 7.4 %collective-permute-done.2.p1 = bf16[512,1024]{1,0:T(8,128)(2,1)} collective-permute-done((bf16[512,1024]{1,0:T(8,128)(2,1)}, bf16[512,1024]{1,0:T(8,128)(2,1)}, u32[]{:S(2)}, u32[]{:S(2)}) %collective-permute-start.2) | collective-permute-done | bytes 1048608 | tf_op jit(solution)/shard_map/ppermute | solution.py:423
  75.8 7.3 %multiply_convert_fusion.xn_ref = bf16[1536,1024]{1,0:T(8,128)(2,1)} fusion(f32[1024]{0:T(1024)S(1)} %bitcast.88, f32[1536]{0:T(1024)S(1)} %add_rsqrt_fusion, bf16[512,1024]{1,0:T(8,128)(2,1)S(1)} %get-tuple-element.217, bf16[512,1024]{1,0:T(8,128)(2,1)S(1)} %bitcast.73, bf16[512,1024]{1,0:T(8,128)(2,1)S(1)} %get-tuple-element.216), kind=kLoop, calls=%fused_computation.2 | loop fusion | flops 14155776 | bytes 6301696 | tf_op jit(solution)/shard_map/convert_element_type | solution.py:576
  83.1 5.6 %collective-permute-done.3.p3 = bf16[512,1024]{1,0:T(8,128)(2,1)} collective-permute-done((bf16[512,1024]{1,0:T(8,128)(2,1)}, bf16[512,1024]{1,0:T(8,128)(2,1)}, u32[]{:S(2)}, u32[]{:S(2)}) %collective-permute-start.3) | collective-permute-done | bytes 1048608 | tf_op jit(solution)/shard_map/ppermute | solution.py:423
  94.4 6.8 %collective-permute-done.6 = bf16[256,1024]{1,0:T(8,128)(2,1)S(1)} collective-permute-done((bf16[256,1024]{1,0:T(8,128)(2,1)S(1)}, bf16[256,1024]{1,0:T(8,128)(2,1)S(1)}, u32[]{:S(2)}, u32[]{:S(2)}) %collective-permute-start.6) | collective-permute-done | bytes 524320 | tf_op jit(solution)/shard_map/ppermute | solution.py:423
  101.2 2.3 collective-permute-done.7
  109.5 44.5 %attention_forward.1 = (bf16[512,1024]{1,0:T(8,128)(2,1)}, bf16[1536,1024]{1,0:T(8,128)(2,1)}, bf16[1536,1024]{1,0:T(8,128)(2,1)}, bf16[512,1024]{1,0:T(8,128)(2...) custom-call(s32[2]{0:T(128)} %pad_add_fusion.place_ref, ...), custom_call_target="tpu_custom_call" | custom-call | flops 1000000 | bytes 10000 | tf_op jit(solution)/shard_map/attention_forward/pallas_call | solution.py:229
  154.0 3.3 multiply_reduce_fusion.2
  158.9 10.0 %collective-permute-done.10.p3 = bf16[512,1408]{1,0:T(8,128)(2,1)} collective-permute-done((bf16[512,1408]{1,0:T(8,128)(2,1)S(1)}, bf16[512,1408]{1,0:T(8,128)(2,1)}, u32[]{:S(2)}, u32[]{:S(2)}) %collective-permute-start.10) | collective-permute-done | bytes 1441824 | tf_op jit(solution)/shard_map/ppermute | solution.py:423
  173.3 2.2 collective-permute-done.12.p2
  177.8 31.2 %feed_forward.1 = (bf16[512,2816]{1,0:T(8,128)(2,1)}, bf16[512,5632]{1,0:T(8,128)(2,1)}, bf16[512,1024]{1,0:T(8,128)(2,1)}, bf16[512,1024]{1,0:T(8,128)(2,1)}, f...) custom-call(s32[2]{0:T(128)} %pad_add_fusion.place_ref, ...), custom_call_target="tpu_custom_call" | custom-call | flops 1000000 | bytes 10000 | tf_op jit(solution)/shard_map/feed_forward/pallas_call | solution.py:328
  209.1 8.4 %convolution_convert_fusion = bf16[512,5632]{1,0:T(8,128)(2,1)} fusion(bf16[512,5632]{1,0:T(8,128)(2,1)} %get-tuple-element.240, pred[]{:T(512)S(6)} %eq.180, bf16[512,128]{1,0:T(8,128)(2,1)S(1)} %get-tuple-element.342, bf16[512,128]{1,0:T(8,128)(2,1)S(1)} %get-tuple-element.343, bf16[512,128]{1,0:T(8,128)(2,1)S(1)} %get-tuple-element.344, ...), kind=kOutput, calls=%fused_computation.1 | convolution fusion | flops 2960130048 | bytes 12582913 | tf_op jit(solution)/shard_map/dot_general | solution.py:23
  217.4 5.1 convolution_convert_fusion.1
  227.2 2.6 convolution_convert_fusion.2
  229.8 3.0 collective-permute-done.15
  232.9 7.5 %add_convert_fusion = bf16[512,5632]{1,0:T(8,128)(2,1)S(1)} fusion(bf16[512,5632]{1,0:T(8,128)(2,1)} %collective-permute-done.15, bf16[512,5632]{1,0:T(8,128)(2,1)} %get-tuple-element.240, pred[]{:T(512)S(6)} %eq.180, bf16[512,128]{1,0:T(8,128)(2,1)S(1)} %copy-done.36, bf16[512,128]{1,0:T(8,128)(2,1)S(1)} %copy-done.38, bf16[512,128]{1,0:T(8,128)(2,1)S(1)} %copy-done.40, ...), kind=kOutput, calls=%fused_computation | convolution fusion | flops 2965897216 | bytes 18350080 | tf_op jit(solution)/shard_map/dot_general | solution.py:23
  243.8 3.6 collective-permute-start.16
  250.9 36.7 %attention_backward.2 = (bf16[512,512]{1,0:T(8,128)(2,1)}, bf16[1536,1024]{1,0:T(8,128)(2,1)}, f32[4,1,256]{2,1,0:T(1,128)}, f32[4,1,256]{2,1,0:T(1,128)}, f32[4,8,128]{2,1,0:T(8,128)}) custom-call(s32[2]{0:T(128)} %pad_add_fusion.place_ref, bf16[512,1024]{1,0:T(8,128)(2,1)} %get-tuple-element.222.q_ref, bf16[1536,1024]{1,0:T(8,128)(2,1)} %get-tuple-element.223.k_ref, ...), custom_call_target="tpu_custom_call" | custom-call | flops 1000000 | bytes 10000 | tf_op jit(solution)/shard_map/attention_backward/pallas_call | solution.py:347
  292.6 2.3 convolution_convert_fusion.6
  294.9 4.8 convolution_convert_fusion.4
  305.4 3.1 add_convert_fusion.4
  312.8 35.5 %attention_backward.3 = (bf16[512,512]{1,0:T(8,128)(2,1)}, bf16[1536,1024]{1,0:T(8,128)(2,1)}, f32[4,1,256]{2,1,0:T(1,128)}, f32[4,1,256]{2,1,0:T(1,128)}, f32[4,8,128]{2,1,0:T(8,128)}) custom-call(s32[2]{0:T(128)} %pad_add_fusion.place_ref, bf16[512,1024]{1,0:T(8,128)(2,1)} %get-tuple-element.222.q_ref, bf16[1536,1024]{1,0:T(8,128)(2,1)} %get-tuple-element.223.k_ref, ...), custom_call_target="tpu_custom_call" | custom-call | flops 1000000 | bytes 10000 | tf_op jit(solution)/shard_map/attention_backward/pallas_call | solution.py:347
  352.6 3.5 all-to-all-start.1
  356.2 3.4 add_convert_fusion.1
  359.7 6.2 %fusion.3 = f32[1536,1024]{1,0:T(8,128)S(1)} fusion(bf16[1536,1024]{1,0:T(8,128)(2,1)} %get-tuple-element.294, bf16[1024,2048]{1,0:T(8,128)(2,1)} %get-tuple-element.259), kind=kOutput, calls=%fused_computation.17 | convolution fusion | flops 3221225472 | bytes 11534336 | tf_op jit(solution)/shard_map/dot_general | solution.py:22
  365.9 5.9 %fusion.76 = (bf16[1536,1024]{1,0:T(8,128)(2,1)S(1)}, f32[1536,1024]{1,0:T(8,128)}) fusion(f32[1536,1024]{1,0:T(8,128)S(1)} %fusion.3, bf16[1536,1024]{1,0:T(8,128)(2,1)S(1)} %copy-done.74, bf16[1024,2048]{1,0:T(8,128)(2,1)S(1)} %copy-done.72), kind=kOutput, calls=%fused_computation.212 | convolution fusion | flops 3224371200 | bytes 20971520 | tf_op jit(solution)/shard_map/dot_general | solution.py:22
  376.1 2.8 convolution_convert_fusion.3
  378.9 19.6 %collective-permute-done.24 = bf16[512,1024]{1,0:T(8,128)(2,1)} collective-permute-done((bf16[512,1024]{1,0:T(8,128)(2,1)S(1)}, bf16[512,1024]{1,0:T(8,128)(2,1)}, u32[]{:S(2)}, u32[]{:S(2)}) %collective-permute-start.24) | collective-permute-done | bytes 1048608 | tf_op jit(solution)/shard_map/ppermute | solution.py:433
  409.7 3.5 all-to-all-start.2
  414.7 7.0 %collective-permute-done.27 = bf16[512,768]{1,0:T(8,128)(2,1)} collective-permute-done((bf16[512,768]{1,0:T(8,128)(2,1)}, bf16[512,768]{1,0:T(8,128)(2,1)}, u32[]{:S(2)}, u32[]{:S(2)}) %collective-permute-start.27) | collective-permute-done | bytes 786464 | tf_op jit(solution)/shard_map/ppermute | solution.py:423
  421.8 15.3 %all-to-all-done.2 = bf16[4,120,1024]{2,1,0:T(8,128)(2,1)S(1)} async-done(((bf16[4,120,1024]{2,1,0:T(8,128)(2,1)}), bf16[4,120,1024]{2,1,0:T(8,128)(2,1)S(1)}, u32[]{:S(2)}, u32[]{:S(2)}) %all-to-all-start.2) | async-done | bytes 983072 | tf_op jit(solution)/shard_map/all_to_all | solution.py:443
  441.4 3.7 all-to-all-start.3
  445.1 3.3 add_convert_fusion.2
  451.7 4.9 maximum_convert_fusion
  460.7 3.6 all-to-all-done.3.refs_0_
  464.3 2.5 reduce-scatter.11.cloned.1.call-done
  468.7 3.7 all-to-all-start.4
  472.4 14.5 %collective-permute-done.30 = bf16[512,1024]{1,0:T(8,128)(2,1)} collective-permute-done((bf16[512,1024]{1,0:T(8,128)(2,1)}, bf16[512,1024]{1,0:T(8,128)(2,1)}, u32[]{:S(2)}, u32[]{:S(2)}) %collective-permute-start.30) | collective-permute-done | bytes 1048608 | tf_op jit(solution)/shard_map/ppermute | solution.py:423
  486.9 4.7 multiply_reduce_fusion.1
  491.6 3.5 add_bitcast_fusion
  (365 shorter events, 100.9 us)
Async XLA Ops:
  7.2 41.5 %all-gather.4.cloned.1.call-start = ((), (), s32[]{:S(2)}) async-start(), calls=%async_computation.9 | async-start | bytes 2359296 | tf_op jit(solution)/shard_map/all_gather | solution.py:528
  9.1 79.6 %all-gather.6.cloned.1.call-start = ((), (), s32[]{:S(2)}) async-start(), calls=%async_computation.10 | async-start | bytes 3244032 | tf_op jit(solution)/shard_map/all_gather | solution.py:529
  10.9 166.9 %all-gather.8.cloned.1.call-start = ((), (), s32[]{:S(2)}) async-start(), calls=%async_computation.11 | async-start | bytes 6488064 | tf_op jit(solution)/shard_map/all_gather | solution.py:535
  11.0 26.3 %collective-permute-start = (bf16[512,1024]{1,0:T(8,128)(2,1)S(1)}, bf16[512,1024]{1,0:T(8,128)(2,1)}, u32[]{:S(2)}, u32[]{:S(2)}) collective-permute-start(bf16[512,1024]{1,0:T(8,128)(2,1)S(1)} %bitcast.71), channel_id=1, source_target_pairs={{0,8},{8,0},{16,24},{24,16},{1,9},{9,1},{17,25},{25,17},{2,10},{10... | collective-permute-start | bytes 3145736 | tf_op jit(solution)/shard_map/ppermute | solution.py:423
  37.2 25.5 %collective-permute-start.1 = (bf16[512,1024]{1,0:T(8,128)(2,1)}, bf16[512,1024]{1,0:T(8,128)(2,1)}, u32[]{:S(2)}, u32[]{:S(2)}) collective-permute-start(bf16[512,1024]{1,0:T(8,128)(2,1)} %collective-permute-done), channel_id=1, source_target_pairs={{0,16},{24,8},{1,17},{25,9},{2,18},{26,10},{3,19},{27,11},{4,20},{... | collective-permute-start | bytes 3145736 | tf_op jit(solution)/shard_map/ppermute | solution.py:544
  51.0 24.1 %collective-permute-start.2 = (bf16[512,1024]{1,0:T(8,128)(2,1)}, bf16[512,1024]{1,0:T(8,128)(2,1)}, u32[]{:S(2)}, u32[]{:S(2)}) collective-permute-start(bf16[512,1024]{1,0:T(8,128)(2,1)} %constant_dynamic-slice_fusion.4), channel_id=1, source_target_pairs={{0,8},{8,0},{16,24},{24,16},{1,9},{9,1},{17,25},{25,17},{2,10},{10... | collective-permute-start | bytes 3145736 | tf_op jit(solution)/shard_map/ppermute | solution.py:423
  55.3 11.8 %all-to-all-start = ((bf16[8,16,128]{2,1,0:T(8,128)(2,1)}), bf16[8,16,128]{2,1,0:T(8,128)(2,1)S(1)}, u32[]{:S(2)}, u32[]{:S(2)}) async-start(bf16[8,16,128]{2,1,0:T(8,128)(2,1)} %broadcast_in_dim.196), calls=%async_computation | async-start | bytes 65536 | tf_op jit(solution)/shard_map/all_to_all | solution.py:553
  60.2 231.7 %reduce-scatter.5.cloned.1.call-start = ((), (), s32[]{:S(2)}) async-start(), calls=%async_computation.12 | async-start | bytes 6488064 | tf_op jit(solution)/shard_map/reduce_scatter | solution.py:607
  64.5 24.2 %collective-permute-start.3 = (bf16[512,1024]{1,0:T(8,128)(2,1)}, bf16[512,1024]{1,0:T(8,128)(2,1)}, u32[]{:S(2)}, u32[]{:S(2)}) collective-permute-start(bf16[512,1024]{1,0:T(8,128)(2,1)} %constant_dynamic-slice_fusion.4), channel_id=1, source_target_pairs={{0,16},{8,24},{16,0},{24,8},{1,17},{9,25},{17,1},{25,9},{2,18},{10... | collective-permute-start | bytes 3145736 | tf_op jit(solution)/shard_map/ppermute | solution.py:423
  90.0 11.2 %collective-permute-start.6 = (bf16[256,1024]{1,0:T(8,128)(2,1)S(1)}, bf16[256,1024]{1,0:T(8,128)(2,1)S(1)}, u32[]{:S(2)}, u32[]{:S(2)}) collective-permute-start(bf16[256,1024]{1,0:T(8,128)(2,1)S(1)} %slice.427), channel_id=1, source_target_pairs={{0,16},{8,24},{16,0},{24,8},{1,17},{9,25},{17,1},{25,9},{2,18},{10... | collective-permute-start | bytes 1572872 | tf_op jit(solution)/shard_map/ppermute | solution.py:423
  92.8 10.7 %collective-permute-start.7 = (bf16[256,1024]{1,0:T(8,128)(2,1)S(1)}, bf16[256,1024]{1,0:T(8,128)(2,1)S(1)}, u32[]{:S(2)}, u32[]{:S(2)}) collective-permute-start(bf16[256,1024]{1,0:T(8,128)(2,1)S(1)} %slice.428), channel_id=1, source_target_pairs={{0,8},{8,0},{16,24},{24,16},{1,9},{9,1},{17,25},{25,17},{2,10},{10... | collective-permute-start | bytes 1572872 | tf_op jit(solution)/shard_map/ppermute | solution.py:423
  93.2 12.7 %collective-permute-start.4 = (bf16[512,1024]{1,0:T(8,128)(2,1)}, bf16[512,1024]{1,0:T(8,128)(2,1)S(1)}, u32[]{:S(2)}, u32[]{:S(2)}) collective-permute-start(bf16[512,1024]{1,0:T(8,128)(2,1)} %collective-permute-done.2.p1), channel_id=1, source_target_pairs={{0,1},{1,0},{2,3},{3,2},{4,5},{5,4},{6,7},{7,6},{8,9},{9,8},{10,11... | collective-permute-start | bytes 3145736 | tf_op jit(solution)/shard_map/ppermute | solution.py:423
  93.9 14.3 %collective-permute-start.5 = (bf16[512,1024]{1,0:T(8,128)(2,1)}, bf16[512,1024]{1,0:T(8,128)(2,1)S(1)}, u32[]{:S(2)}, u32[]{:S(2)}) collective-permute-start(bf16[512,1024]{1,0:T(8,128)(2,1)} %collective-permute-done.3.p3), channel_id=1, source_target_pairs={{0,1},{1,0},{2,3},{3,2},{4,5},{5,4},{6,7},{7,6},{8,9},{9,8},{10,11... | collective-permute-start | bytes 3145736 | tf_op jit(solution)/shard_map/ppermute | solution.py:423
  103.6 4.6 collective-permute-start.8
  103.8 65.0 %collective-permute-start.10 = (bf16[512,1408]{1,0:T(8,128)(2,1)S(1)}, bf16[512,1408]{1,0:T(8,128)(2,1)}, u32[]{:S(2)}, u32[]{:S(2)}) collective-permute-start(bf16[512,1408]{1,0:T(8,128)(2,1)S(1)} %constant_dynamic-slice_fusion.2), channel_id=1, source_target_pairs={{0,16},{8,24},{16,0},{24,8},{1,17},{9,25},{17,1},{25,9},{2,18},{10... | collective-permute-start | bytes 4325384 | tf_op jit(solution)/shard_map/ppermute | solution.py:423
  104.5 64.4 %collective-permute-start.11 = (bf16[512,1408]{1,0:T(8,128)(2,1)S(1)}, bf16[512,1408]{1,0:T(8,128)(2,1)}, u32[]{:S(2)}, u32[]{:S(2)}) collective-permute-start(bf16[512,1408]{1,0:T(8,128)(2,1)S(1)} %constant_dynamic-slice_fusion.2), channel_id=1, source_target_pairs={{0,24},{8,16},{16,8},{24,0},{1,25},{9,17},{17,9},{25,1},{2,26},{10... | collective-permute-start | bytes 4325384 | tf_op jit(solution)/shard_map/ppermute | solution.py:423
  105.9 64.2 %collective-permute-start.9 = (bf16[512,1408]{1,0:T(8,128)(2,1)S(1)}, bf16[512,1408]{1,0:T(8,128)(2,1)}, u32[]{:S(2)}, u32[]{:S(2)}) collective-permute-start(bf16[512,1408]{1,0:T(8,128)(2,1)S(1)} %constant_dynamic-slice_fusion.2), channel_id=1, source_target_pairs={{0,8},{8,0},{16,24},{24,16},{1,9},{9,1},{17,25},{25,17},{2,10},{10... | collective-permute-start | bytes 4325384 | tf_op jit(solution)/shard_map/ppermute | solution.py:423
  170.1 5.5 %collective-permute-start.12 = (bf16[512,1408]{1,0:T(8,128)(2,1)}, bf16[512,1408]{1,0:T(8,128)(2,1)S(1)}, u32[]{:S(2)}, u32[]{:S(2)}) collective-permute-start(bf16[512,1408]{1,0:T(8,128)(2,1)} %collective-permute-done.9.p1), channel_id=1, source_target_pairs={{0,1},{1,0},{2,3},{3,2},{4,5},{5,4},{6,7},{7,6},{8,9},{9,8},{10,11... | collective-permute-start | bytes 4325384 | tf_op jit(solution)/shard_map/ppermute | solution.py:423
  170.1 5.6 %collective-permute-start.13 = (bf16[512,1408]{1,0:T(8,128)(2,1)}, bf16[512,1408]{1,0:T(8,128)(2,1)}, u32[]{:S(2)}, u32[]{:S(2)}) collective-permute-start(bf16[512,1408]{1,0:T(8,128)(2,1)} %collective-permute-done.10.p3), channel_id=1, source_target_pairs={{0,1},{1,0},{2,3},{3,2},{4,5},{5,4},{6,7},{7,6},{8,9},{9,8},{10,11... | collective-permute-start | bytes 4325384 | tf_op jit(solution)/shard_map/ppermute | solution.py:423
  170.6 7.2 %collective-permute-start.14 = (bf16[512,1408]{1,0:T(8,128)(2,1)}, bf16[512,1408]{1,0:T(8,128)(2,1)}, u32[]{:S(2)}, u32[]{:S(2)}) collective-permute-start(bf16[512,1408]{1,0:T(8,128)(2,1)} %collective-permute-done.11.p5), channel_id=1, source_target_pairs={{0,1},{1,0},{2,3},{3,2},{4,5},{5,4},{6,7},{7,6},{8,9},{9,8},{10,11... | collective-permute-start | bytes 4325384 | tf_op jit(solution)/shard_map/ppermute | solution.py:423
  222.5 127.9 %reduce-scatter.7.cloned.1.call-start = ((), (), s32[]{:S(2)}) async-start(), calls=%async_computation.13 | async-start | bytes 2359296 | tf_op jit(solution)/shard_map/reduce_scatter | solution.py:622
  223.0 9.8 %collective-permute-start.15 = (bf16[512,5632]{1,0:T(8,128)(2,1)}, bf16[512,5632]{1,0:T(8,128)(2,1)}, u32[]{:S(2)}, u32[]{:S(2)}) collective-permute-start(bf16[512,5632]{1,0:T(8,128)(2,1)} %convolution_convert_fusion), channel_id=1, source_target_pairs={{0,1},{1,0},{2,3},{3,2},{4,5},{5,4},{6,7},{7,6},{8,9},{9,8},{10,11... | collective-permute-start | bytes 17301512 | tf_op jit(solution)/shard_map/ppermute | solution.py:423
  243.8 43.9 %collective-permute-start.16 = (bf16[256,1408]{1,0:T(8,128)(2,1)}, bf16[256,1408]{1,0:T(8,128)(2,1)}, u32[]{:S(2)}, u32[]{:S(2)}) collective-permute-start(bf16[256,1408]{1,0:T(8,128)(2,1)} %get-tuple-element.336), channel_id=1, source_target_pairs={{0,8},{8,0},{16,24},{24,16},{1,9},{9,1},{17,25},{25,17},{2,10},{10... | collective-permute-start | bytes 2162696 | tf_op jit(solution)/shard_map/ppermute | solution.py:423
  247.4 40.4 %collective-permute-start.17 = (bf16[256,1408]{1,0:T(8,128)(2,1)}, bf16[256,1408]{1,0:T(8,128)(2,1)}, u32[]{:S(2)}, u32[]{:S(2)}) collective-permute-start(bf16[256,1408]{1,0:T(8,128)(2,1)} %get-tuple-element.335), channel_id=1, source_target_pairs={{0,16},{8,24},{16,0},{24,8},{1,17},{9,25},{17,1},{25,9},{2,18},{10... | collective-permute-start | bytes 2162696 | tf_op jit(solution)/shard_map/ppermute | solution.py:423
  250.9 54.5 %copy-start.28 = (bf16[1536,512]{1,0:T(8,128)(2,1)}, bf16[1536,512]{1,0:T(8,128)(2,1)S(1)}, u32[]{:S(2)}) copy-start(bf16[1536,512]{1,0:T(8,128)(2,1)S(1)} %get-tuple-element.324) | copy-start | bytes 4718596
  299.8 5.6 %collective-permute-start.19 = (bf16[512,1024]{1,0:T(8,128)(2,1)}, bf16[512,1024]{1,0:T(8,128)(2,1)}, u32[]{:S(2)}, u32[]{:S(2)}) collective-permute-start(bf16[512,1024]{1,0:T(8,128)(2,1)} %convolution_convert_fusion.4), channel_id=1, source_target_pairs={{0,1},{1,0},{2,3},{3,2},{4,5},{5,4},{6,7},{7,6},{8,9},{9,8},{10,11... | collective-permute-start | bytes 3145736 | tf_op jit(solution)/shard_map/ppermute | solution.py:423
  299.8 3.9 collective-permute-start.18
  301.7 48.7 %collective-permute-start.22 = (bf16[512,1408]{1,0:T(8,128)(2,1)}, bf16[512,1408]{1,0:T(8,128)(2,1)S(1)}, u32[]{:S(2)}, u32[]{:S(2)}) collective-permute-start(bf16[512,1408]{1,0:T(8,128)(2,1)} %pad_maximum_fusion.2), channel_id=1, source_target_pairs={{0,8},{8,0},{16,24},{24,16},{1,9},{9,1},{17,25},{25,17},{2,10},{10... | collective-permute-start | bytes 4325384 | tf_op jit(solution)/shard_map/ppermute | solution.py:423
  301.8 48.6 %collective-permute-start.23 = (bf16[512,1408]{1,0:T(8,128)(2,1)}, bf16[512,1408]{1,0:T(8,128)(2,1)}, u32[]{:S(2)}, u32[]{:S(2)}) collective-permute-start(bf16[512,1408]{1,0:T(8,128)(2,1)} %pad_maximum_fusion.3), channel_id=1, source_target_pairs={{0,16},{8,24},{16,0},{24,8},{1,17},{9,25},{17,1},{25,9},{2,18},{10... | collective-permute-start | bytes 4325384 | tf_op jit(solution)/shard_map/ppermute | solution.py:423
  310.5 39.8 %collective-permute-start.20 = (bf16[256,768]{1,0:T(8,128)(2,1)}, bf16[256,768]{1,0:T(8,128)(2,1)S(1)}, u32[]{:S(2)}, u32[]{:S(2)}) collective-permute-start(bf16[256,768]{1,0:T(8,128)(2,1)} %get-tuple-element.350), channel_id=1, source_target_pairs={{0,8},{8,0},{16,24},{24,16},{1,9},{9,1},{17,25},{25,17},{2,10},{10... | collective-permute-start | bytes 1179656 | tf_op jit(solution)/shard_map/ppermute | solution.py:423
  311.3 37.0 %copy-start.66 = (f32[4,1,256]{2,1,0:T(1,128)S(1)}, f32[4,1,256]{2,1,0:T(1,128)}, u32[]{:S(2)}) copy-start(f32[4,1,256]{2,1,0:T(1,128)} %get-tuple-element.282) | copy-start | bytes 12292
  311.3 37.0 %copy-start.67 = (f32[4,1,256]{2,1,0:T(1,128)S(1)}, f32[4,1,256]{2,1,0:T(1,128)}, u32[]{:S(2)}) copy-start(f32[4,1,256]{2,1,0:T(1,128)} %get-tuple-element.284) | copy-start | bytes 12292
  311.3 37.8 %copy-start.68 = (f32[4,8,128]{2,1,0:T(8,128)S(1)}, f32[4,8,128]{2,1,0:T(8,128)}, u32[]{:S(2)}) copy-start(f32[4,8,128]{2,1,0:T(8,128)} %get-tuple-element.286) | copy-start | bytes 49156
  311.3 39.1 %copy-start.52 = (bf16[352,1024]{1,0:T(8,128)(2,1)S(1)}, bf16[352,1024]{1,0:T(8,128)(2,1)}, u32[]{:S(2)}) copy-start(bf16[352,1024]{1,0:T(8,128)(2,1)} %reduce-scatter.5.cloned.1.call-done) | copy-start | bytes 2162692
  311.3 39.1 %collective-permute-start.21 = (bf16[256,768]{1,0:T(8,128)(2,1)}, bf16[256,768]{1,0:T(8,128)(2,1)S(1)}, u32[]{:S(2)}, u32[]{:S(2)}) collective-permute-start(bf16[256,768]{1,0:T(8,128)(2,1)} %get-tuple-element.349), channel_id=1, source_target_pairs={{0,16},{8,24},{16,0},{24,8},{1,17},{9,25},{17,1},{25,9},{2,18},{10... | collective-permute-start | bytes 1179656 | tf_op jit(solution)/shard_map/ppermute | solution.py:423
  352.6 19.4 %all-to-all-start.1 = ((bf16[4,120,1024]{2,1,0:T(8,128)(2,1)}), bf16[4,120,1024]{2,1,0:T(8,128)(2,1)S(1)}, u32[]{:S(2)}, u32[]{:S(2)}) async-start(bf16[4,120,1024]{2,1,0:T(8,128)(2,1)} %bitcast.21), calls=%async_computation.3 | async-start | bytes 1966080 | tf_op jit(solution)/shard_map/all_to_all | solution.py:484
  356.1 42.4 %reduce-scatter.9.cloned.1.call-start = ((), (), s32[]{:S(2)}) async-start(), calls=%async_computation.14 | async-start | bytes 1802240 | tf_op jit(solution)/shard_map/reduce_scatter | solution.py:479
  372.1 26.4 %collective-permute-start.24 = (bf16[512,1024]{1,0:T(8,128)(2,1)S(1)}, bf16[512,1024]{1,0:T(8,128)(2,1)}, u32[]{:S(2)}, u32[]{:S(2)}) collective-permute-start(bf16[512,1024]{1,0:T(8,128)(2,1)S(1)} %broadcast_select_fusion.2), channel_id=1, source_target_pairs={{8,24},{16,0},{9,25},{17,1},{10,26},{18,2},{11,27},{19,3},{12,28},... | collective-permute-start | bytes 3145736 | tf_op jit(solution)/shard_map/ppermute | solution.py:433
  398.5 4.1 collective-permute-start.26
  398.5 3.6 collective-permute-start.25
  401.1 20.7 %collective-permute-start.27 = (bf16[512,768]{1,0:T(8,128)(2,1)}, bf16[512,768]{1,0:T(8,128)(2,1)}, u32[]{:S(2)}, u32[]{:S(2)}) collective-permute-start(bf16[512,768]{1,0:T(8,128)(2,1)} %pad_maximum_fusion.10), channel_id=1, source_target_pairs={{0,8},{8,0},{16,24},{24,16},{1,9},{9,1},{17,25},{25,17},{2,10},{10... | collective-permute-start | bytes 2359304 | tf_op jit(solution)/shard_map/ppermute | solution.py:423
  406.8 30.3 %collective-permute-start.28 = (bf16[512,768]{1,0:T(8,128)(2,1)}, bf16[512,768]{1,0:T(8,128)(2,1)}, u32[]{:S(2)}, u32[]{:S(2)}) collective-permute-start(bf16[512,768]{1,0:T(8,128)(2,1)} %fusion.16), channel_id=1, source_target_pairs={{0,16},{8,24},{16,0},{24,8},{1,17},{9,25},{17,1},{25,9},{2,18},{10... | collective-permute-start | bytes 2359304 | tf_op jit(solution)/shard_map/ppermute | solution.py:423
  409.7 27.4 %all-to-all-start.2 = ((bf16[4,120,1024]{2,1,0:T(8,128)(2,1)}), bf16[4,120,1024]{2,1,0:T(8,128)(2,1)S(1)}, u32[]{:S(2)}, u32[]{:S(2)}) async-start(bf16[4,120,1024]{2,1,0:T(8,128)(2,1)} %broadcast_in_dim.220), calls=%async_computation.5 | async-start | bytes 1966080 | tf_op jit(solution)/shard_map/all_to_all | solution.py:443
  413.2 53.6 %reduce-scatter.11.cloned.1.call-start = ((), (), s32[]{:S(2)}) async-start(), calls=%async_computation.15 | async-start | bytes 1146880 | tf_op jit(solution)/shard_map/reduce_scatter | solution.py:479
  413.3 1.4 collective-permute-start.29
  441.4 23.0 %all-to-all-start.3 = ((bf16[4,128,1408]{2,1,0:T(8,128)(2,1)}), bf16[4,128,1408]{2,1,0:T(8,128)(2,1)S(1)}, u32[]{:S(2)}, u32[]{:S(2)}) async-start(bf16[4,128,1408]{2,1,0:T(8,128)(2,1)} %broadcast_in_dim.221), calls=%async_computation.7 | async-start | bytes 2883584 | tf_op jit(solution)/shard_map/all_to_all | solution.py:443
  448.3 38.6 %collective-permute-start.30 = (bf16[512,1024]{1,0:T(8,128)(2,1)}, bf16[512,1024]{1,0:T(8,128)(2,1)}, u32[]{:S(2)}, u32[]{:S(2)}) collective-permute-start(bf16[512,1024]{1,0:T(8,128)(2,1)} %add_convert_fusion.2), channel_id=1, source_target_pairs={{0,8},{8,0},{16,24},{24,16},{1,9},{9,1},{17,25},{25,17},{2,10},{10... | collective-permute-start | bytes 3145736 | tf_op jit(solution)/shard_map/ppermute | solution.py:423
  468.7 28.4 %all-to-all-start.4 = ((bf16[4,128,896]{2,1,0:T(8,128)(2,1)}), bf16[4,128,896]{2,1,0:T(8,128)(2,1)S(1)}, u32[]{:S(2)}, u32[]{:S(2)}) async-start(bf16[4,128,896]{2,1,0:T(8,128)(2,1)} %broadcast_in_dim.222), calls=%async_computation.8 | async-start | bytes 1835008 | tf_op jit(solution)/shard_map/all_to_all | solution.py:443
  (81 other events, 873.8 us)
Sparse Core Ops, SparseCore 0:
  10.2 31.7 all-gather.3
  44.3 36.3 all-gather.5
  82.3 59.2 all-gather.7
  222.7 68.2 reduce-scatter.4
  293.7 34.1 reduce-scatter.6
  359.8 35.0 reduce-scatter.8
  440.3 26.4 reduce-scatter.10
